TPU v7x, 32 devices: a whole 2x2x4 slice. The times are simulated.
32 devices in a mesh: space: 16 (over z, x, core), tm: 2 (over y).
Axes of the slice: x: 2, y: 2, z: 4, core: 2. Of those that a mesh axis runs over, the one named last changes fastest.
Arguments:
- start_state: float32 [2, 2, 256, 4096], P('tm', None, 'space'), may hold values from -6 to 6
- start_step: int32 [2], P('tm'), may hold values from 0 to 511
- velocity_x: float32 [256, 4096], P('space'), may hold values from -0.45 to 0.45
- velocity_y: float32 [256, 4096], P('space'), may hold values from -0.3 to 0.3
- amplitude: float32 [256, 4096], P('space'), may hold values from 0.2 to 1
- frequency: float32 [256, 4096], P('space'), may hold values from 0.3 to 2.5
- phase: float32 [256, 4096], P('space'), may hold values from -3.140625 to 3.140625
- sketch: float32 [64, 32], replicated, may hold values from -0.75 to 0.75
Outputs:
- piece: float32 [32, 256, 4096], P(None, 'space', 'tm')
- end_state: float32 [2, 2, 256, 4096], P('tm', None, 'space')
All inputs are finite; a program needn't handle non-finite values.
Results may differ from a plain program's by a relative error of at most 0.0003.
Values sent between devices are 32-bit elements; how exact they have to be, the bound alone decides.
No kernel may reach another device: no remote copies, remote signals or barrier semaphores. Data moves between devices by JAX's collectives and lax.ppermute only.
A program may use at most 64 MiB of HBM per device.

v0:
```python
import jax
import jax.numpy as jnp
from jax import lax
from jax.sharding import PartitionSpec as P

STEPS = 16


KAPPA = (0.06, 0.02)


def with_halo(block, sides, width, periodic):
    for axis, dim in sides:
        count = lax.axis_size(axis)
        forward = [(i, i + 1) for i in range(count - 1)]
        if periodic:
            forward.append((count - 1, 0))
        backward = [(target, source) for source, target in forward]
        low = lax.ppermute(
            lax.slice_in_dim(block, block.shape[dim] - width, None, axis=dim), axis, forward
        )
        high = lax.ppermute(lax.slice_in_dim(block, 0, width, axis=dim), axis, backward)
        block = jnp.concatenate([low, block, high], axis=dim)
    return block


def coefficients(gram, sketch):
    highest = lax.Precision.HIGHEST
    left = jnp.dot(sketch.T, gram, precision=highest)
    small = jnp.dot(left, sketch, precision=highest)
    lower = jnp.linalg.cholesky(small)
    proj = lax.linalg.triangular_solve(lower, left, left_side=True, lower=True)
    outer = jnp.dot(proj, proj.T, precision=highest)
    factor = jnp.linalg.cholesky(outer)
    mix_matrix = lax.linalg.triangular_solve(
        lower, factor, left_side=True, lower=True, transpose_a=True
    )
    return jnp.dot(sketch, mix_matrix, precision=highest)


def advance_step(state, padded, moment, velocity_x, velocity_y, amplitude, frequency, phase):
    east_side = padded[..., 2:, 1:-1]
    west_side = padded[..., :-2, 1:-1]
    north_side = padded[..., 1:-1, 2:]
    south_side = padded[..., 1:-1, :-2]
    kappa = jnp.array(KAPPA, jnp.float32).reshape(2, 1, 1)
    laplace_term = east_side + west_side + north_side + south_side - 4.0 * state
    transport = (
        jnp.maximum(velocity_x, 0.0) * (state - west_side)
        + jnp.minimum(velocity_x, 0.0) * (east_side - state)
        + jnp.maximum(velocity_y, 0.0) * (state - south_side)
        + jnp.minimum(velocity_y, 0.0) * (north_side - state)
    )
    angle = frequency * moment[:, None, None] + phase
    source = jnp.stack([amplitude * jnp.sin(angle), amplitude * jnp.cos(angle) * 0.5], axis=1)
    return state + kappa * laplace_term - transport + source


def arrange_snaps(snaps, state):
    groups, _, rows_x, rows_y = state.shape
    return jnp.transpose(snaps, (1, 2, 0, 3, 4)).reshape(groups, 2 * STEPS, rows_x, rows_y)


def run_steps(state, starts, fields, pad_state):

    def stepper(current, counter):
        padded = pad_state(current)
        moment = starts + counter.astype(jnp.float32)
        fresh = advance_step(current, padded, moment, *fields)
        return (fresh, fresh)

    final, snaps = lax.scan(stepper, state, jnp.arange(STEPS, dtype=jnp.int32))
    return (final, arrange_snaps(snaps, state))


def body(start_state, start_step, velocity_x, velocity_y, amplitude, frequency, phase, sketch):
    highest = lax.Precision.HIGHEST
    groups = lax.axis_size("tm")
    levels = groups.bit_length() - 1
    member = lax.axis_index("tm")
    full_y = velocity_x.shape[1]
    block_y = full_y // groups
    states = lax.all_to_all(start_state, "tm", split_axis=3, concat_axis=0, tiled=True)
    starts = lax.all_gather(start_step, "tm", axis=0, tiled=True).astype(jnp.float32)
    offset = member * block_y
    fields = tuple(
        (
            lax.dynamic_slice_in_dim(field, offset, block_y, 1)
            for field in (velocity_x, velocity_y, amplitude, frequency, phase)
        )
    )

    def pad_blocks(current):
        rimmed = with_halo(current, (("space", 2),), 1, True)
        return with_halo(rimmed, (("tm", 3),), 1, False)

    final, snaps = run_steps(states, starts, fields, pad_blocks)
    pieces = snaps
    for level in range(levels):
        count, columns, rows_x, rows_y = pieces.shape
        joined = pieces.reshape(count // 2, 2 * columns, rows_x, rows_y)
        gram = jnp.einsum("gcxy,gdxy->gcd", joined, joined, precision=highest)
        gram = lax.psum(gram, ("space", "tm"))
        coeff = jax.vmap(coefficients, in_axes=(0, None))(gram, sketch)
        pieces = jnp.einsum("gcxy,gcr->grxy", joined, coeff, precision=highest)
    end_state = lax.all_to_all(final, "tm", split_axis=0, concat_axis=3, tiled=True)
    return (pieces[0], end_state)


def solution(mesh):
    placed = (
        P("tm", None, "space", None),
        P("tm"),
        P("space", None),
        P("space", None),
        P("space", None),
        P("space", None),
        P("space", None),
        P(),
    )
    return jax.shard_map(
        body,
        mesh=mesh,
        in_specs=placed,
        out_specs=(P(None, "space", "tm"), P("tm", None, "space", None)),
        check_vma=False,
    )
```

profile of v0, /device:TPU:0, one launch (start us, length us, event | category | flops | bytes accessed | tf_op | source)
XLA Modules:
  0.0 404.9 jit_solution(10554948953794608500)
XLA Ops:
  0.7 5.7 %copy.24 = f32[1,2,16,4096]{2,1,0,3:T(2,128)} copy(f32[1,2,16,4096]{3,2,1,0:T(8,128)} %param.12) | data formatting | bytes 1048576 | tf_op args[0]
  6.4 7.9 %reshape.147 = f32[2,1,65536]{2,1,0:T(1,128)} reshape(f32[4096,1,2,16]{3,2,1,0:T(2,128)} %bitcast.66) | data formatting | bytes 1048576
  14.4 4.2 %all-to-all-start = ((f32[2,1,65536]{2,1,0:T(1,128)}), f32[2,1,65536]{2,1,0:T(1,128)S(1)}, u32[]{:S(2)}, u32[]{:S(2)}) async-start(f32[2,1,65536]{2,1,0:T(1,128)} %reshape.147), calls=%async_computation | async-start | bytes 1048576 | tf_op jit(solution)/shard_map/all_to_all | solution.py:83
  20.6 6.8 %all-reduce = s32[2]{0:T(128)S(1)} all-reduce(s32[2]{0:T(128)S(1)} %dynamic-update-slice), channel_id=1, replica_groups=mesh['space'=16,'tm'=2] {'tm'}, use_global_device_ids=true, to_apply=%add | all-reduce | flops 2 | bytes 16
  30.3 7.6 %reshape.148 = f32[4096,1,2,16]{3,2,1,0:T(2,128)} reshape(f32[2,65536]{1,0:T(2,128)S(1)} %reduce.27) | data formatting | bytes 1048576
  37.9 6.3 %copy.26 = f32[2,2,16,2048]{3,2,1,0:T(8,128)} copy(f32[2,2,16,2048]{2,1,3,0:T(2,128)} %bitcast.65) | data formatting | bytes 1048576
  44.2 268.0 %while.13 = (s32[]{:T(128)}, f32[2,2,16,2048]{3,2,1,0:T(8,128)}, f32[16,2,2,16,2048]{4,3,0,2,1:T(8,128)}, f32[16,2048]{1,0:T(8,128)S(1)}, f32[16,2048]{1,0:T(8,1...) while((s32[]{:T(128)}, f32[2,2,16,2048]{3,2,1,0:T(8,128)}, ...), condition=%wide.region_1.2_spmd.clone, body=%wide.region_0.1_spmd.sunk.clone.sunk | while | flops 4260133 | bytes 6426329 | solution.py:72
  45.3 3.4 collective-permute-start
  50.9 3.8 collective-permute-done.1
  54.8 2.5 collective-permute-start.2
  59.1 4.3 %collective-permute-done.3 = f32[2,2,18,1]{3,2,1,0:T(8,128)S(1)} collective-permute-done((f32[2,2,18,1]{3,2,1,0:T(8,128)S(1)}, f32[2,2,18,1]{3,2,1,0:T(8,128)S(1)}, u32[]{:S(2)}, u32[]{:S(2)}) %collective-permute-start.3) | collective-permute-done | bytes 320 | tf_op jit(solution)/shard_map/while/body/eval_jaxpr/ppermute | solution.py:22
  68.8 3.3 collective-permute-done.1
  75.5 4.3 %collective-permute-done.3 = f32[2,2,18,1]{3,2,1,0:T(8,128)S(1)} collective-permute-done((f32[2,2,18,1]{3,2,1,0:T(8,128)S(1)}, f32[2,2,18,1]{3,2,1,0:T(8,128)S(1)}, u32[]{:S(2)}, u32[]{:S(2)}) %collective-permute-start.3) | collective-permute-done | bytes 320 | tf_op jit(solution)/shard_map/while/body/eval_jaxpr/ppermute | solution.py:22
  85.3 3.3 collective-permute-done.1
  92.0 4.3 %collective-permute-done.3 = f32[2,2,18,1]{3,2,1,0:T(8,128)S(1)} collective-permute-done((f32[2,2,18,1]{3,2,1,0:T(8,128)S(1)}, f32[2,2,18,1]{3,2,1,0:T(8,128)S(1)}, u32[]{:S(2)}, u32[]{:S(2)}) %collective-permute-start.3) | collective-permute-done | bytes 320 | tf_op jit(solution)/shard_map/while/body/eval_jaxpr/ppermute | solution.py:22
  101.8 3.3 collective-permute-done.1
  108.5 4.3 %collective-permute-done.3 = f32[2,2,18,1]{3,2,1,0:T(8,128)S(1)} collective-permute-done((f32[2,2,18,1]{3,2,1,0:T(8,128)S(1)}, f32[2,2,18,1]{3,2,1,0:T(8,128)S(1)}, u32[]{:S(2)}, u32[]{:S(2)}) %collective-permute-start.3) | collective-permute-done | bytes 320 | tf_op jit(solution)/shard_map/while/body/eval_jaxpr/ppermute | solution.py:22
  118.2 3.3 collective-permute-done.1
  125.0 4.3 %collective-permute-done.3 = f32[2,2,18,1]{3,2,1,0:T(8,128)S(1)} collective-permute-done((f32[2,2,18,1]{3,2,1,0:T(8,128)S(1)}, f32[2,2,18,1]{3,2,1,0:T(8,128)S(1)}, u32[]{:S(2)}, u32[]{:S(2)}) %collective-permute-start.3) | collective-permute-done | bytes 320 | tf_op jit(solution)/shard_map/while/body/eval_jaxpr/ppermute | solution.py:22
  134.7 3.3 collective-permute-done.1
  141.5 4.3 %collective-permute-done.3 = f32[2,2,18,1]{3,2,1,0:T(8,128)S(1)} collective-permute-done((f32[2,2,18,1]{3,2,1,0:T(8,128)S(1)}, f32[2,2,18,1]{3,2,1,0:T(8,128)S(1)}, u32[]{:S(2)}, u32[]{:S(2)}) %collective-permute-start.3) | collective-permute-done | bytes 320 | tf_op jit(solution)/shard_map/while/body/eval_jaxpr/ppermute | solution.py:22
  151.2 3.3 collective-permute-done.1
  158.0 4.3 %collective-permute-done.3 = f32[2,2,18,1]{3,2,1,0:T(8,128)S(1)} collective-permute-done((f32[2,2,18,1]{3,2,1,0:T(8,128)S(1)}, f32[2,2,18,1]{3,2,1,0:T(8,128)S(1)}, u32[]{:S(2)}, u32[]{:S(2)}) %collective-permute-start.3) | collective-permute-done | bytes 320 | tf_op jit(solution)/shard_map/while/body/eval_jaxpr/ppermute | solution.py:22
  167.7 3.3 collective-permute-done.1
  174.4 4.3 %collective-permute-done.3 = f32[2,2,18,1]{3,2,1,0:T(8,128)S(1)} collective-permute-done((f32[2,2,18,1]{3,2,1,0:T(8,128)S(1)}, f32[2,2,18,1]{3,2,1,0:T(8,128)S(1)}, u32[]{:S(2)}, u32[]{:S(2)}) %collective-permute-start.3) | collective-permute-done | bytes 320 | tf_op jit(solution)/shard_map/while/body/eval_jaxpr/ppermute | solution.py:22
  184.2 3.3 collective-permute-done.1
  190.9 4.3 %collective-permute-done.3 = f32[2,2,18,1]{3,2,1,0:T(8,128)S(1)} collective-permute-done((f32[2,2,18,1]{3,2,1,0:T(8,128)S(1)}, f32[2,2,18,1]{3,2,1,0:T(8,128)S(1)}, u32[]{:S(2)}, u32[]{:S(2)}) %collective-permute-start.3) | collective-permute-done | bytes 320 | tf_op jit(solution)/shard_map/while/body/eval_jaxpr/ppermute | solution.py:22
  200.7 3.3 collective-permute-done.1
  207.4 4.3 %collective-permute-done.3 = f32[2,2,18,1]{3,2,1,0:T(8,128)S(1)} collective-permute-done((f32[2,2,18,1]{3,2,1,0:T(8,128)S(1)}, f32[2,2,18,1]{3,2,1,0:T(8,128)S(1)}, u32[]{:S(2)}, u32[]{:S(2)}) %collective-permute-start.3) | collective-permute-done | bytes 320 | tf_op jit(solution)/shard_map/while/body/eval_jaxpr/ppermute | solution.py:22
  217.2 3.3 collective-permute-done.1
  223.9 4.3 %collective-permute-done.3 = f32[2,2,18,1]{3,2,1,0:T(8,128)S(1)} collective-permute-done((f32[2,2,18,1]{3,2,1,0:T(8,128)S(1)}, f32[2,2,18,1]{3,2,1,0:T(8,128)S(1)}, u32[]{:S(2)}, u32[]{:S(2)}) %collective-permute-start.3) | collective-permute-done | bytes 320 | tf_op jit(solution)/shard_map/while/body/eval_jaxpr/ppermute | solution.py:22
  233.7 3.3 collective-permute-done.1
  240.4 4.3 %collective-permute-done.3 = f32[2,2,18,1]{3,2,1,0:T(8,128)S(1)} collective-permute-done((f32[2,2,18,1]{3,2,1,0:T(8,128)S(1)}, f32[2,2,18,1]{3,2,1,0:T(8,128)S(1)}, u32[]{:S(2)}, u32[]{:S(2)}) %collective-permute-start.3) | collective-permute-done | bytes 320 | tf_op jit(solution)/shard_map/while/body/eval_jaxpr/ppermute | solution.py:22
  250.1 3.3 collective-permute-done.1
  256.9 4.3 %collective-permute-done.3 = f32[2,2,18,1]{3,2,1,0:T(8,128)S(1)} collective-permute-done((f32[2,2,18,1]{3,2,1,0:T(8,128)S(1)}, f32[2,2,18,1]{3,2,1,0:T(8,128)S(1)}, u32[]{:S(2)}, u32[]{:S(2)}) %collective-permute-start.3) | collective-permute-done | bytes 320 | tf_op jit(solution)/shard_map/while/body/eval_jaxpr/ppermute | solution.py:22
  266.6 3.3 collective-permute-done.1
  273.4 4.3 %collective-permute-done.3 = f32[2,2,18,1]{3,2,1,0:T(8,128)S(1)} collective-permute-done((f32[2,2,18,1]{3,2,1,0:T(8,128)S(1)}, f32[2,2,18,1]{3,2,1,0:T(8,128)S(1)}, u32[]{:S(2)}, u32[]{:S(2)}) %collective-permute-start.3) | collective-permute-done | bytes 320 | tf_op jit(solution)/shard_map/while/body/eval_jaxpr/ppermute | solution.py:22
  283.1 3.3 collective-permute-done.1
  289.9 4.3 %collective-permute-done.3 = f32[2,2,18,1]{3,2,1,0:T(8,128)S(1)} collective-permute-done((f32[2,2,18,1]{3,2,1,0:T(8,128)S(1)}, f32[2,2,18,1]{3,2,1,0:T(8,128)S(1)}, u32[]{:S(2)}, u32[]{:S(2)}) %collective-permute-start.3) | collective-permute-done | bytes 320 | tf_op jit(solution)/shard_map/while/body/eval_jaxpr/ppermute | solution.py:22
  299.6 3.3 collective-permute-done.1
  306.4 4.3 %collective-permute-done.3 = f32[2,2,18,1]{3,2,1,0:T(8,128)S(1)} collective-permute-done((f32[2,2,18,1]{3,2,1,0:T(8,128)S(1)}, f32[2,2,18,1]{3,2,1,0:T(8,128)S(1)}, u32[]{:S(2)}, u32[]{:S(2)}) %collective-permute-start.3) | collective-permute-done | bytes 320 | tf_op jit(solution)/shard_map/while/body/eval_jaxpr/ppermute | solution.py:22
  312.2 21.8 %fusion.19 = f32[64,64]{1,0:T(8,128)S(1)} fusion(f32[64,16,2048]{2,1,0:T(8,128)} %bitcast.63), kind=kOutput, calls=%fused_computation.39 | convolution fusion | flops 1610612736 | bytes 8404992 | tf_op jit(solution)/shard_map/gcxy,gdxy->gcd/dot_general | solution.py:102
  334.0 37.3 %psum.7 = f32[64,64]{1,0:T(8,128)S(1)} all-reduce(f32[64,64]{1,0:T(8,128)S(1)} %fusion.19), channel_id=1, replica_groups=mesh['space'=16,'tm'=2] {'space','tm'}, use_global_device_ids=true, to_apply=%region_2.3 | all-reduce | flops 4096 | bytes 32768 | tf_op jit(solution)/shard_map/psum | solution.py:103
  371.7 2.9 custom-call.10
  378.8 2.9 custom-call.11
  383.4 3.6 all-to-all-start.1
  387.0 12.6 %fusion.15 = f32[32,16,2048]{2,0,1:T(8,128)S(1)} fusion(f32[32,64,1]{1,0,2:T(8,128)S(1)} %convolution_bitcast_fusion, f32[64,16,2048]{2,1,0:T(8,128)} %bitcast.64), kind=kOutput, calls=%fused_computation.35 | convolution fusion | flops 805306368 | bytes 12591104 | tf_op jit(solution)/shard_map/gcxy,gcr->grxy/dot_general | solution.py:105
  399.6 4.4 %copy.35 = f32[32,16,2048]{2,1,0:T(8,128)} copy(f32[32,16,2048]{2,0,1:T(8,128)S(1)} %fusion.15) | data formatting | bytes 8388608
  (268 shorter events, 140.6 us)
Async XLA Ops:
  14.4 13.1 %all-to-all-start = ((f32[2,1,65536]{2,1,0:T(1,128)}), f32[2,1,65536]{2,1,0:T(1,128)S(1)}, u32[]{:S(2)}, u32[]{:S(2)}) async-start(f32[2,1,65536]{2,1,0:T(1,128)} %reshape.147), calls=%async_computation | async-start | bytes 1048576 | tf_op jit(solution)/shard_map/all_to_all | solution.py:83
  45.3 5.6 %collective-permute-start = (f32[2,2,1,2048]{3,2,1,0:T(1,128)S(1)}, f32[2,2,1,2048]{3,2,1,0:T(1,128)S(1)}, u32[]{:S(2)}, u32[]{:S(2)}) collective-permute-start(f32[2,2,1,2048]{3,2,1,0:T(1,128)S(1)} %get-tuple-element.239), channel_id=1, source_target_pairs={{2,0},{4,2},{6,4},{8,6},{10,8},{12,10},{14,12},{16,14},{18,16},{20... | collective-permute-start | bytes 98312 | tf_op jit(solution)/shard_map/while/body/eval_jaxpr/ppermute | solution.py:22
  48.7 6.0 %collective-permute-start.1 = (f32[2,2,1,2048]{3,2,1,0:T(1,128)S(1)}, f32[2,2,1,2048]{3,2,1,0:T(1,128)S(1)}, u32[]{:S(2)}, u32[]{:S(2)}) collective-permute-start(f32[2,2,1,2048]{3,2,1,0:T(1,128)S(1)} %get-tuple-element.240), channel_id=1, source_target_pairs={{0,2},{2,4},{4,6},{6,8},{8,10},{10,12},{12,14},{14,16},{16,18},{18... | collective-permute-start | bytes 98312 | tf_op jit(solution)/shard_map/while/body/eval_jaxpr/ppermute | solution.py:19
  54.8 4.3 %collective-permute-start.2 = (f32[2,2,18,1]{3,2,1,0:T(8,128)S(1)}, f32[2,2,18,1]{3,2,1,0:T(8,128)S(1)}, u32[]{:S(2)}, u32[]{:S(2)}) collective-permute-start(f32[2,2,18,1]{3,2,1,0:T(8,128)S(1)} %get-tuple-element.241), channel_id=1, source_target_pairs={{0,1},{2,3},{4,5},{6,7},{8,9},{10,11},{12,13},{14,15},{16,17},{18,... | collective-permute-start | bytes 872 | tf_op jit(solution)/shard_map/while/body/eval_jaxpr/ppermute | solution.py:19
  57.3 6.0 %collective-permute-start.3 = (f32[2,2,18,1]{3,2,1,0:T(8,128)S(1)}, f32[2,2,18,1]{3,2,1,0:T(8,128)S(1)}, u32[]{:S(2)}, u32[]{:S(2)}) collective-permute-start(f32[2,2,18,1]{3,2,1,0:T(8,128)S(1)} %get-tuple-element.242), channel_id=1, source_target_pairs={{1,0},{3,2},{5,4},{7,6},{9,8},{11,10},{13,12},{15,14},{17,16},{19,... | collective-permute-start | bytes 872 | tf_op jit(solution)/shard_map/while/body/eval_jaxpr/ppermute | solution.py:22
  66.0 6.1 %collective-permute-start.1 = (f32[2,2,1,2048]{3,2,1,0:T(1,128)S(1)}, f32[2,2,1,2048]{3,2,1,0:T(1,128)S(1)}, u32[]{:S(2)}, u32[]{:S(2)}) collective-permute-start(f32[2,2,1,2048]{3,2,1,0:T(1,128)S(1)} %get-tuple-element.240), channel_id=1, source_target_pairs={{0,2},{2,4},{4,6},{6,8},{8,10},{10,12},{12,14},{14,16},{16,18},{18... | collective-permute-start | bytes 98312 | tf_op jit(solution)/shard_map/while/body/eval_jaxpr/ppermute | solution.py:19
  72.2 3.3 collective-permute-start.2
  73.8 6.0 %collective-permute-start.3 = (f32[2,2,18,1]{3,2,1,0:T(8,128)S(1)}, f32[2,2,18,1]{3,2,1,0:T(8,128)S(1)}, u32[]{:S(2)}, u32[]{:S(2)}) collective-permute-start(f32[2,2,18,1]{3,2,1,0:T(8,128)S(1)} %get-tuple-element.242), channel_id=1, source_target_pairs={{1,0},{3,2},{5,4},{7,6},{9,8},{11,10},{13,12},{15,14},{17,16},{19,... | collective-permute-start | bytes 872 | tf_op jit(solution)/shard_map/while/body/eval_jaxpr/ppermute | solution.py:22
  82.5 6.1 %collective-permute-start.1 = (f32[2,2,1,2048]{3,2,1,0:T(1,128)S(1)}, f32[2,2,1,2048]{3,2,1,0:T(1,128)S(1)}, u32[]{:S(2)}, u32[]{:S(2)}) collective-permute-start(f32[2,2,1,2048]{3,2,1,0:T(1,128)S(1)} %get-tuple-element.240), channel_id=1, source_target_pairs={{0,2},{2,4},{4,6},{6,8},{8,10},{10,12},{12,14},{14,16},{16,18},{18... | collective-permute-start | bytes 98312 | tf_op jit(solution)/shard_map/while/body/eval_jaxpr/ppermute | solution.py:19
  88.7 3.3 collective-permute-start.2
  90.3 6.0 %collective-permute-start.3 = (f32[2,2,18,1]{3,2,1,0:T(8,128)S(1)}, f32[2,2,18,1]{3,2,1,0:T(8,128)S(1)}, u32[]{:S(2)}, u32[]{:S(2)}) collective-permute-start(f32[2,2,18,1]{3,2,1,0:T(8,128)S(1)} %get-tuple-element.242), channel_id=1, source_target_pairs={{1,0},{3,2},{5,4},{7,6},{9,8},{11,10},{13,12},{15,14},{17,16},{19,... | collective-permute-start | bytes 872 | tf_op jit(solution)/shard_map/while/body/eval_jaxpr/ppermute | solution.py:22
  99.0 6.1 %collective-permute-start.1 = (f32[2,2,1,2048]{3,2,1,0:T(1,128)S(1)}, f32[2,2,1,2048]{3,2,1,0:T(1,128)S(1)}, u32[]{:S(2)}, u32[]{:S(2)}) collective-permute-start(f32[2,2,1,2048]{3,2,1,0:T(1,128)S(1)} %get-tuple-element.240), channel_id=1, source_target_pairs={{0,2},{2,4},{4,6},{6,8},{8,10},{10,12},{12,14},{14,16},{16,18},{18... | collective-permute-start | bytes 98312 | tf_op jit(solution)/shard_map/while/body/eval_jaxpr/ppermute | solution.py:19
  105.2 3.3 collective-permute-start.2
  106.8 6.0 %collective-permute-start.3 = (f32[2,2,18,1]{3,2,1,0:T(8,128)S(1)}, f32[2,2,18,1]{3,2,1,0:T(8,128)S(1)}, u32[]{:S(2)}, u32[]{:S(2)}) collective-permute-start(f32[2,2,18,1]{3,2,1,0:T(8,128)S(1)} %get-tuple-element.242), channel_id=1, source_target_pairs={{1,0},{3,2},{5,4},{7,6},{9,8},{11,10},{13,12},{15,14},{17,16},{19,... | collective-permute-start | bytes 872 | tf_op jit(solution)/shard_map/while/body/eval_jaxpr/ppermute | solution.py:22
  115.5 6.1 %collective-permute-start.1 = (f32[2,2,1,2048]{3,2,1,0:T(1,128)S(1)}, f32[2,2,1,2048]{3,2,1,0:T(1,128)S(1)}, u32[]{:S(2)}, u32[]{:S(2)}) collective-permute-start(f32[2,2,1,2048]{3,2,1,0:T(1,128)S(1)} %get-tuple-element.240), channel_id=1, source_target_pairs={{0,2},{2,4},{4,6},{6,8},{8,10},{10,12},{12,14},{14,16},{16,18},{18... | collective-permute-start | bytes 98312 | tf_op jit(solution)/shard_map/while/body/eval_jaxpr/ppermute | solution.py:19
  121.7 3.3 collective-permute-start.2
  123.3 6.0 %collective-permute-start.3 = (f32[2,2,18,1]{3,2,1,0:T(8,128)S(1)}, f32[2,2,18,1]{3,2,1,0:T(8,128)S(1)}, u32[]{:S(2)}, u32[]{:S(2)}) collective-permute-start(f32[2,2,18,1]{3,2,1,0:T(8,128)S(1)} %get-tuple-element.242), channel_id=1, source_target_pairs={{1,0},{3,2},{5,4},{7,6},{9,8},{11,10},{13,12},{15,14},{17,16},{19,... | collective-permute-start | bytes 872 | tf_op jit(solution)/shard_map/while/body/eval_jaxpr/ppermute | solution.py:22
  132.0 6.1 %collective-permute-start.1 = (f32[2,2,1,2048]{3,2,1,0:T(1,128)S(1)}, f32[2,2,1,2048]{3,2,1,0:T(1,128)S(1)}, u32[]{:S(2)}, u32[]{:S(2)}) collective-permute-start(f32[2,2,1,2048]{3,2,1,0:T(1,128)S(1)} %get-tuple-element.240), channel_id=1, source_target_pairs={{0,2},{2,4},{4,6},{6,8},{8,10},{10,12},{12,14},{14,16},{16,18},{18... | collective-permute-start | bytes 98312 | tf_op jit(solution)/shard_map/while/body/eval_jaxpr/ppermute | solution.py:19
  138.1 3.3 collective-permute-start.2
  139.7 6.0 %collective-permute-start.3 = (f32[2,2,18,1]{3,2,1,0:T(8,128)S(1)}, f32[2,2,18,1]{3,2,1,0:T(8,128)S(1)}, u32[]{:S(2)}, u32[]{:S(2)}) collective-permute-start(f32[2,2,18,1]{3,2,1,0:T(8,128)S(1)} %get-tuple-element.242), channel_id=1, source_target_pairs={{1,0},{3,2},{5,4},{7,6},{9,8},{11,10},{13,12},{15,14},{17,16},{19,... | collective-permute-start | bytes 872 | tf_op jit(solution)/shard_map/while/body/eval_jaxpr/ppermute | solution.py:22
  148.4 6.1 %collective-permute-start.1 = (f32[2,2,1,2048]{3,2,1,0:T(1,128)S(1)}, f32[2,2,1,2048]{3,2,1,0:T(1,128)S(1)}, u32[]{:S(2)}, u32[]{:S(2)}) collective-permute-start(f32[2,2,1,2048]{3,2,1,0:T(1,128)S(1)} %get-tuple-element.240), channel_id=1, source_target_pairs={{0,2},{2,4},{4,6},{6,8},{8,10},{10,12},{12,14},{14,16},{16,18},{18... | collective-permute-start | bytes 98312 | tf_op jit(solution)/shard_map/while/body/eval_jaxpr/ppermute | solution.py:19
  154.6 3.3 collective-permute-start.2
  156.2 6.0 %collective-permute-start.3 = (f32[2,2,18,1]{3,2,1,0:T(8,128)S(1)}, f32[2,2,18,1]{3,2,1,0:T(8,128)S(1)}, u32[]{:S(2)}, u32[]{:S(2)}) collective-permute-start(f32[2,2,18,1]{3,2,1,0:T(8,128)S(1)} %get-tuple-element.242), channel_id=1, source_target_pairs={{1,0},{3,2},{5,4},{7,6},{9,8},{11,10},{13,12},{15,14},{17,16},{19,... | collective-permute-start | bytes 872 | tf_op jit(solution)/shard_map/while/body/eval_jaxpr/ppermute | solution.py:22
  164.9 6.1 %collective-permute-start.1 = (f32[2,2,1,2048]{3,2,1,0:T(1,128)S(1)}, f32[2,2,1,2048]{3,2,1,0:T(1,128)S(1)}, u32[]{:S(2)}, u32[]{:S(2)}) collective-permute-start(f32[2,2,1,2048]{3,2,1,0:T(1,128)S(1)} %get-tuple-element.240), channel_id=1, source_target_pairs={{0,2},{2,4},{4,6},{6,8},{8,10},{10,12},{12,14},{14,16},{16,18},{18... | collective-permute-start | bytes 98312 | tf_op jit(solution)/shard_map/while/body/eval_jaxpr/ppermute | solution.py:19
  171.1 3.3 collective-permute-start.2
  172.7 6.0 %collective-permute-start.3 = (f32[2,2,18,1]{3,2,1,0:T(8,128)S(1)}, f32[2,2,18,1]{3,2,1,0:T(8,128)S(1)}, u32[]{:S(2)}, u32[]{:S(2)}) collective-permute-start(f32[2,2,18,1]{3,2,1,0:T(8,128)S(1)} %get-tuple-element.242), channel_id=1, source_target_pairs={{1,0},{3,2},{5,4},{7,6},{9,8},{11,10},{13,12},{15,14},{17,16},{19,... | collective-permute-start | bytes 872 | tf_op jit(solution)/shard_map/while/body/eval_jaxpr/ppermute | solution.py:22
  181.4 6.1 %collective-permute-start.1 = (f32[2,2,1,2048]{3,2,1,0:T(1,128)S(1)}, f32[2,2,1,2048]{3,2,1,0:T(1,128)S(1)}, u32[]{:S(2)}, u32[]{:S(2)}) collective-permute-start(f32[2,2,1,2048]{3,2,1,0:T(1,128)S(1)} %get-tuple-element.240), channel_id=1, source_target_pairs={{0,2},{2,4},{4,6},{6,8},{8,10},{10,12},{12,14},{14,16},{16,18},{18... | collective-permute-start | bytes 98312 | tf_op jit(solution)/shard_map/while/body/eval_jaxpr/ppermute | solution.py:19
  187.6 3.3 collective-permute-start.2
  189.2 6.0 %collective-permute-start.3 = (f32[2,2,18,1]{3,2,1,0:T(8,128)S(1)}, f32[2,2,18,1]{3,2,1,0:T(8,128)S(1)}, u32[]{:S(2)}, u32[]{:S(2)}) collective-permute-start(f32[2,2,18,1]{3,2,1,0:T(8,128)S(1)} %get-tuple-element.242), channel_id=1, source_target_pairs={{1,0},{3,2},{5,4},{7,6},{9,8},{11,10},{13,12},{15,14},{17,16},{19,... | collective-permute-start | bytes 872 | tf_op jit(solution)/shard_map/while/body/eval_jaxpr/ppermute | solution.py:22
  197.9 6.1 %collective-permute-start.1 = (f32[2,2,1,2048]{3,2,1,0:T(1,128)S(1)}, f32[2,2,1,2048]{3,2,1,0:T(1,128)S(1)}, u32[]{:S(2)}, u32[]{:S(2)}) collective-permute-start(f32[2,2,1,2048]{3,2,1,0:T(1,128)S(1)} %get-tuple-element.240), channel_id=1, source_target_pairs={{0,2},{2,4},{4,6},{6,8},{8,10},{10,12},{12,14},{14,16},{16,18},{18... | collective-permute-start | bytes 98312 | tf_op jit(solution)/shard_map/while/body/eval_jaxpr/ppermute | solution.py:19
  204.1 3.3 collective-permute-start.2
  205.7 6.0 %collective-permute-start.3 = (f32[2,2,18,1]{3,2,1,0:T(8,128)S(1)}, f32[2,2,18,1]{3,2,1,0:T(8,128)S(1)}, u32[]{:S(2)}, u32[]{:S(2)}) collective-permute-start(f32[2,2,18,1]{3,2,1,0:T(8,128)S(1)} %get-tuple-element.242), channel_id=1, source_target_pairs={{1,0},{3,2},{5,4},{7,6},{9,8},{11,10},{13,12},{15,14},{17,16},{19,... | collective-permute-start | bytes 872 | tf_op jit(solution)/shard_map/while/body/eval_jaxpr/ppermute | solution.py:22
  214.4 6.1 %collective-permute-start.1 = (f32[2,2,1,2048]{3,2,1,0:T(1,128)S(1)}, f32[2,2,1,2048]{3,2,1,0:T(1,128)S(1)}, u32[]{:S(2)}, u32[]{:S(2)}) collective-permute-start(f32[2,2,1,2048]{3,2,1,0:T(1,128)S(1)} %get-tuple-element.240), channel_id=1, source_target_pairs={{0,2},{2,4},{4,6},{6,8},{8,10},{10,12},{12,14},{14,16},{16,18},{18... | collective-permute-start | bytes 98312 | tf_op jit(solution)/shard_map/while/body/eval_jaxpr/ppermute | solution.py:19
  220.6 3.3 collective-permute-start.2
  222.2 6.0 %collective-permute-start.3 = (f32[2,2,18,1]{3,2,1,0:T(8,128)S(1)}, f32[2,2,18,1]{3,2,1,0:T(8,128)S(1)}, u32[]{:S(2)}, u32[]{:S(2)}) collective-permute-start(f32[2,2,18,1]{3,2,1,0:T(8,128)S(1)} %get-tuple-element.242), channel_id=1, source_target_pairs={{1,0},{3,2},{5,4},{7,6},{9,8},{11,10},{13,12},{15,14},{17,16},{19,... | collective-permute-start | bytes 872 | tf_op jit(solution)/shard_map/while/body/eval_jaxpr/ppermute | solution.py:22
  230.9 6.1 %collective-permute-start.1 = (f32[2,2,1,2048]{3,2,1,0:T(1,128)S(1)}, f32[2,2,1,2048]{3,2,1,0:T(1,128)S(1)}, u32[]{:S(2)}, u32[]{:S(2)}) collective-permute-start(f32[2,2,1,2048]{3,2,1,0:T(1,128)S(1)} %get-tuple-element.240), channel_id=1, source_target_pairs={{0,2},{2,4},{4,6},{6,8},{8,10},{10,12},{12,14},{14,16},{16,18},{18... | collective-permute-start | bytes 98312 | tf_op jit(solution)/shard_map/while/body/eval_jaxpr/ppermute | solution.py:19
  237.1 3.3 collective-permute-start.2
  238.7 6.0 %collective-permute-start.3 = (f32[2,2,18,1]{3,2,1,0:T(8,128)S(1)}, f32[2,2,18,1]{3,2,1,0:T(8,128)S(1)}, u32[]{:S(2)}, u32[]{:S(2)}) collective-permute-start(f32[2,2,18,1]{3,2,1,0:T(8,128)S(1)} %get-tuple-element.242), channel_id=1, source_target_pairs={{1,0},{3,2},{5,4},{7,6},{9,8},{11,10},{13,12},{15,14},{17,16},{19,... | collective-permute-start | bytes 872 | tf_op jit(solution)/shard_map/while/body/eval_jaxpr/ppermute | solution.py:22
  247.4 6.1 %collective-permute-start.1 = (f32[2,2,1,2048]{3,2,1,0:T(1,128)S(1)}, f32[2,2,1,2048]{3,2,1,0:T(1,128)S(1)}, u32[]{:S(2)}, u32[]{:S(2)}) collective-permute-start(f32[2,2,1,2048]{3,2,1,0:T(1,128)S(1)} %get-tuple-element.240), channel_id=1, source_target_pairs={{0,2},{2,4},{4,6},{6,8},{8,10},{10,12},{12,14},{14,16},{16,18},{18... | collective-permute-start | bytes 98312 | tf_op jit(solution)/shard_map/while/body/eval_jaxpr/ppermute | solution.py:19
  253.5 3.3 collective-permute-start.2
  255.1 6.0 %collective-permute-start.3 = (f32[2,2,18,1]{3,2,1,0:T(8,128)S(1)}, f32[2,2,18,1]{3,2,1,0:T(8,128)S(1)}, u32[]{:S(2)}, u32[]{:S(2)}) collective-permute-start(f32[2,2,18,1]{3,2,1,0:T(8,128)S(1)} %get-tuple-element.242), channel_id=1, source_target_pairs={{1,0},{3,2},{5,4},{7,6},{9,8},{11,10},{13,12},{15,14},{17,16},{19,... | collective-permute-start | bytes 872 | tf_op jit(solution)/shard_map/while/body/eval_jaxpr/ppermute | solution.py:22
  263.9 6.1 %collective-permute-start.1 = (f32[2,2,1,2048]{3,2,1,0:T(1,128)S(1)}, f32[2,2,1,2048]{3,2,1,0:T(1,128)S(1)}, u32[]{:S(2)}, u32[]{:S(2)}) collective-permute-start(f32[2,2,1,2048]{3,2,1,0:T(1,128)S(1)} %get-tuple-element.240), channel_id=1, source_target_pairs={{0,2},{2,4},{4,6},{6,8},{8,10},{10,12},{12,14},{14,16},{16,18},{18... | collective-permute-start | bytes 98312 | tf_op jit(solution)/shard_map/while/body/eval_jaxpr/ppermute | solution.py:19
  271.6 6.0 %collective-permute-start.3 = (f32[2,2,18,1]{3,2,1,0:T(8,128)S(1)}, f32[2,2,18,1]{3,2,1,0:T(8,128)S(1)}, u32[]{:S(2)}, u32[]{:S(2)}) collective-permute-start(f32[2,2,18,1]{3,2,1,0:T(8,128)S(1)} %get-tuple-element.242), channel_id=1, source_target_pairs={{1,0},{3,2},{5,4},{7,6},{9,8},{11,10},{13,12},{15,14},{17,16},{19,... | collective-permute-start | bytes 872 | tf_op jit(solution)/shard_map/while/body/eval_jaxpr/ppermute | solution.py:22
  280.4 6.1 %collective-permute-start.1 = (f32[2,2,1,2048]{3,2,1,0:T(1,128)S(1)}, f32[2,2,1,2048]{3,2,1,0:T(1,128)S(1)}, u32[]{:S(2)}, u32[]{:S(2)}) collective-permute-start(f32[2,2,1,2048]{3,2,1,0:T(1,128)S(1)} %get-tuple-element.240), channel_id=1, source_target_pairs={{0,2},{2,4},{4,6},{6,8},{8,10},{10,12},{12,14},{14,16},{16,18},{18... | collective-permute-start | bytes 98312 | tf_op jit(solution)/shard_map/while/body/eval_jaxpr/ppermute | solution.py:19
  288.2 6.0 %collective-permute-start.3 = (f32[2,2,18,1]{3,2,1,0:T(8,128)S(1)}, f32[2,2,18,1]{3,2,1,0:T(8,128)S(1)}, u32[]{:S(2)}, u32[]{:S(2)}) collective-permute-start(f32[2,2,18,1]{3,2,1,0:T(8,128)S(1)} %get-tuple-element.242), channel_id=1, source_target_pairs={{1,0},{3,2},{5,4},{7,6},{9,8},{11,10},{13,12},{15,14},{17,16},{19,... | collective-permute-start | bytes 872 | tf_op jit(solution)/shard_map/while/body/eval_jaxpr/ppermute | solution.py:22
  296.9 6.1 %collective-permute-start.1 = (f32[2,2,1,2048]{3,2,1,0:T(1,128)S(1)}, f32[2,2,1,2048]{3,2,1,0:T(1,128)S(1)}, u32[]{:S(2)}, u32[]{:S(2)}) collective-permute-start(f32[2,2,1,2048]{3,2,1,0:T(1,128)S(1)} %get-tuple-element.240), channel_id=1, source_target_pairs={{0,2},{2,4},{4,6},{6,8},{8,10},{10,12},{12,14},{14,16},{16,18},{18... | collective-permute-start | bytes 98312 | tf_op jit(solution)/shard_map/while/body/eval_jaxpr/ppermute | solution.py:19
  304.7 6.0 %collective-permute-start.3 = (f32[2,2,18,1]{3,2,1,0:T(8,128)S(1)}, f32[2,2,18,1]{3,2,1,0:T(8,128)S(1)}, u32[]{:S(2)}, u32[]{:S(2)}) collective-permute-start(f32[2,2,18,1]{3,2,1,0:T(8,128)S(1)} %get-tuple-element.242), channel_id=1, source_target_pairs={{1,0},{3,2},{5,4},{7,6},{9,8},{11,10},{13,12},{15,14},{17,16},{19,... | collective-permute-start | bytes 872 | tf_op jit(solution)/shard_map/while/body/eval_jaxpr/ppermute | solution.py:22
  383.4 20.6 %all-to-all-start.1 = ((f32[2,2,16,2048]{3,2,1,0:T(8,128)}), f32[2,2,16,2048]{3,2,1,0:T(8,128)S(1)}, u32[]{:S(2)}, u32[]{:S(2)}) async-start(f32[2,2,16,2048]{3,2,1,0:T(8,128)} %get-tuple-element.62), calls=%async_computation.1 | async-start | bytes 1048576 | tf_op jit(solution)/shard_map/all_to_all | solution.py:106
  (26 other events, 279.7 us)
where the time goes:
time: 408 us; the launch traced here: 405 us
  waiting for transfers between devices  128 us (31%)
  starting transfers between devices  66.6 us (16%)
  local copies, waits for them, and re-layouts  61.7 us (15%)
  other arithmetic  56 us (14%)
  blocking collectives  44 us (11%)
  matrix products  36 us (9%)
  loops' own time  11.4 us (3%)
    ppermute x32, waiting for transfers between devices, with_halo(): lax.ppermute(lax.slice_in_dim(block, 0, width, axis=dim), axis, backward)  68.1 us
    ppermute x32, waiting for transfers between devices, with_halo(): lax.ppermute(lax.slice_in_dim(block, block.shape[dim] - width, None, axis...  59.6 us
    psum x1, blocking collectives, body(): gram = lax.psum(gram, ('space', 'tm'))  37.3 us
    ppermute x32, starting transfers between devices, with_halo(): lax.ppermute(lax.slice_in_dim(block, block.shape[dim] - width, None, axis...  33.9 us
    unnamed x24, local copies, waits for them, and re-layouts  33.4 us
    dynamic_update_slice x16, other arithmetic, run_steps(): final, snaps = lax.scan(stepper, state, jnp.arange(STEPS, dtype=jnp.int32))  25.1 us
    ppermute x32, starting transfers between devices, with_halo(): lax.ppermute(lax.slice_in_dim(block, 0, width, axis=dim), axis, backward)  24.9 us
    dot_general x1, matrix products, body(): gram = jnp.einsum('gcxy,gdxy->gcd', joined, joined, precision=highest)  21.8 us
  transfers between devices with their start and end apart: 66, of which 48 were waited for; matrix products, arithmetic and copies ran while one was open for 11% of the time, Pallas kernels for 0%

commit v1 on v0

v1 whole, which is shorter than its diff:
```python
import functools

import jax
import jax.numpy as jnp
import numpy as np
from jax import lax
from jax.experimental import pallas as pl
from jax.experimental.pallas import tpu as pltpu
from jax.sharding import PartitionSpec as P

STEPS = 16
KAPPA = (0.06, 0.02)
HIGHEST = lax.Precision.HIGHEST
AXES = ("space", "tm")
TILE = 128
GUARD = 8
BATCH = 4
VMEM = pl.BlockSpec(memory_space=pltpu.VMEM)
SMEM = pl.BlockSpec(memory_space=pltpu.SMEM)


def mm(a, b):
    return jnp.dot(a, b, precision=HIGHEST, preferred_element_type=jnp.float32)


def mm_nt(a, b):
    return lax.dot_general(
        a, b, (((1,), (1,)), ((), ())), precision=HIGHEST, preferred_element_type=jnp.float32
    )


def lanes_of(shape):
    return lax.broadcasted_iota(jnp.int32, shape, len(shape) - 1)


def pack_kernel(groups, block, step_ref, state_ref, vx, vy, amp, freq, phase, own_ref, *peer_refs):
    full = vx.shape[1]
    me = lax.axis_index("tm")
    start = step_ref[0].astype(jnp.float32)
    rows = vx.shape[0]
    lane = lanes_of((rows, TILE))

    def cut(read, target, write, is_state):
        first = target * block
        write(pl.ds(0, block), read(pl.ds(pl.multiple_of(first, TILE), block)))
        above = jnp.minimum(first + block, full - TILE)
        below = jnp.maximum(first - TILE, 0)
        high = read(pl.ds(pl.multiple_of(above, TILE), TILE))
        low = read(pl.ds(pl.multiple_of(below, TILE), TILE))
        high = jnp.where(target < groups - 1, high, 0.0)
        low = jnp.where(target > 0, low, 0.0)
        halo = jnp.where(lane < TILE // 2, high, low)
        if is_state:
            halo = jnp.where((lane >= TILE // 4) & (lane < 3 * TILE // 4), start, halo)
        write(pl.ds(block, TILE), halo)

    def writer(ref, index):
        def write(columns, value):
            ref[index, :, columns] = value

        return write

    for index, ref in enumerate((vx, vy, amp, freq, phase)):
        cut(lambda columns, ref=ref: ref[:, columns], me, writer(own_ref, index), False)
    for shift in range(groups):
        target = lax.rem(me + shift, groups)
        for field in range(2):
            if shift == 0:
                write = writer(own_ref, 5 + field)
            else:
                write = writer(peer_refs[shift - 1], field)
            cut(lambda columns, field=field: state_ref[0, field, :, columns], target, write, True)


def sin_cos(angle):
    turns = jnp.floor(angle * np.float32(2.0 / np.pi) + 0.5)
    r = angle - turns * np.float32(1.5703125)
    r = r - turns * np.float32(4.837512969970703125e-4)
    r = r - turns * np.float32(7.54978995489188216e-8)
    z = r * r
    sine = r + r * z * (
        np.float32(-1.6666654611e-1)
        + z * (np.float32(8.3321608736e-3) + z * np.float32(-1.9515295891e-4))
    )
    cosine = (
        1.0
        - 0.5 * z
        + z
        * z
        * (
            np.float32(4.166664568298827e-2)
            + z * (np.float32(-1.388731625493765e-3) + z * np.float32(2.443315711809948e-5))
        )
    )
    quadrant = turns.astype(jnp.int32)
    odd = (quadrant & 1) == 1
    s = jnp.where(odd, cosine, sine)
    c = jnp.where(odd, sine, cosine)
    s = jnp.where((quadrant & 2) == 2, -s, s)
    c = jnp.where(((quadrant + 1) & 2) == 2, -c, c)
    return s, c


def stencil_kernel(groups, halves, with_left, *refs):
    count = 3 * groups
    sources = [refs[3 * i : 3 * i + 3] for i in range(groups)]
    refs = refs[count:]
    if with_left:
        select_ref, fold_ref = refs[:2]
        refs = refs[2:]
        snap_ref, end_ref, left_ref = refs[:3]
        refs = refs[3:]
    else:
        snap_ref, end_ref = refs[:2]
        refs = refs[2:]
    qa, qb, xa, xb, twice, cw, ce, cs, cn, c0 = refs
    rows = sources[0][0].shape[1]
    block = sources[0][0].shape[2] - TILE
    length = block // halves
    tiles = length // TILE + 1
    subs = halves * groups * 2
    total = 3 * rows
    me = lax.axis_index("tm")

    sub = lax.broadcasted_iota(jnp.int32, (1, subs, TILE), 1)
    kappa = jnp.where((sub & 1) == 0, np.float32(KAPPA[0]), np.float32(KAPPA[1]))
    half_of = sub // (2 * groups)
    lane3 = lanes_of((1, subs, TILE))
    lowest = (me == 0) & (half_of == 0) & (lane3 >= TILE // 2)
    highest = (me == groups - 1) & (half_of == halves - 1) & (lane3 < TILE // 2)
    inside = jnp.where(lowest | highest, 0.0, 1.0).astype(jnp.float32)
    lane2 = lanes_of((8, TILE))

    for guard in (GUARD - 1, GUARD + total):
        qa[guard] = jnp.zeros(qa.shape[1:], jnp.float32)
        qb[guard] = jnp.zeros(qb.shape[1:], jnp.float32)

    def turned(parts):
        return jnp.swapaxes(jnp.stack(parts, axis=0), 0, 1)

    def prepare(place, base, tile, halo):
        def cut(ref, index, half):
            line = pl.ds(base, 8)
            if not halo:
                return ref[index, line, pl.ds(pl.multiple_of(half * length + tile * TILE, TILE), TILE)]
            above = (half + 1) * length
            below = half * length - TILE if half > 0 else block
            high = ref[index, line, above : above + TILE]
            if above == below:
                return high
            low = ref[index, line, below : below + TILE]
            return jnp.where(lane2 < TILE // 2, high, low)

        own = sources[0][place]
        starts, first, second, flow_x, flow_y, doubled = [], [], [], [], [], []
        for half in range(halves):
            vx, vy, amp, freq, phase = (cut(own, index, half) for index in range(5))
            sin_f, cos_f = sin_cos(freq)
            for group in range(groups):
                ref, at = sources[group][place], 5 if group == 0 else 0
                step = ref[at, pl.ds(base, 8), block : block + TILE][:, TILE // 2 : TILE // 2 + 1]
                s, c = sin_cos(freq * step + phase)
                s, c = amp * s, amp * c
                for field in range(2):
                    starts.append(cut(ref, at + field, half))
                    x, y = (s, c) if field == 0 else (0.5 * c, -0.5 * s)
                    first.append(x)
                    second.append(x * cos_f + y * sin_f)
                    flow_x.append(vx)
                    flow_y.append(vy)
                    doubled.append(2.0 * cos_f)
        where = pl.ds(place * rows + base, 8)
        columns = pl.ds(pl.multiple_of(tile * TILE, TILE), TILE)
        vx, vy = turned(flow_x), turned(flow_y)
        west = kappa + jnp.maximum(vx, 0.0)
        east = kappa - jnp.minimum(vx, 0.0)
        south = kappa + jnp.maximum(vy, 0.0)
        north = kappa - jnp.minimum(vy, 0.0)
        centre = 1.0 - (west + east + south + north)
        state, x0, x1 = turned(starts), turned(first), turned(second)
        if halo:
            west, east, south, north, centre, state, x0, x1 = (
                v * inside for v in (west, east, south, north, centre, state, x0, x1)
            )
        cw[where, :, columns] = west
        ce[where, :, columns] = east
        cs[where, :, columns] = south
        cn[where, :, columns] = north
        c0[where, :, columns] = centre
        xa[where, :, columns] = x0
        xb[where, :, columns] = x1
        twice[where, :, columns] = turned(doubled)
        qa[pl.ds(GUARD + place * rows + base, 8), :, columns] = state

    for place in range(3):

        def by_rows(number, carry, place=place):
            base = pl.multiple_of(number * 8, 8)

            def by_tiles(tile, inner):
                prepare(place, base, tile, False)
                return inner

            lax.fori_loop(0, tiles - 1, by_tiles, 0)
            prepare(place, base, tiles - 1, True)
            return carry

        lax.fori_loop(0, rows // 8, by_rows, 0)

    def advance(source, target, now, later, row, step, keep):
        for r in range(BATCH):
            x = row + r
            south = [
                pltpu.roll(source[GUARD + x, :, t * TILE : (t + 1) * TILE], 1, 1) for t in range(tiles)
            ]
            north = [
                pltpu.roll(source[GUARD + x, :, t * TILE : (t + 1) * TILE], TILE - 1, 1)
                for t in range(tiles)
            ]
            lane = lanes_of((subs, TILE))
            for t in range(tiles):
                cols = slice(t * TILE, (t + 1) * TILE)
                s = jnp.where(lane == 0, south[t - 1], south[t])
                n = jnp.where(lane == TILE - 1, north[(t + 1) % tiles], north[t])
                drive = now[x, :, cols]
                fresh = (
                    c0[x, :, cols] * source[GUARD + x, :, cols]
                    + cw[x, :, cols] * source[GUARD + x - 1, :, cols]
                    + ce[x, :, cols] * source[GUARD + x + 1, :, cols]
                    + cs[x, :, cols] * s
                    + cn[x, :, cols] * n
                    + drive
                )
                target[GUARD + x, :, cols] = fresh
                now[x, :, cols] = twice[x, :, cols] * later[x, :, cols] - drive
                if keep and t < tiles - 1:
                    snap_ref[x - rows, pl.ds(pl.multiple_of(step * subs, subs), subs), cols] = fresh

    def one(source, target, now, later, step):
        low = (step + 1) // BATCH
        high = (total - 1 - step + BATCH - 1) // BATCH

        def halo_rows(i, carry):
            advance(source, target, now, later, i * BATCH, step, False)
            return carry

        def own_rows(i, carry):
            advance(source, target, now, later, i * BATCH, step, True)
            return carry

        lax.fori_loop(low, rows // BATCH, halo_rows, 0)
        lax.fori_loop(rows // BATCH, 2 * rows // BATCH, own_rows, 0)
        lax.fori_loop(2 * rows // BATCH, high, halo_rows, 0)

    def pair(i, carry):
        one(qa, qb, xa, xb, 2 * i)
        one(qb, qa, xb, xa, 2 * i + 1)
        return carry

    lax.fori_loop(0, STEPS // 2, pair, 0)

    for base in range(0, rows, 8):
        for t in range(tiles - 1):
            cols = slice(t * TILE, (t + 1) * TILE)
            value = jnp.swapaxes(qa[GUARD + rows + base : GUARD + rows + base + 8, :, cols], 0, 1)
            for half in range(halves):
                for group in range(groups):
                    for field in range(2):
                        end_ref[
                            group, field, base : base + 8, half * length + t * TILE : half * length + (t + 1) * TILE
                        ] = value[half * groups * 2 + group * 2 + field]

    if with_left:
        width = STEPS * subs

        def add(x, gram):
            a = snap_ref[x]
            return gram + mm_nt(a, a)

        gram = lax.fori_loop(0, rows, add, jnp.zeros((width, width), jnp.float32))
        lane = lanes_of((1, width))
        left = jnp.zeros((select_ref.shape[0], width), jnp.float32)
        for half in range(halves):
            part = mm(select_ref[:, half * width : (half + 1) * width], gram)
            left = left + jnp.where((lane % subs) // (2 * groups) == half, part, 0.0)
        left_ref[...] = mm(left, fold_ref[...])


def eliminate(m, rank):
    row = lax.broadcasted_iota(jnp.int32, m.shape, 0)
    lane = lanes_of(m.shape)
    for k in range(rank):
        line = m[k : k + 1, :]
        pivot = m[k : k + 1, k : k + 1]
        column = m[:, k : k + 1] * (1.0 / pivot)
        m = m - jnp.where(row > k, column, 0.0) * line
    diagonal = jnp.sum(jnp.where(row == lane, m, 0.0), axis=1, keepdims=True)
    return m * lax.rsqrt(diagonal)


def merge_kernel(halves, subs, left_ref, spread_ref, unit_ref, expand_ref, snap_ref, out_ref):
    rank = left_ref.shape[0]
    wide = left_ref.shape[1]
    lane = lanes_of((rank, 128))
    whole = eliminate(mm(left_ref[...], spread_ref[...]) + unit_ref[...], rank)
    proj = jnp.where((lane >= rank) & (lane < rank + wide), whole, 0.0)
    outer = mm_nt(proj, proj)
    factor = eliminate(outer, rank)
    upper = jnp.where(
        lax.broadcasted_iota(jnp.int32, (rank, rank), 0) <= lanes_of((rank, rank)), factor, 0.0
    )
    mix = mm(upper, whole)
    width = snap_ref.shape[1]
    weights = jnp.concatenate(
        [mm(mix, expand_ref[:, half * width : (half + 1) * width]) for half in range(halves)], axis=0
    )
    rows = snap_ref.shape[0]
    length = snap_ref.shape[2]
    chunk = 256

    def columns(i, carry):
        at = pl.multiple_of(i * chunk, chunk)
        for base in range(0, rows, 8):
            parts = [mm(weights, snap_ref[base + x, :, pl.ds(at, chunk)]) for x in range(8)]
            for half in range(halves):
                for r in range(0, rank, 8):
                    first = half * rank + r
                    block = jnp.swapaxes(jnp.stack([p[first : first + 8] for p in parts], axis=0), 0, 1)
                    out_ref[r : r + 8, base : base + 8, pl.ds(pl.multiple_of(half * length + at, chunk), chunk)] = block
        return carry

    lax.fori_loop(0, length // chunk, columns, 0)


def shifted(value, along_space, along_tm):
    space, tm = lax.axis_size("space"), lax.axis_size("tm")
    moves = [
        (s * tm + t, (s + along_space) % space * tm + (t + along_tm) % tm)
        for s in range(space)
        for t in range(tm)
    ]
    return lax.ppermute(value, AXES, moves)


def turn(value, start):
    return lax.dynamic_slice_in_dim(jnp.concatenate([value, value]), start, value.shape[0], 0)


def total_of(value):
    size = lax.axis_size("space") * lax.axis_size("tm")
    if size & (size - 1):
        return lax.psum(value, AXES)
    bit = 1
    while bit < size:
        value = value + lax.ppermute(value, AXES, [(i, i ^ bit) for i in range(size)])
        bit *= 2
    return value


def coefficients(gram, sketch):
    left = jnp.dot(sketch.T, gram, precision=HIGHEST)
    small = jnp.dot(left, sketch, precision=HIGHEST)
    lower = jnp.linalg.cholesky(small)
    proj = lax.linalg.triangular_solve(lower, left, left_side=True, lower=True)
    outer = jnp.dot(proj, proj.T, precision=HIGHEST)
    factor = jnp.linalg.cholesky(outer)
    mix = lax.linalg.triangular_solve(lower, factor, left_side=True, lower=True, transpose_a=True)
    return jnp.dot(sketch, mix, precision=HIGHEST)


def merge_levels(pieces, sketch):
    while pieces.shape[0] > 1:
        count, columns, rows, length = pieces.shape
        joined = pieces.reshape(count // 2, 2 * columns, rows, length)
        gram = jnp.einsum("gcxy,gdxy->gcd", joined, joined, precision=HIGHEST)
        gram = lax.psum(gram, AXES)
        coeff = jax.vmap(coefficients, in_axes=(0, None))(gram, sketch)
        pieces = jnp.einsum("gcxy,gcr->grxy", joined, coeff, precision=HIGHEST)
    return pieces[0]


def body(start_state, start_step, velocity_x, velocity_y, amplitude, frequency, phase, sketch):
    groups = lax.axis_size("tm")
    me = lax.axis_index("tm")
    rows, full = velocity_x.shape
    block = full // groups
    halves = max(1, 8 // (2 * groups))
    subs = halves * groups * 2
    length = block // halves
    span = length + TILE
    width = STEPS * subs
    fast = groups == 2
    f32 = jnp.float32

    packed = pl.pallas_call(
        functools.partial(pack_kernel, groups, block),
        out_shape=[jax.ShapeDtypeStruct((7, rows, block + TILE), f32)]
        + [jax.ShapeDtypeStruct((2, rows, block + TILE), f32)] * (groups - 1),
        in_specs=[SMEM] + [VMEM] * 6,
        out_specs=[VMEM] * groups,
        name="pack",
    )(start_step, start_state, velocity_x, velocity_y, amplitude, frequency, phase)
    sources = [shifted(packed[0], 1, 0), packed[0], shifted(packed[0], -1, 0)]
    for shift in range(1, groups):
        sources += [shifted(packed[shift], move, shift) for move in (1, 0, -1)]

    extra = []
    if fast:
        column = np.arange(width)
        half_of = column % subs // (2 * groups)
        picks = np.zeros((groups, halves, 2 * STEPS * groups, width), np.float32)
        for member in range(groups):
            group = (member - column % (2 * groups) // 2) % groups
            index = group * 2 * STEPS + column % 2 * STEPS + column // subs
            picks[member, half_of, index, column] = 1.0
        pick = lax.dynamic_index_in_dim(jnp.asarray(picks), me, 0, keepdims=False)
        pick = jnp.concatenate([pick[half] for half in range(halves)], axis=1)
        select = jnp.dot(sketch.T, pick, precision=HIGHEST)
        fold = sum(pick[:, half * width : (half + 1) * width] for half in range(halves)).T
        rank, wide = sketch.shape[1], sketch.shape[0]
        spread = jnp.concatenate(
            [sketch, jnp.eye(wide, dtype=f32), jnp.zeros((wide, 128 - rank - wide), f32)], axis=1
        )
        unit = jnp.eye(rank, 128, 128 - rank, dtype=f32)
        expand = jnp.concatenate([jnp.zeros((128 - rank, halves * width), f32), select], axis=0)
        extra = [select, fold]

    outs = [
        jax.ShapeDtypeStruct((rows, width, length), f32),
        jax.ShapeDtypeStruct((groups, 2, rows, block), f32),
    ]
    if fast:
        outs.append(jax.ShapeDtypeStruct((sketch.shape[1], sketch.shape[0]), f32))
    grid_of = (3 * rows, subs, span)
    made = pl.pallas_call(
        functools.partial(stencil_kernel, groups, halves, fast),
        out_shape=outs,
        in_specs=[VMEM] * (len(sources) + len(extra)),
        out_specs=[VMEM] * len(outs),
        scratch_shapes=[pltpu.VMEM((3 * rows + 2 * GUARD, subs, span), f32)] * 2
        + [pltpu.VMEM(grid_of, f32)] * 8,
        compiler_params=pltpu.CompilerParams(vmem_limit_bytes=56 * 2**20),
        name="stencil",
    )(*sources, *extra)

    if fast:
        left = total_of(made[2])
        piece = pl.pallas_call(
            functools.partial(merge_kernel, halves, subs),
            out_shape=jax.ShapeDtypeStruct((rank, rows, block), f32),
            in_specs=[VMEM] * 5,
            out_specs=VMEM,
            compiler_params=pltpu.CompilerParams(vmem_limit_bytes=40 * 2**20),
            name="merge",
        )(left, spread, unit, expand, made[0])
    else:
        snaps = made[0].reshape(rows, STEPS, halves, groups, 2, length)
        snaps = jnp.transpose(snaps, (3, 4, 1, 0, 2, 5)).reshape(groups, 2 * STEPS, rows, block)
        snaps = turn(jnp.flip(snaps, 0), groups - 1 - me)
        piece = merge_levels(snaps, sketch)

    ends = [made[1][0]]
    for shift in range(1, groups):
        ends.append(shifted(made[1][shift], 0, groups - shift))
    if groups == 2:
        end_state = jnp.where(
            me == 0,
            jnp.concatenate([ends[0], ends[1]], axis=-1),
            jnp.concatenate([ends[1], ends[0]], axis=-1),
        )
    else:
        stacked = turn(jnp.stack(ends), groups - me)
        end_state = jnp.moveaxis(stacked, 0, -2).reshape(2, rows, full)
    return (piece, end_state[None])


def solution(mesh):
    placed = (
        P("tm", None, "space", None),
        P("tm"),
        P("space", None),
        P("space", None),
        P("space", None),
        P("space", None),
        P("space", None),
        P(),
    )
    return jax.shard_map(
        body,
        mesh=mesh,
        in_specs=placed,
        out_specs=(P(None, "space", "tm"), P("tm", None, "space", None)),
        check_vma=False,
    )
```

time: 408 us -> 115 us (0.28)
  waiting for transfers between devices: 128 us -> 15.1 us
  Pallas kernels: 0 us -> 56.1 us
  other arithmetic: 56 us -> 3.24 us
  local copies, waits for them, and re-layouts: 61.7 us -> 9.11 us
  blocking collectives: 44 us -> 0 us
  starting transfers between devices: 66.6 us -> 27.7 us
  matrix products: 36 us -> 1.56 us
  loops' own time: 11.4 us -> 0 us
    ppermute x64 -> x11, waiting for transfers between devices: 128 us -> 15.1 us  [the longest x5 8.06 us: total_of(): lax.ppermute(value, AXES, [(i, i ^ bit) for i in range(size)])]
    pallas_call x0 -> x3, Pallas kernels: none -> 56.1 us  [the longest x1 40.9 us: body(): pl.pallas_call(functools.partial(stencil_kernel, groups, halves, fast), o...]
    psum x1 -> x0, blocking collectives: 37.3 us -> none  [body(): gram = lax.psum(gram, ('space', 'tm'))]
    dot_general x6 -> x1, matrix products: 35 us -> 1.56 us  [body(): select = jnp.dot(sketch.T, pick, precision=HIGHEST)]
    ppermute x64 -> x11, starting transfers between devices: 58.8 us -> 27.7 us  [the longest x5 14.7 us: total_of(): lax.ppermute(value, AXES, [(i, i ^ bit) for i in range(size)])]
    unnamed x24 -> x13, local copies, waits for them, and re-layouts: 33.4 us -> 6.32 us
    dynamic_update_slice x16 -> x0, other arithmetic: 25.1 us -> none  [run_steps(): final, snaps = lax.scan(stepper, state, jnp.arange(STEPS, dtype=jnp.int32))]
    while x16 -> x0, local copies, waits for them, and re-layouts: 16.7 us -> none
  transfers between devices with their start and end apart: 66 -> 11, of which waited for: 48 -> 7; matrix products, arithmetic and copies ran while one was open for 11% -> 6% of each run, Pallas kernels for 0% -> 11%
where the time goes in v1:
time: 115 us; the launch traced here: 114 us
  Pallas kernels  56.1 us (49%)
  starting transfers between devices  27.7 us (24%)
  waiting for transfers between devices  15.1 us (13%)
  local copies, waits for them, and re-layouts  9.11 us (8%)
  other arithmetic  3.24 us (3%)
  matrix products  1.56 us (1%)
  between operations  1.34 us (1%)
    pallas_call x1, Pallas kernels, body(): pl.pallas_call(functools.partial(stencil_kernel, groups, halves, fast), o...  40.9 us
    ppermute x5, starting transfers between devices, total_of(): lax.ppermute(value, AXES, [(i, i ^ bit) for i in range(size)])  14.7 us
    ppermute x6, starting transfers between devices, shifted(): return lax.ppermute(value, AXES, moves)  13 us
    pallas_call x1, Pallas kernels, body(): pl.pallas_call(functools.partial(merge_kernel, halves, subs), out_shape=j...  12.6 us
    ppermute x5, waiting for transfers between devices, total_of(): lax.ppermute(value, AXES, [(i, i ^ bit) for i in range(size)])  8.06 us
    ppermute x6, waiting for transfers between devices, shifted(): return lax.ppermute(value, AXES, moves)  7.07 us
    unnamed x13, local copies, waits for them, and re-layouts  6.32 us
    pallas_call x1, Pallas kernels, body(): pl.pallas_call(functools.partial(pack_kernel, groups, block), out_shape=[...  2.54 us
  transfers between devices with their start and end apart: 11, of which 7 were waited for; matrix products, arithmetic and copies ran while one was open for 6% of the time, Pallas kernels for 11%

profile of v1, /device:TPU:0, one launch (start us, length us, event | category | flops | bytes accessed | tf_op | source)
XLA Modules:
  0.0 114.2 jit_solution(8812805552822582683)
XLA Ops:
  1.3 2.5 %pack.1 = (f32[7,16,2176]{2,1,0:T(8,128)}, f32[2,16,2176]{2,1,0:T(8,128)}) custom-call(s32[1]{0:T(128)S(6)} %copy.12.step_ref, f32[1,2,16,4096]{3,2,1,0:T(8,128)} %state_ref.1, f32[16,4096]{1,0:T(8,128)} %vx.1, f32[16,4096]{1,0:T(8,128)} %vy.1, f32[16,4096]{1,0:T(8,128)} %amp.1, f32[16,4096]{1,0:T(8,128)} %freq.1, f32[16,4096]{1,0:T(8,128)} %phase.1), custom_call_target="tpu_custom_call" | custom-call | tf_op jit(solution)/shard_map/pack/pallas_call | solution.py:395
  3.8 0.5 collective-permute-start
  4.3 5.0 %collective-permute-start.1 = (f32[7,16,2176]{2,1,0:T(8,128)}, f32[7,16,2176]{2,1,0:T(8,128)S(1)}, u32[]{:S(2)}, u32[]{:S(2)}) collective-permute-start(f32[7,16,2176]{2,1,0:T(8,128)} %get-tuple-element.7.refs_1_), channel_id=1, source_target_pairs={{0,30},{1,31},{2,0},{3,1},{4,2},{5,3},{6,4},{7,5},{8,6},{9,7},{10,... | collective-permute-start | bytes 2924552 | tf_op jit(solution)/shard_map/ppermute | solution.py:342
  9.2 0.0 collective-permute-start.2
  9.2 2.0 %collective-permute-start.3 = (f32[2,16,2176]{2,1,0:T(8,128)}, f32[2,16,2176]{2,1,0:T(8,128)S(1)}, u32[]{:S(2)}, u32[]{:S(2)}) collective-permute-start(f32[2,16,2176]{2,1,0:T(8,128)} %get-tuple-element.8), channel_id=1, source_target_pairs={{0,1},{1,0},{2,3},{3,2},{4,5},{5,4},{6,7},{7,6},{8,9},{9,8},{10,11... | collective-permute-start | bytes 835592 | tf_op jit(solution)/shard_map/ppermute | solution.py:342
  11.2 5.1 %collective-permute-start.4 = (f32[2,16,2176]{2,1,0:T(8,128)}, f32[2,16,2176]{2,1,0:T(8,128)S(1)}, u32[]{:S(2)}, u32[]{:S(2)}) collective-permute-start(f32[2,16,2176]{2,1,0:T(8,128)} %get-tuple-element.8), channel_id=1, source_target_pairs={{0,31},{1,30},{2,1},{3,0},{4,3},{5,2},{6,5},{7,4},{8,7},{9,6},{10,... | collective-permute-start | bytes 835592 | tf_op jit(solution)/shard_map/ppermute | solution.py:342
  16.3 0.9 dynamic-slice_bitcast_fusion.1
  17.2 1.5 %add_bitcast_fusion.refs_7_ = f32[128,64]{1,0:T(8,128)} fusion(f32[2,2,64,128]{2,3,1,0:T(8,128)} %constant.18.clone, s32[]{:T(128)S(6)} %select_n.19, s32[]{:T(128)S(6)} %add.40), kind=kLoop, calls=%fused_computation.8 | loop fusion | flops 8192 | bytes 98312 | tf_op jit(solution)/shard_map/transpose | solution.py:419
  18.7 1.6 %convolution_bitcast_fusion.refs_6_ = f32[32,256]{1,0:T(8,128)} fusion(f32[64,32]{0,1:T(8,128)} %param.16, f32[64,128]{0,1:T(8,128)S(1)} %get-tuple-element.15, f32[64,128]{0,1:T(8,128)S(1)} %get-tuple-element.14), kind=kOutput, calls=%fused_computation | convolution fusion | flops 6307840 | bytes 106496 | tf_op jit(solution)/shard_map/dot_general | solution.py:418
  20.2 5.5 %collective-permute-done.2.refs_3_ = f32[2,16,2176]{2,1,0:T(8,128)S(1)} collective-permute-done((f32[2,16,2176]{2,1,0:T(8,128)}, f32[2,16,2176]{2,1,0:T(8,128)S(1)}, u32[]{:S(2)}, u32[]{:S(2)}) %collective-permute-start.2) | collective-permute-done | bytes 278560 | tf_op jit(solution)/shard_map/ppermute | solution.py:342
  25.8 0.0 copy-start.3
  25.8 1.5 %collective-permute-done.3.refs_4_ = f32[2,16,2176]{2,1,0:T(8,128)S(1)} collective-permute-done((f32[2,16,2176]{2,1,0:T(8,128)}, f32[2,16,2176]{2,1,0:T(8,128)S(1)}, u32[]{:S(2)}, u32[]{:S(2)}) %collective-permute-start.3) | collective-permute-done | bytes 278560 | tf_op jit(solution)/shard_map/ppermute | solution.py:342
  27.3 0.0 copy-start.4
  27.3 0.0 collective-permute-done.4.refs_5_
  27.3 0.0 copy-start.5
  27.3 0.0 collective-permute-done.refs_0_
  27.3 0.0 copy-start.1
  27.3 0.0 collective-permute-done.1.refs_2_
  27.3 0.0 copy-done.3
  27.3 0.7 copy-done.4
  28.0 0.1 copy-done.5
  28.1 0.4 copy-done.1
  28.6 0.0 copy-start.2
  28.6 0.9 copy-done.2
  29.5 40.9 %stencil.1 = (f32[16,128,1024]{2,1,0:T(8,128)}, f32[2,2,16,2048]{3,2,1,0:T(8,128)}, f32[32,64]{1,0:T(8,128)}) custom-call(f32[7,16,2176]{2,1,0:T(8,128)} %copy-done.1, f32[7,16,2176]{2,1,0:T(8,128)} %get-tuple-element.7.refs_1_, f32[7,16,2176]{2,1,0:T(8,128)} %copy-done.2, f32[2,16,2176]{2,1,0:T(8,128)} %copy-done.3, f32[2,16,2176]{2,1,0:T(8,128)} %copy-done.4, ...), custom_call_target="tpu_custom_call" | custom-call | tf_op jit(solution)/shard_map/stencil/pallas_call | solution.py:435
  70.4 0.5 collective-permute-start.5
  70.9 0.8 copy.11
  71.7 0.1 pad.7.clone
  71.8 2.6 %collective-permute-done.5 = f32[32,64]{1,0:T(8,128)S(1)} collective-permute-done((f32[32,64]{1,0:T(8,128)}, f32[32,64]{1,0:T(8,128)S(1)}, u32[]{:S(2)}, u32[]{:S(2)}) %collective-permute-start.5) | collective-permute-done | bytes 8224 | tf_op jit(solution)/shard_map/ppermute | solution.py:355
  74.4 0.7 add.33
  75.1 9.3 %collective-permute-start.6 = (f32[32,64]{1,0:T(8,128)S(1)}, f32[32,64]{1,0:T(8,128)S(1)}, u32[]{:S(2)}, u32[]{:S(2)}) collective-permute-start(f32[32,64]{1,0:T(8,128)S(1)} %add.33), channel_id=1, source_target_pairs={{0,2},{1,3},{2,0},{3,1},{4,6},{5,7},{6,4},{7,5},{8,10},{9,11},{10,... | collective-permute-start | bytes 24584 | tf_op jit(solution)/shard_map/ppermute | solution.py:355
  84.4 0.1 maximum_maximum_fusion.spread_ref
  84.5 0.8 collective-permute-done.6
  85.3 1.6 %collective-permute-start.7 = (f32[32,64]{1,0:T(8,128)S(1)}, f32[32,64]{1,0:T(8,128)S(1)}, u32[]{:S(2)}, u32[]{:S(2)}) collective-permute-start(f32[32,64]{1,0:T(8,128)S(1)} %add.34), channel_id=1, source_target_pairs={{0,4},{1,5},{2,6},{3,7},{4,0},{5,1},{6,2},{7,3},{8,12},{9,13},{10,... | collective-permute-start | bytes 24584 | tf_op jit(solution)/shard_map/ppermute | solution.py:355
  86.8 1.1 fusion.6
  87.9 0.6 collective-permute-start.10
  88.5 0.5 collective-permute-done.7
  89.0 1.1 collective-permute-start.8
  90.1 2.6 %collective-permute-done.8 = f32[32,64]{1,0:T(8,128)S(1)} collective-permute-done((f32[32,64]{1,0:T(8,128)S(1)}, f32[32,64]{1,0:T(8,128)S(1)}, u32[]{:S(2)}, u32[]{:S(2)}) %collective-permute-start.8) | collective-permute-done | bytes 8224 | tf_op jit(solution)/shard_map/ppermute | solution.py:355
  92.7 2.2 %collective-permute-start.9 = (f32[32,64]{1,0:T(8,128)S(1)}, f32[32,64]{1,0:T(8,128)S(1)}, u32[]{:S(2)}, u32[]{:S(2)}) collective-permute-start(f32[32,64]{1,0:T(8,128)S(1)} %add.36), channel_id=1, source_target_pairs={{0,16},{1,17},{2,18},{3,19},{4,20},{5,21},{6,22},{7,23},{8,24},{9,... | collective-permute-start | bytes 24584 | tf_op jit(solution)/shard_map/ppermute | solution.py:355
  94.9 0.1 fusion.4.unit_ref
  95.0 0.8 concatenate.33.expand_ref
  95.7 1.6 %collective-permute-done.9 = f32[32,64]{1,0:T(8,128)S(1)} collective-permute-done((f32[32,64]{1,0:T(8,128)S(1)}, f32[32,64]{1,0:T(8,128)S(1)}, u32[]{:S(2)}, u32[]{:S(2)}) %collective-permute-start.9) | collective-permute-done | bytes 8224 | tf_op jit(solution)/shard_map/ppermute | solution.py:355
  97.4 0.0 copy-start
  97.4 3.4 %copy-done = f32[16,128,1024]{2,1,0:T(8,128)S(1)} copy-done((f32[16,128,1024]{2,1,0:T(8,128)S(1)}, f32[16,128,1024]{2,1,0:T(8,128)}, u32[]{:S(2)}) %copy-start) | copy-done | bytes 8388632
  100.8 12.6 %merge.1 = f32[32,16,2048]{2,1,0:T(8,128)} custom-call(f32[32,64]{1,0:T(8,128)S(1)} %add.37.left_ref, f32[64,128]{1,0:T(8,128)S(1)} %maximum_maximum_fusion.spread_ref, f32[32,128]{1,0:T(8,128)S(1)} %fusion.4.unit_ref, f32[128,256]{1,0:T(8,128)S(1)} %concatenate.33.expand_ref, f32[16,128,1024]{2,1,0:T(8,128)S(1)} %copy-done), custom_call_target="tpu_custom_call" | custom-call | tf_op jit(solution)/shard_map/merge/pallas_call | solution.py:448
  113.4 0.0 collective-permute-done.10
  113.4 0.8 maximum_select_fusion
  (7 shorter events, 0.0 us)
Async XLA Ops:
  3.8 23.5 %collective-permute-start = (f32[7,16,2176]{2,1,0:T(8,128)}, f32[7,16,2176]{2,1,0:T(8,128)S(1)}, u32[]{:S(2)}, u32[]{:S(2)}) collective-permute-start(f32[7,16,2176]{2,1,0:T(8,128)} %get-tuple-element.7.refs_1_), channel_id=1, source_target_pairs={{0,2},{1,3},{2,4},{3,5},{4,6},{5,7},{6,8},{7,9},{8,10},{9,11},{10,... | collective-permute-start | bytes 2924552 | tf_op jit(solution)/shard_map/ppermute | solution.py:342
  4.3 23.1 %collective-permute-start.1 = (f32[7,16,2176]{2,1,0:T(8,128)}, f32[7,16,2176]{2,1,0:T(8,128)S(1)}, u32[]{:S(2)}, u32[]{:S(2)}) collective-permute-start(f32[7,16,2176]{2,1,0:T(8,128)} %get-tuple-element.7.refs_1_), channel_id=1, source_target_pairs={{0,30},{1,31},{2,0},{3,1},{4,2},{5,3},{6,4},{7,5},{8,6},{9,7},{10,... | collective-permute-start | bytes 2924552 | tf_op jit(solution)/shard_map/ppermute | solution.py:342
  9.2 16.5 %collective-permute-start.2 = (f32[2,16,2176]{2,1,0:T(8,128)}, f32[2,16,2176]{2,1,0:T(8,128)S(1)}, u32[]{:S(2)}, u32[]{:S(2)}) collective-permute-start(f32[2,16,2176]{2,1,0:T(8,128)} %get-tuple-element.8), channel_id=1, source_target_pairs={{0,3},{1,2},{2,5},{3,4},{4,7},{5,6},{6,9},{7,8},{8,11},{9,10},{10,... | collective-permute-start | bytes 835592 | tf_op jit(solution)/shard_map/ppermute | solution.py:342
  9.2 18.1 %collective-permute-start.3 = (f32[2,16,2176]{2,1,0:T(8,128)}, f32[2,16,2176]{2,1,0:T(8,128)S(1)}, u32[]{:S(2)}, u32[]{:S(2)}) collective-permute-start(f32[2,16,2176]{2,1,0:T(8,128)} %get-tuple-element.8), channel_id=1, source_target_pairs={{0,1},{1,0},{2,3},{3,2},{4,5},{5,4},{6,7},{7,6},{8,9},{9,8},{10,11... | collective-permute-start | bytes 835592 | tf_op jit(solution)/shard_map/ppermute | solution.py:342
  11.2 16.1 %collective-permute-start.4 = (f32[2,16,2176]{2,1,0:T(8,128)}, f32[2,16,2176]{2,1,0:T(8,128)S(1)}, u32[]{:S(2)}, u32[]{:S(2)}) collective-permute-start(f32[2,16,2176]{2,1,0:T(8,128)} %get-tuple-element.8), channel_id=1, source_target_pairs={{0,31},{1,30},{2,1},{3,0},{4,3},{5,2},{6,5},{7,4},{8,7},{9,6},{10,... | collective-permute-start | bytes 835592 | tf_op jit(solution)/shard_map/ppermute | solution.py:342
  25.8 1.6 %copy-start.3 = (f32[2,16,2176]{2,1,0:T(8,128)}, f32[2,16,2176]{2,1,0:T(8,128)S(1)}, u32[]{:S(2)}) copy-start(f32[2,16,2176]{2,1,0:T(8,128)S(1)} %collective-permute-done.2.refs_3_) | copy-start | bytes 835588
  27.3 0.7 copy-start.4
  27.3 0.8 copy-start.5
  27.3 1.2 %copy-start.1 = (f32[7,16,2176]{2,1,0:T(8,128)}, f32[7,16,2176]{2,1,0:T(8,128)S(1)}, u32[]{:S(2)}) copy-start(f32[7,16,2176]{2,1,0:T(8,128)S(1)} %collective-permute-done.refs_0_) | copy-start | bytes 2924548
  28.6 0.9 copy-start.2
  70.4 3.9 %collective-permute-start.5 = (f32[32,64]{1,0:T(8,128)}, f32[32,64]{1,0:T(8,128)S(1)}, u32[]{:S(2)}, u32[]{:S(2)}) collective-permute-start(f32[32,64]{1,0:T(8,128)} %get-tuple-element.9), channel_id=1, source_target_pairs={{0,1},{1,0},{2,3},{3,2},{4,5},{5,4},{6,7},{7,6},{8,9},{9,8},{10,11... | collective-permute-start | bytes 24584 | tf_op jit(solution)/shard_map/ppermute | solution.py:355
  75.1 10.1 %collective-permute-start.6 = (f32[32,64]{1,0:T(8,128)S(1)}, f32[32,64]{1,0:T(8,128)S(1)}, u32[]{:S(2)}, u32[]{:S(2)}) collective-permute-start(f32[32,64]{1,0:T(8,128)S(1)} %add.33), channel_id=1, source_target_pairs={{0,2},{1,3},{2,0},{3,1},{4,6},{5,7},{6,4},{7,5},{8,10},{9,11},{10,... | collective-permute-start | bytes 24584 | tf_op jit(solution)/shard_map/ppermute | solution.py:355
  85.3 3.7 %collective-permute-start.7 = (f32[32,64]{1,0:T(8,128)S(1)}, f32[32,64]{1,0:T(8,128)S(1)}, u32[]{:S(2)}, u32[]{:S(2)}) collective-permute-start(f32[32,64]{1,0:T(8,128)S(1)} %add.34), channel_id=1, source_target_pairs={{0,4},{1,5},{2,6},{3,7},{4,0},{5,1},{6,2},{7,3},{8,12},{9,13},{10,... | collective-permute-start | bytes 24584 | tf_op jit(solution)/shard_map/ppermute | solution.py:355
  87.9 25.4 %collective-permute-start.10 = (f32[2,16,2048]{2,1,0:T(8,128)S(1)}, f32[2,16,2048]{2,1,0:T(8,128)S(1)}, u32[]{:S(2)}, u32[]{:S(2)}) collective-permute-start(f32[2,16,2048]{2,1,0:T(8,128)S(1)} %get-tuple-element.13), channel_id=1, source_target_pairs={{0,1},{1,0},{2,3},{3,2},{4,5},{5,4},{6,7},{7,6},{8,9},{9,8},{10,11... | collective-permute-start | bytes 786440 | tf_op jit(solution)/shard_map/ppermute | solution.py:342
  89.0 3.7 %collective-permute-start.8 = (f32[32,64]{1,0:T(8,128)S(1)}, f32[32,64]{1,0:T(8,128)S(1)}, u32[]{:S(2)}, u32[]{:S(2)}) collective-permute-start(f32[32,64]{1,0:T(8,128)S(1)} %add.35), channel_id=1, source_target_pairs={{0,8},{1,9},{2,10},{3,11},{4,12},{5,13},{6,14},{7,15},{8,0},{9,1},... | collective-permute-start | bytes 24584 | tf_op jit(solution)/shard_map/ppermute | solution.py:355
  92.7 4.6 %collective-permute-start.9 = (f32[32,64]{1,0:T(8,128)S(1)}, f32[32,64]{1,0:T(8,128)S(1)}, u32[]{:S(2)}, u32[]{:S(2)}) collective-permute-start(f32[32,64]{1,0:T(8,128)S(1)} %add.36), channel_id=1, source_target_pairs={{0,16},{1,17},{2,18},{3,19},{4,20},{5,21},{6,22},{7,23},{8,24},{9,... | collective-permute-start | bytes 24584 | tf_op jit(solution)/shard_map/ppermute | solution.py:355
  97.4 3.4 %copy-start = (f32[16,128,1024]{2,1,0:T(8,128)S(1)}, f32[16,128,1024]{2,1,0:T(8,128)}, u32[]{:S(2)}) copy-start(f32[16,128,1024]{2,1,0:T(8,128)} %get-tuple-element.10.snap_ref) | copy-start | bytes 25165828

commit v2 on v1

--- a/solution.py
+++ b/solution.py
@@ -15,6 +15,7 @@
 TILE = 128
 GUARD = 8
 BATCH = 4
+OWN = 8
 VMEM = pl.BlockSpec(memory_space=pltpu.VMEM)
 SMEM = pl.BlockSpec(memory_space=pltpu.SMEM)
 
@@ -113,7 +114,7 @@
     else:
         snap_ref, end_ref = refs[:2]
         refs = refs[2:]
-    qa, qb, xa, xb, twice, cw, ce, cs, cn, c0 = refs
+    qa, qb, xa, xb, twice, cw, ce, cs, cn, c0, snap, sems = refs
     rows = sources[0][0].shape[1]
     block = sources[0][0].shape[2] - TILE
     length = block // halves
@@ -207,50 +208,65 @@
 
         lax.fori_loop(0, rows // 8, by_rows, 0)
 
-    def advance(source, target, now, later, row, step, keep):
-        for r in range(BATCH):
-            x = row + r
-            south = [
-                pltpu.roll(source[GUARD + x, :, t * TILE : (t + 1) * TILE], 1, 1) for t in range(tiles)
-            ]
-            north = [
-                pltpu.roll(source[GUARD + x, :, t * TILE : (t + 1) * TILE], TILE - 1, 1)
-                for t in range(tiles)
-            ]
-            lane = lanes_of((subs, TILE))
-            for t in range(tiles):
-                cols = slice(t * TILE, (t + 1) * TILE)
-                s = jnp.where(lane == 0, south[t - 1], south[t])
-                n = jnp.where(lane == TILE - 1, north[(t + 1) % tiles], north[t])
+    lane2s = lanes_of((subs, TILE))
+    first_lane, last_lane = lane2s == 0, lane2s == TILE - 1
+
+    def advance(source, target, now, later, row, count, step, keep):
+        def tile_of(r, t):
+            return source[GUARD + row + r, :, t * TILE : (t + 1) * TILE]
+
+        held, up, down = {}, {}, {}
+
+        def load(t):
+            for r in range(-1, count + 1):
+                held[r, t] = tile_of(r, t)
+            for r in range(count):
+                up[r, t] = pltpu.roll(held[r, t], 1, 1)
+                down[r, t] = pltpu.roll(held[r, t], TILE - 1, 1)
+
+        load(tiles - 1)
+        load(0)
+        for r in range(count):
+            up[r, -1], down[r, tiles] = up[r, tiles - 1], down[r, 0]
+        for t in range(tiles):
+            if t + 1 < tiles - 1:
+                load(t + 1)
+            cols = slice(t * TILE, (t + 1) * TILE)
+            for r in range(count):
+                x = row + r
+                south = jnp.where(first_lane, up[r, t - 1], up[r, t])
+                north = jnp.where(last_lane, down[r, t + 1], down[r, t])
                 drive = now[x, :, cols]
                 fresh = (
-                    c0[x, :, cols] * source[GUARD + x, :, cols]
-                    + cw[x, :, cols] * source[GUARD + x - 1, :, cols]
-                    + ce[x, :, cols] * source[GUARD + x + 1, :, cols]
-                    + cs[x, :, cols] * s
-                    + cn[x, :, cols] * n
-                    + drive
+                    (c0[x, :, cols] * held[r, t] + cw[x, :, cols] * held[r - 1, t])
+                    + (ce[x, :, cols] * held[r + 1, t] + cs[x, :, cols] * south)
+                    + (cn[x, :, cols] * north + drive)
                 )
                 target[GUARD + x, :, cols] = fresh
                 now[x, :, cols] = twice[x, :, cols] * later[x, :, cols] - drive
                 if keep and t < tiles - 1:
-                    snap_ref[x - rows, pl.ds(pl.multiple_of(step * subs, subs), subs), cols] = fresh
+                    snap[x - rows, pl.ds(pl.multiple_of(step * subs, subs), subs), cols] = fresh
 
     def one(source, target, now, later, step):
         low = (step + 1) // BATCH
         high = (total - 1 - step + BATCH - 1) // BATCH
 
         def halo_rows(i, carry):
-            advance(source, target, now, later, i * BATCH, step, False)
+            advance(source, target, now, later, i * BATCH, BATCH, step, False)
             return carry
 
         def own_rows(i, carry):
-            advance(source, target, now, later, i * BATCH, step, True)
+            advance(source, target, now, later, i * OWN, OWN, step, True)
             return carry
 
         lax.fori_loop(low, rows // BATCH, halo_rows, 0)
-        lax.fori_loop(rows // BATCH, 2 * rows // BATCH, own_rows, 0)
+        lax.fori_loop(rows // OWN, 2 * rows // OWN, own_rows, 0)
+        copy_out(step).start()
         lax.fori_loop(2 * rows // BATCH, high, halo_rows, 0)
+
+    def copy_out(step):
+        part = pl.ds(pl.multiple_of(step * subs, subs), subs)
+        return pltpu.make_async_copy(snap.at[:, part, :], snap_ref.at[:, part, :], sems.at[step])
 
     def pair(i, carry):
         one(qa, qb, xa, xb, 2 * i)
@@ -273,11 +289,17 @@
     if with_left:
         width = STEPS * subs
 
-        def add(x, gram):
-            a = snap_ref[x]
-            return gram + mm_nt(a, a)
-
-        gram = lax.fori_loop(0, rows, add, jnp.zeros((width, width), jnp.float32))
+        def add(x, total):
+            a = snap[x]
+            high = a.astype(jnp.bfloat16)
+            low = (a - high.astype(jnp.float32)).astype(jnp.bfloat16)
+            both = jnp.concatenate([high, low], axis=0)
+            return total + lax.dot_general(
+                both, both, (((1,), (1,)), ((), ())), preferred_element_type=jnp.float32
+            )
+
+        gram = lax.fori_loop(0, rows, add, jnp.zeros((2 * width, 2 * width), jnp.float32))
+        gram = (gram[:width, :width] + gram[width:, width:]) + (gram[:width, width:] + gram[width:, :width])
         lane = lanes_of((1, width))
         left = jnp.zeros((select_ref.shape[0], width), jnp.float32)
         for half in range(halves):
@@ -285,22 +307,58 @@
             left = left + jnp.where((lane % subs) // (2 * groups) == half, part, 0.0)
         left_ref[...] = mm(left, fold_ref[...])
 
+    def drained(step, carry):
+        copy_out(step).wait()
+        return carry
+
+    lax.fori_loop(0, STEPS, drained, 0)
+
 
 def eliminate(m, rank):
     row = lax.broadcasted_iota(jnp.int32, m.shape, 0)
     lane = lanes_of(m.shape)
-    for k in range(rank):
-        line = m[k : k + 1, :]
-        pivot = m[k : k + 1, k : k + 1]
-        column = m[:, k : k + 1] * (1.0 / pivot)
-        m = m - jnp.where(row > k, column, 0.0) * line
+    for k in range(0, rank, 2):
+        line, after = m[k : k + 1, :], m[k + 1 : k + 2, :]
+        column, beside = m[:, k : k + 1], m[:, k + 1 : k + 2]
+        a, b, d = m[k : k + 1, k : k + 1], m[k + 1 : k + 2, k : k + 1], m[k + 1 : k + 2, k + 1 : k + 2]
+        inverse = 1.0 / a
+        ratio = b * inverse
+        pivot = 1.0 / (d - ratio * b)
+        after = after - ratio * line
+        beside = (beside - ratio * column) * pivot
+        m = (
+            m
+            - jnp.where(row > k, column * inverse, 0.0) * line
+            - jnp.where(row > k + 1, beside, 0.0) * after
+        )
     diagonal = jnp.sum(jnp.where(row == lane, m, 0.0), axis=1, keepdims=True)
     return m * lax.rsqrt(diagonal)
 
 
-def merge_kernel(halves, subs, left_ref, spread_ref, unit_ref, expand_ref, snap_ref, out_ref):
+def in_two(x):
+    high = x.astype(jnp.bfloat16)
+    return high, (x - high.astype(jnp.float32)).astype(jnp.bfloat16)
+
+
+CHUNK = 256
+
+
+def merge_kernel(halves, left_ref, spread_ref, unit_ref, expand_ref, snap_ref, out_ref, snap, out, arrived, left_sems):
     rank = left_ref.shape[0]
     wide = left_ref.shape[1]
+    rows, width, length = snap.shape
+    parts = length // CHUNK
+
+    def fetch(i):
+        at = pl.ds(i * CHUNK, CHUNK)
+        return pltpu.make_async_copy(snap_ref.at[:, :, at], snap.at[:, :, at], arrived.at[i])
+
+    def store(i, half):
+        at = pl.ds(half * length + i * CHUNK, CHUNK)
+        return pltpu.make_async_copy(out.at[:, :, at], out_ref.at[:, :, at], left_sems.at[i, half])
+
+    for i in range(parts):
+        fetch(i).start()
     lane = lanes_of((rank, 128))
     whole = eliminate(mm(left_ref[...], spread_ref[...]) + unit_ref[...], rank)
     proj = jnp.where((lane >= rank) & (lane < rank + wide), whole, 0.0)
@@ -310,26 +368,33 @@
         lax.broadcasted_iota(jnp.int32, (rank, rank), 0) <= lanes_of((rank, rank)), factor, 0.0
     )
     mix = mm(upper, whole)
-    width = snap_ref.shape[1]
     weights = jnp.concatenate(
         [mm(mix, expand_ref[:, half * width : (half + 1) * width]) for half in range(halves)], axis=0
     )
-    rows = snap_ref.shape[0]
-    length = snap_ref.shape[2]
-    chunk = 256
-
-    def columns(i, carry):
-        at = pl.multiple_of(i * chunk, chunk)
+    count = halves * rank
+    high, low = in_two(weights)
+    weights = jnp.concatenate(
+        [jnp.concatenate([high, high], axis=1), jnp.concatenate([low, low], axis=1)], axis=0
+    )
+    for i in range(parts):
+        fetch(i).wait()
         for base in range(0, rows, 8):
-            parts = [mm(weights, snap_ref[base + x, :, pl.ds(at, chunk)]) for x in range(8)]
+            made = []
+            for x in range(base, base + 8):
+                values = jnp.concatenate(in_two(snap[x, :, i * CHUNK : (i + 1) * CHUNK]), axis=0)
+                both = jnp.dot(weights, values, preferred_element_type=jnp.float32)
+                made.append(both[:count] + both[count:])
             for half in range(halves):
+                at = half * length + i * CHUNK
                 for r in range(0, rank, 8):
                     first = half * rank + r
-                    block = jnp.swapaxes(jnp.stack([p[first : first + 8] for p in parts], axis=0), 0, 1)
-                    out_ref[r : r + 8, base : base + 8, pl.ds(pl.multiple_of(half * length + at, chunk), chunk)] = block
-        return carry
-
-    lax.fori_loop(0, length // chunk, columns, 0)
+                    block = jnp.stack([p[first : first + 8] for p in made], axis=0)
+                    out[r : r + 8, base : base + 8, at : at + CHUNK] = jnp.swapaxes(block, 0, 1)
+        for half in range(halves):
+            store(i, half).start()
+    for i in range(parts):
+        for half in range(halves):
+            store(i, half).wait()
 
 
 def shifted(value, along_space, along_tm):
@@ -436,21 +501,28 @@
         functools.partial(stencil_kernel, groups, halves, fast),
         out_shape=outs,
         in_specs=[VMEM] * (len(sources) + len(extra)),
-        out_specs=[VMEM] * len(outs),
+        out_specs=[pl.BlockSpec(memory_space=pl.ANY)] + [VMEM] * (len(outs) - 1),
         scratch_shapes=[pltpu.VMEM((3 * rows + 2 * GUARD, subs, span), f32)] * 2
-        + [pltpu.VMEM(grid_of, f32)] * 8,
-        compiler_params=pltpu.CompilerParams(vmem_limit_bytes=56 * 2**20),
+        + [pltpu.VMEM(grid_of, f32)] * 8
+        + [pltpu.VMEM((rows, width, length), f32), pltpu.SemaphoreType.DMA((STEPS,))],
+        compiler_params=pltpu.CompilerParams(vmem_limit_bytes=36 * 2**20),
         name="stencil",
     )(*sources, *extra)
 
     if fast:
         left = total_of(made[2])
         piece = pl.pallas_call(
-            functools.partial(merge_kernel, halves, subs),
+            functools.partial(merge_kernel, halves),
             out_shape=jax.ShapeDtypeStruct((rank, rows, block), f32),
-            in_specs=[VMEM] * 5,
-            out_specs=VMEM,
-            compiler_params=pltpu.CompilerParams(vmem_limit_bytes=40 * 2**20),
+            in_specs=[VMEM] * 4 + [pl.BlockSpec(memory_space=pl.ANY)],
+            out_specs=pl.BlockSpec(memory_space=pl.ANY),
+            scratch_shapes=[
+                pltpu.VMEM((rows, width, length), f32),
+                pltpu.VMEM((rank, rows, block), f32),
+                pltpu.SemaphoreType.DMA((length // CHUNK,)),
+                pltpu.SemaphoreType.DMA((length // CHUNK, halves)),
+            ],
+            compiler_params=pltpu.CompilerParams(vmem_limit_bytes=24 * 2**20),
             name="merge",
         )(left, spread, unit, expand, made[0])
     else:

time: 115 us -> 106 us (0.922)
  Pallas kernels: 56.1 us -> 46 us
  waiting for transfers between devices: 15.1 us -> 18.5 us
  other arithmetic: 3.24 us -> 1.91 us
    pallas_call x1, Pallas kernels: 40.9 us -> 31.8 us  [body(): pl.pallas_call(functools.partial(stencil_kernel, groups, halves, fast), o...]
    unnamed x13 -> x7, local copies, waits for them, and re-layouts: 6.32 us -> 8.59 us
    ppermute x5, waiting for transfers between devices: 8.06 us -> 10.2 us  [total_of(): lax.ppermute(value, AXES, [(i, i ^ bit) for i in range(size)])]
    ppermute x6, waiting for transfers between devices: 7.07 us -> 8.27 us  [shifted(): return lax.ppermute(value, AXES, moves)]
  transfers between devices with their start and end apart: 11 -> 11, of which waited for: 7 -> 7; matrix products, arithmetic and copies ran while one was open for 6% -> 4% of each run, Pallas kernels for 11% -> 11%
where the time goes in v2:
time: 106 us
  Pallas kernels  46 us (43%)
  starting transfers between devices  27.3 us (26%)
  waiting for transfers between devices  18.5 us (17%)
  local copies, waits for them, and re-layouts  9.59 us (9%)
  other arithmetic  1.91 us (2%)
  between operations  1.36 us (1%)
    pallas_call x1, Pallas kernels, body(): pl.pallas_call(functools.partial(stencil_kernel, groups, halves, fast), o...  31.8 us
    ppermute x5, starting transfers between devices, total_of(): lax.ppermute(value, AXES, [(i, i ^ bit) for i in range(size)])  14.3 us
    ppermute x6, starting transfers between devices, shifted(): return lax.ppermute(value, AXES, moves)  13 us
    pallas_call x1, Pallas kernels, body(): pl.pallas_call(functools.partial(merge_kernel, halves), out_shape=jax.Sha...  11.7 us
    ppermute x5, waiting for transfers between devices, total_of(): lax.ppermute(value, AXES, [(i, i ^ bit) for i in range(size)])  10.2 us
    unnamed x7, local copies, waits for them, and re-layouts  8.59 us
    ppermute x6, waiting for transfers between devices, shifted(): return lax.ppermute(value, AXES, moves)  8.27 us
    pallas_call x1, Pallas kernels, body(): pl.pallas_call(functools.partial(pack_kernel, groups, block), out_shape=[...  2.54 us
  transfers between devices with their start and end apart: 11, of which 7 were waited for; matrix products, arithmetic and copies ran while one was open for 4% of the time, Pallas kernels for 11%

profile of v2, /device:TPU:0, one launch (start us, length us, event | category | flops | bytes accessed | tf_op | source)
XLA Modules:
  0.0 105.6 jit_solution(336597301878229968)
XLA Ops:
  1.3 2.5 %pack.1 = (f32[7,16,2176]{2,1,0:T(8,128)}, f32[2,16,2176]{2,1,0:T(8,128)}) custom-call(s32[1]{0:T(128)S(6)} %copy.12.step_ref, f32[1,2,16,4096]{3,2,1,0:T(8,128)} %state_ref.1, f32[16,4096]{1,0:T(8,128)} %vx.1, f32[16,4096]{1,0:T(8,128)} %vy.1, f32[16,4096]{1,0:T(8,128)} %amp.1, f32[16,4096]{1,0:T(8,128)} %freq.1, f32[16,4096]{1,0:T(8,128)} %phase.1), custom_call_target="tpu_custom_call" | custom-call | tf_op jit(solution)/shard_map/pack/pallas_call | solution.py:460
  3.8 0.5 collective-permute-start
  4.3 5.0 %collective-permute-start.1 = (f32[7,16,2176]{2,1,0:T(8,128)}, f32[7,16,2176]{2,1,0:T(8,128)S(1)}, u32[]{:S(2)}, u32[]{:S(2)}) collective-permute-start(f32[7,16,2176]{2,1,0:T(8,128)} %get-tuple-element.7.refs_1_), channel_id=1, source_target_pairs={{0,30},{1,31},{2,0},{3,1},{4,2},{5,3},{6,4},{7,5},{8,6},{9,7},{10,... | collective-permute-start | bytes 2924552 | tf_op jit(solution)/shard_map/ppermute | solution.py:407
  9.2 0.0 collective-permute-start.2
  9.2 2.0 %collective-permute-start.3 = (f32[2,16,2176]{2,1,0:T(8,128)}, f32[2,16,2176]{2,1,0:T(8,128)S(1)}, u32[]{:S(2)}, u32[]{:S(2)}) collective-permute-start(f32[2,16,2176]{2,1,0:T(8,128)} %get-tuple-element.8), channel_id=1, source_target_pairs={{0,1},{1,0},{2,3},{3,2},{4,5},{5,4},{6,7},{7,6},{8,9},{9,8},{10,11... | collective-permute-start | bytes 835592 | tf_op jit(solution)/shard_map/ppermute | solution.py:407
  11.2 5.1 %collective-permute-start.4 = (f32[2,16,2176]{2,1,0:T(8,128)}, f32[2,16,2176]{2,1,0:T(8,128)S(1)}, u32[]{:S(2)}, u32[]{:S(2)}) collective-permute-start(f32[2,16,2176]{2,1,0:T(8,128)} %get-tuple-element.8), channel_id=1, source_target_pairs={{0,31},{1,30},{2,1},{3,0},{4,3},{5,2},{6,5},{7,4},{8,7},{9,6},{10,... | collective-permute-start | bytes 835592 | tf_op jit(solution)/shard_map/ppermute | solution.py:407
  16.3 0.9 dynamic-slice_bitcast_fusion.1
  17.2 0.9 add_bitcast_fusion.refs_7_
  18.1 1.0 convolution_bitcast_fusion.refs_6_
  19.0 6.7 %collective-permute-done.2.refs_3_ = f32[2,16,2176]{2,1,0:T(8,128)S(1)} collective-permute-done((f32[2,16,2176]{2,1,0:T(8,128)}, f32[2,16,2176]{2,1,0:T(8,128)S(1)}, u32[]{:S(2)}, u32[]{:S(2)}) %collective-permute-start.2) | collective-permute-done | bytes 278560 | tf_op jit(solution)/shard_map/ppermute | solution.py:407
  25.8 1.5 %collective-permute-done.3.refs_4_ = f32[2,16,2176]{2,1,0:T(8,128)S(1)} collective-permute-done((f32[2,16,2176]{2,1,0:T(8,128)}, f32[2,16,2176]{2,1,0:T(8,128)S(1)}, u32[]{:S(2)}, u32[]{:S(2)}) %collective-permute-start.3) | collective-permute-done | bytes 278560 | tf_op jit(solution)/shard_map/ppermute | solution.py:407
  27.3 0.0 collective-permute-done.4.refs_5_
  27.3 0.0 collective-permute-done.refs_0_
  27.3 0.0 collective-permute-done.1.refs_2_
  27.3 0.0 copy-start.2
  27.3 1.2 %copy-done.2 = f32[7,16,2176]{2,1,0:T(8,128)S(1)} copy-done((f32[7,16,2176]{2,1,0:T(8,128)S(1)}, f32[7,16,2176]{2,1,0:T(8,128)}, u32[]{:S(2)}) %copy-start.2) | copy-done | bytes 974872
  28.5 31.8 %stencil.1 = (f32[16,128,1024]{2,1,0:T(8,128)S(1)}, f32[2,2,16,2048]{3,2,1,0:T(8,128)S(1)}, f32[32,64]{1,0:T(8,128)S(1)}) custom-call(f32[7,16,2176]{2,1,0:T(8,128)S(1)} %collective-permute-done.refs_0_, f32[7,16,2176]{2,1,0:T(8,128)S(1)} %copy-done.2, f32[7,16,2176]{2,1,0:T(8,128)S(1)} %collective-permute-done.1.refs_2_, ...), custom_call_target="tpu_custom_call" | custom-call | tf_op jit(solution)/shard_map/stencil/pallas_call | solution.py:500
  60.3 0.0 copy-start
  60.3 3.2 %copy-done = f32[16,128,1024]{2,1,0:T(8,128)} copy-done((f32[16,128,1024]{2,1,0:T(8,128)}, f32[16,128,1024]{2,1,0:T(8,128)S(1)}, u32[]{:S(2)}) %copy-start) | copy-done | bytes 8388632
  63.5 0.5 collective-permute-start.5
  64.1 0.8 copy.11
  64.9 0.1 pad.7.clone
  64.9 2.4 %collective-permute-done.5 = f32[32,64]{1,0:T(8,128)S(1)} collective-permute-done((f32[32,64]{1,0:T(8,128)S(1)}, f32[32,64]{1,0:T(8,128)S(1)}, u32[]{:S(2)}, u32[]{:S(2)}) %collective-permute-start.5) | collective-permute-done | bytes 8224 | tf_op jit(solution)/shard_map/ppermute | solution.py:420
  67.3 9.4 %collective-permute-start.6 = (f32[32,64]{1,0:T(8,128)S(1)}, f32[32,64]{1,0:T(8,128)S(1)}, u32[]{:S(2)}, u32[]{:S(2)}) collective-permute-start(f32[32,64]{1,0:T(8,128)S(1)} %add.33), channel_id=1, source_target_pairs={{0,2},{1,3},{2,0},{3,1},{4,6},{5,7},{6,4},{7,5},{8,10},{9,11},{10,... | collective-permute-start | bytes 24584 | tf_op jit(solution)/shard_map/ppermute | solution.py:420
  76.7 0.1 maximum_maximum_fusion.spread_ref
  76.8 0.8 collective-permute-done.6
  77.6 1.4 %collective-permute-start.7 = (f32[32,64]{1,0:T(8,128)S(1)}, f32[32,64]{1,0:T(8,128)S(1)}, u32[]{:S(2)}, u32[]{:S(2)}) collective-permute-start(f32[32,64]{1,0:T(8,128)S(1)} %add.34), channel_id=1, source_target_pairs={{0,4},{1,5},{2,6},{3,7},{4,0},{5,1},{6,2},{7,3},{8,12},{9,13},{10,... | collective-permute-start | bytes 24584 | tf_op jit(solution)/shard_map/ppermute | solution.py:420
  79.0 0.6 collective-permute-start.10
  79.6 1.7 %collective-permute-done.7 = f32[32,64]{1,0:T(8,128)S(1)} collective-permute-done((f32[32,64]{1,0:T(8,128)S(1)}, f32[32,64]{1,0:T(8,128)S(1)}, u32[]{:S(2)}, u32[]{:S(2)}) %collective-permute-start.7) | collective-permute-done | bytes 8224 | tf_op jit(solution)/shard_map/ppermute | solution.py:420
  81.3 0.9 collective-permute-start.8
  82.3 2.8 %collective-permute-done.8 = f32[32,64]{1,0:T(8,128)S(1)} collective-permute-done((f32[32,64]{1,0:T(8,128)S(1)}, f32[32,64]{1,0:T(8,128)S(1)}, u32[]{:S(2)}, u32[]{:S(2)}) %collective-permute-start.8) | collective-permute-done | bytes 8224 | tf_op jit(solution)/shard_map/ppermute | solution.py:420
  85.1 2.0 %collective-permute-start.9 = (f32[32,64]{1,0:T(8,128)S(1)}, f32[32,64]{1,0:T(8,128)S(1)}, u32[]{:S(2)}, u32[]{:S(2)}) collective-permute-start(f32[32,64]{1,0:T(8,128)S(1)} %add.36), channel_id=1, source_target_pairs={{0,16},{1,17},{2,18},{3,19},{4,20},{5,21},{6,22},{7,23},{8,24},{9,... | collective-permute-start | bytes 24584 | tf_op jit(solution)/shard_map/ppermute | solution.py:420
  87.0 0.1 fusion.4.unit_ref
  87.1 2.6 %collective-permute-done.9 = f32[32,64]{1,0:T(8,128)S(1)} collective-permute-done((f32[32,64]{1,0:T(8,128)S(1)}, f32[32,64]{1,0:T(8,128)S(1)}, u32[]{:S(2)}, u32[]{:S(2)}) %collective-permute-start.9) | collective-permute-done | bytes 8224 | tf_op jit(solution)/shard_map/ppermute | solution.py:420
  89.7 0.0 copy-start.1
  89.7 3.4 %copy-done.1 = f32[16,128,1024]{2,1,0:T(8,128)S(1)} copy-done((f32[16,128,1024]{2,1,0:T(8,128)S(1)}, f32[16,128,1024]{2,1,0:T(8,128)}, u32[]{:S(2)}) %copy-start.1) | copy-done | bytes 8388632
  93.1 11.7 %merge.1 = f32[32,16,2048]{2,1,0:T(8,128)} custom-call(f32[32,64]{1,0:T(8,128)S(1)} %add.37.left_ref, f32[64,128]{1,0:T(8,128)S(1)} %maximum_maximum_fusion.spread_ref, f32[32,128]{1,0:T(8,128)S(1)} %fusion.4.unit_ref, f32[128,256]{1,0:T(8,128)S(1)} %concatenate.33.expand_ref, f32[16,128,1024]{2,1,0:T(8,128)S(1)} %copy-done.1), custom_call_target="tpu_custom_call" | custom-call | tf_op jit(solution)/shard_map/merge/pallas_call | solution.py:514
  104.7 0.0 collective-permute-done.10
  104.8 0.8 maximum_select_fusion
  (10 shorter events, 0.1 us)
Async XLA Ops:
  3.8 23.5 %collective-permute-start = (f32[7,16,2176]{2,1,0:T(8,128)}, f32[7,16,2176]{2,1,0:T(8,128)S(1)}, u32[]{:S(2)}, u32[]{:S(2)}) collective-permute-start(f32[7,16,2176]{2,1,0:T(8,128)} %get-tuple-element.7.refs_1_), channel_id=1, source_target_pairs={{0,2},{1,3},{2,4},{3,5},{4,6},{5,7},{6,8},{7,9},{8,10},{9,11},{10,... | collective-permute-start | bytes 2924552 | tf_op jit(solution)/shard_map/ppermute | solution.py:407
  4.3 23.0 %collective-permute-start.1 = (f32[7,16,2176]{2,1,0:T(8,128)}, f32[7,16,2176]{2,1,0:T(8,128)S(1)}, u32[]{:S(2)}, u32[]{:S(2)}) collective-permute-start(f32[7,16,2176]{2,1,0:T(8,128)} %get-tuple-element.7.refs_1_), channel_id=1, source_target_pairs={{0,30},{1,31},{2,0},{3,1},{4,2},{5,3},{6,4},{7,5},{8,6},{9,7},{10,... | collective-permute-start | bytes 2924552 | tf_op jit(solution)/shard_map/ppermute | solution.py:407
  9.2 16.5 %collective-permute-start.2 = (f32[2,16,2176]{2,1,0:T(8,128)}, f32[2,16,2176]{2,1,0:T(8,128)S(1)}, u32[]{:S(2)}, u32[]{:S(2)}) collective-permute-start(f32[2,16,2176]{2,1,0:T(8,128)} %get-tuple-element.8), channel_id=1, source_target_pairs={{0,3},{1,2},{2,5},{3,4},{4,7},{5,6},{6,9},{7,8},{8,11},{9,10},{10,... | collective-permute-start | bytes 835592 | tf_op jit(solution)/shard_map/ppermute | solution.py:407
  9.2 18.1 %collective-permute-start.3 = (f32[2,16,2176]{2,1,0:T(8,128)}, f32[2,16,2176]{2,1,0:T(8,128)S(1)}, u32[]{:S(2)}, u32[]{:S(2)}) collective-permute-start(f32[2,16,2176]{2,1,0:T(8,128)} %get-tuple-element.8), channel_id=1, source_target_pairs={{0,1},{1,0},{2,3},{3,2},{4,5},{5,4},{6,7},{7,6},{8,9},{9,8},{10,11... | collective-permute-start | bytes 835592 | tf_op jit(solution)/shard_map/ppermute | solution.py:407
  11.2 16.1 %collective-permute-start.4 = (f32[2,16,2176]{2,1,0:T(8,128)}, f32[2,16,2176]{2,1,0:T(8,128)S(1)}, u32[]{:S(2)}, u32[]{:S(2)}) collective-permute-start(f32[2,16,2176]{2,1,0:T(8,128)} %get-tuple-element.8), channel_id=1, source_target_pairs={{0,31},{1,30},{2,1},{3,0},{4,3},{5,2},{6,5},{7,4},{8,7},{9,6},{10,... | collective-permute-start | bytes 835592 | tf_op jit(solution)/shard_map/ppermute | solution.py:407
  27.3 1.2 %copy-start.2 = (f32[7,16,2176]{2,1,0:T(8,128)S(1)}, f32[7,16,2176]{2,1,0:T(8,128)}, u32[]{:S(2)}) copy-start(f32[7,16,2176]{2,1,0:T(8,128)} %get-tuple-element.7.refs_1_) | copy-start | bytes 2924548
  60.3 3.2 %copy-start = (f32[16,128,1024]{2,1,0:T(8,128)}, f32[16,128,1024]{2,1,0:T(8,128)S(1)}, u32[]{:S(2)}) copy-start(f32[16,128,1024]{2,1,0:T(8,128)S(1)} %get-tuple-element.10.snap_ref) | copy-start | bytes 25165828
  63.5 3.7 %collective-permute-start.5 = (f32[32,64]{1,0:T(8,128)S(1)}, f32[32,64]{1,0:T(8,128)S(1)}, u32[]{:S(2)}, u32[]{:S(2)}) collective-permute-start(f32[32,64]{1,0:T(8,128)S(1)} %get-tuple-element.9), channel_id=1, source_target_pairs={{0,1},{1,0},{2,3},{3,2},{4,5},{5,4},{6,7},{7,6},{8,9},{9,8},{10,11... | collective-permute-start | bytes 24584 | tf_op jit(solution)/shard_map/ppermute | solution.py:420
  67.3 10.3 %collective-permute-start.6 = (f32[32,64]{1,0:T(8,128)S(1)}, f32[32,64]{1,0:T(8,128)S(1)}, u32[]{:S(2)}, u32[]{:S(2)}) collective-permute-start(f32[32,64]{1,0:T(8,128)S(1)} %add.33), channel_id=1, source_target_pairs={{0,2},{1,3},{2,0},{3,1},{4,6},{5,7},{6,4},{7,5},{8,10},{9,11},{10,... | collective-permute-start | bytes 24584 | tf_op jit(solution)/shard_map/ppermute | solution.py:420
  77.6 3.7 %collective-permute-start.7 = (f32[32,64]{1,0:T(8,128)S(1)}, f32[32,64]{1,0:T(8,128)S(1)}, u32[]{:S(2)}, u32[]{:S(2)}) collective-permute-start(f32[32,64]{1,0:T(8,128)S(1)} %add.34), channel_id=1, source_target_pairs={{0,4},{1,5},{2,6},{3,7},{4,0},{5,1},{6,2},{7,3},{8,12},{9,13},{10,... | collective-permute-start | bytes 24584 | tf_op jit(solution)/shard_map/ppermute | solution.py:420
  79.0 25.7 %collective-permute-start.10 = (f32[2,16,2048]{2,1,0:T(8,128)S(1)}, f32[2,16,2048]{2,1,0:T(8,128)S(1)}, u32[]{:S(2)}, u32[]{:S(2)}) collective-permute-start(f32[2,16,2048]{2,1,0:T(8,128)S(1)} %get-tuple-element.13), channel_id=1, source_target_pairs={{0,1},{1,0},{2,3},{3,2},{4,5},{5,4},{6,7},{7,6},{8,9},{9,8},{10,11... | collective-permute-start | bytes 786440 | tf_op jit(solution)/shard_map/ppermute | solution.py:407
  81.3 3.7 %collective-permute-start.8 = (f32[32,64]{1,0:T(8,128)S(1)}, f32[32,64]{1,0:T(8,128)S(1)}, u32[]{:S(2)}, u32[]{:S(2)}) collective-permute-start(f32[32,64]{1,0:T(8,128)S(1)} %add.35), channel_id=1, source_target_pairs={{0,8},{1,9},{2,10},{3,11},{4,12},{5,13},{6,14},{7,15},{8,0},{9,1},... | collective-permute-start | bytes 24584 | tf_op jit(solution)/shard_map/ppermute | solution.py:420
  85.1 4.6 %collective-permute-start.9 = (f32[32,64]{1,0:T(8,128)S(1)}, f32[32,64]{1,0:T(8,128)S(1)}, u32[]{:S(2)}, u32[]{:S(2)}) collective-permute-start(f32[32,64]{1,0:T(8,128)S(1)} %add.36), channel_id=1, source_target_pairs={{0,16},{1,17},{2,18},{3,19},{4,20},{5,21},{6,22},{7,23},{8,24},{9,... | collective-permute-start | bytes 24584 | tf_op jit(solution)/shard_map/ppermute | solution.py:420
  89.7 3.4 %copy-start.1 = (f32[16,128,1024]{2,1,0:T(8,128)S(1)}, f32[16,128,1024]{2,1,0:T(8,128)}, u32[]{:S(2)}) copy-start(f32[16,128,1024]{2,1,0:T(8,128)} %copy-done) | copy-start | bytes 25165828

commit v3 on v2

--- a/solution.py
+++ b/solution.py
@@ -17,6 +17,7 @@
 BATCH = 4
 OWN = 8
 VMEM = pl.BlockSpec(memory_space=pltpu.VMEM)
+HBM = pl.BlockSpec(memory_space=pltpu.HBM)
 SMEM = pl.BlockSpec(memory_space=pltpu.SMEM)
 
 
@@ -319,8 +320,9 @@
     lane = lanes_of(m.shape)
     for k in range(0, rank, 2):
         line, after = m[k : k + 1, :], m[k + 1 : k + 2, :]
-        column, beside = m[:, k : k + 1], m[:, k + 1 : k + 2]
-        a, b, d = m[k : k + 1, k : k + 1], m[k + 1 : k + 2, k : k + 1], m[k + 1 : k + 2, k + 1 : k + 2]
+        column = jnp.broadcast_to(m[:, k : k + 1], m.shape)
+        beside = jnp.broadcast_to(m[:, k + 1 : k + 2], m.shape)
+        a, b, d = column[k : k + 1], column[k + 1 : k + 2], beside[k + 1 : k + 2]
         inverse = 1.0 / a
         ratio = b * inverse
         pivot = 1.0 / (d - ratio * b)
@@ -491,7 +493,7 @@
         extra = [select, fold]
 
     outs = [
-        jax.ShapeDtypeStruct((rows, width, length), f32),
+        pltpu.HBM((rows, width, length), f32),
         jax.ShapeDtypeStruct((groups, 2, rows, block), f32),
     ]
     if fast:
@@ -501,7 +503,7 @@
         functools.partial(stencil_kernel, groups, halves, fast),
         out_shape=outs,
         in_specs=[VMEM] * (len(sources) + len(extra)),
-        out_specs=[pl.BlockSpec(memory_space=pl.ANY)] + [VMEM] * (len(outs) - 1),
+        out_specs=[HBM] + [VMEM] * (len(outs) - 1),
         scratch_shapes=[pltpu.VMEM((3 * rows + 2 * GUARD, subs, span), f32)] * 2
         + [pltpu.VMEM(grid_of, f32)] * 8
         + [pltpu.VMEM((rows, width, length), f32), pltpu.SemaphoreType.DMA((STEPS,))],
@@ -514,15 +516,15 @@
         piece = pl.pallas_call(
             functools.partial(merge_kernel, halves),
             out_shape=jax.ShapeDtypeStruct((rank, rows, block), f32),
-            in_specs=[VMEM] * 4 + [pl.BlockSpec(memory_space=pl.ANY)],
-            out_specs=pl.BlockSpec(memory_space=pl.ANY),
+            in_specs=[VMEM] * 4 + [HBM],
+            out_specs=HBM,
             scratch_shapes=[
                 pltpu.VMEM((rows, width, length), f32),
                 pltpu.VMEM((rank, rows, block), f32),
                 pltpu.SemaphoreType.DMA((length // CHUNK,)),
                 pltpu.SemaphoreType.DMA((length // CHUNK, halves)),
             ],
-            compiler_params=pltpu.CompilerParams(vmem_limit_bytes=24 * 2**20),
+            compiler_params=pltpu.CompilerParams(vmem_limit_bytes=54 * 2**20),
             name="merge",
         )(left, spread, unit, expand, made[0])
     else:

time: 106 us -> 96.3 us (0.908)
  local copies, waits for them, and re-layouts: 9.59 us -> 3.65 us
  Pallas kernels: 46 us -> 42.2 us
  waiting for transfers between devices: 18.5 us -> 16.6 us
  other arithmetic: 1.91 us -> 3.7 us
    unnamed x7 -> x3, local copies, waits for them, and re-layouts: 8.59 us -> 1.99 us
    pallas_call x1, Pallas kernels: 11.7 us -> 8.5 us  [body(): pl.pallas_call(functools.partial(merge_kernel, halves), out_shape=jax.Sha...]
    ppermute x5, waiting for transfers between devices: 10.2 us -> 8.38 us  [total_of(): lax.ppermute(value, AXES, [(i, i ^ bit) for i in range(size)])]
  transfers between devices with their start and end apart: 11 -> 11, of which waited for: 7 -> 7; matrix products, arithmetic and copies ran while one was open for 4% -> 7% of each run, Pallas kernels for 11% -> 9%
where the time goes in v3:
time: 96.3 us; the launch traced here: 95.8 us
  Pallas kernels  42.2 us (44%)
  starting transfers between devices  27.4 us (28%)
  waiting for transfers between devices  16.6 us (17%)
  other arithmetic  3.7 us (4%)
  local copies, waits for them, and re-layouts  3.65 us (4%)
  between operations  1.35 us (1%)
    pallas_call x1, Pallas kernels, body(): pl.pallas_call(functools.partial(stencil_kernel, groups, halves, fast), o...  31.1 us
    ppermute x5, starting transfers between devices, total_of(): lax.ppermute(value, AXES, [(i, i ^ bit) for i in range(size)])  14.3 us
    ppermute x6, starting transfers between devices, shifted(): return lax.ppermute(value, AXES, moves)  13 us
    pallas_call x1, Pallas kernels, body(): pl.pallas_call(functools.partial(merge_kernel, halves), out_shape=jax.Sha...  8.5 us
    ppermute x5, waiting for transfers between devices, total_of(): lax.ppermute(value, AXES, [(i, i ^ bit) for i in range(size)])  8.38 us
    ppermute x6, waiting for transfers between devices, shifted(): return lax.ppermute(value, AXES, moves)  8.27 us
    pallas_call x1, Pallas kernels, body(): pl.pallas_call(functools.partial(pack_kernel, groups, block), out_shape=[...  2.54 us
    unnamed x3, local copies, waits for them, and re-layouts  1.99 us
  transfers between devices with their start and end apart: 11, of which 7 were waited for; matrix products, arithmetic and copies ran while one was open for 7% of the time, Pallas kernels for 9%

profile of v3, /device:TPU:0, one launch (start us, length us, event | category | flops | bytes accessed | tf_op | source)
XLA Modules:
  0.0 95.8 jit_solution(10409653130850307017)
XLA Ops:
  1.3 2.5 %pack.1 = (f32[7,16,2176]{2,1,0:T(8,128)}, f32[2,16,2176]{2,1,0:T(8,128)}) custom-call(s32[1]{0:T(128)S(6)} %copy.12.step_ref, f32[1,2,16,4096]{3,2,1,0:T(8,128)} %state_ref.1, f32[16,4096]{1,0:T(8,128)} %vx.1, f32[16,4096]{1,0:T(8,128)} %vy.1, f32[16,4096]{1,0:T(8,128)} %amp.1, f32[16,4096]{1,0:T(8,128)} %freq.1, f32[16,4096]{1,0:T(8,128)} %phase.1), custom_call_target="tpu_custom_call" | custom-call | tf_op jit(solution)/shard_map/pack/pallas_call | solution.py:462
  3.8 0.5 collective-permute-start
  4.3 5.0 %collective-permute-start.1 = (f32[7,16,2176]{2,1,0:T(8,128)}, f32[7,16,2176]{2,1,0:T(8,128)S(1)}, u32[]{:S(2)}, u32[]{:S(2)}) collective-permute-start(f32[7,16,2176]{2,1,0:T(8,128)} %get-tuple-element.7.refs_1_), channel_id=1, source_target_pairs={{0,30},{1,31},{2,0},{3,1},{4,2},{5,3},{6,4},{7,5},{8,6},{9,7},{10,... | collective-permute-start | bytes 2924552 | tf_op jit(solution)/shard_map/ppermute | solution.py:409
  9.2 0.0 collective-permute-start.2
  9.2 2.0 %collective-permute-start.3 = (f32[2,16,2176]{2,1,0:T(8,128)}, f32[2,16,2176]{2,1,0:T(8,128)S(1)}, u32[]{:S(2)}, u32[]{:S(2)}) collective-permute-start(f32[2,16,2176]{2,1,0:T(8,128)} %get-tuple-element.8), channel_id=1, source_target_pairs={{0,1},{1,0},{2,3},{3,2},{4,5},{5,4},{6,7},{7,6},{8,9},{9,8},{10,11... | collective-permute-start | bytes 835592 | tf_op jit(solution)/shard_map/ppermute | solution.py:409
  11.2 5.1 %collective-permute-start.4 = (f32[2,16,2176]{2,1,0:T(8,128)}, f32[2,16,2176]{2,1,0:T(8,128)S(1)}, u32[]{:S(2)}, u32[]{:S(2)}) collective-permute-start(f32[2,16,2176]{2,1,0:T(8,128)} %get-tuple-element.8), channel_id=1, source_target_pairs={{0,31},{1,30},{2,1},{3,0},{4,3},{5,2},{6,5},{7,4},{8,7},{9,6},{10,... | collective-permute-start | bytes 835592 | tf_op jit(solution)/shard_map/ppermute | solution.py:409
  16.3 0.9 dynamic-slice_bitcast_fusion.1
  17.2 0.9 add_bitcast_fusion.refs_7_
  18.1 1.0 %convolution_bitcast_fusion.refs_6_ = f32[32,256]{1,0:T(8,128)S(1)} fusion(f32[64,32]{0,1:T(8,128)} %param.16, f32[64,128]{0,1:T(8,128)S(1)} %get-tuple-element.15, f32[64,128]{0,1:T(8,128)S(1)} %get-tuple-element.14), kind=kOutput, calls=%fused_computation | convolution fusion | flops 6307840 | bytes 106496 | tf_op jit(solution)/shard_map/dot_general | solution.py:485
  19.0 6.7 %collective-permute-done.2.refs_3_ = f32[2,16,2176]{2,1,0:T(8,128)S(1)} collective-permute-done((f32[2,16,2176]{2,1,0:T(8,128)}, f32[2,16,2176]{2,1,0:T(8,128)S(1)}, u32[]{:S(2)}, u32[]{:S(2)}) %collective-permute-start.2) | collective-permute-done | bytes 278560 | tf_op jit(solution)/shard_map/ppermute | solution.py:409
  25.8 1.5 %collective-permute-done.3.refs_4_ = f32[2,16,2176]{2,1,0:T(8,128)S(1)} collective-permute-done((f32[2,16,2176]{2,1,0:T(8,128)}, f32[2,16,2176]{2,1,0:T(8,128)S(1)}, u32[]{:S(2)}, u32[]{:S(2)}) %collective-permute-start.3) | collective-permute-done | bytes 278560 | tf_op jit(solution)/shard_map/ppermute | solution.py:409
  27.3 0.0 collective-permute-done.4.refs_5_
  27.3 0.0 collective-permute-done.refs_0_
  27.3 0.0 collective-permute-done.1.refs_2_
  27.3 0.0 copy-start
  27.3 1.2 %copy-done = f32[7,16,2176]{2,1,0:T(8,128)S(1)} copy-done((f32[7,16,2176]{2,1,0:T(8,128)S(1)}, f32[7,16,2176]{2,1,0:T(8,128)}, u32[]{:S(2)}) %copy-start) | copy-done | bytes 974872
  28.5 31.1 %stencil.1 = (f32[16,128,1024]{2,1,0:T(8,128)}, f32[2,2,16,2048]{3,2,1,0:T(8,128)S(1)}, f32[32,64]{1,0:T(8,128)S(1)}) custom-call(f32[7,16,2176]{2,1,0:T(8,128)S(1)} %collective-permute-done.refs_0_, f32[7,16,2176]{2,1,0:T(8,128)S(1)} %copy-done, f32[7,16,2176]{2,1,0:T(8,128)S(1)} %collective-permute-done.1.refs_2_, ...), custom_call_target="tpu_custom_call" | custom-call | tf_op jit(solution)/shard_map/stencil/pallas_call | solution.py:502
  59.7 0.6 collective-permute-start.5
  60.2 0.8 copy.11
  61.0 0.1 pad.7.clone
  61.1 2.3 %collective-permute-done.5 = f32[32,64]{1,0:T(8,128)S(1)} collective-permute-done((f32[32,64]{1,0:T(8,128)S(1)}, f32[32,64]{1,0:T(8,128)S(1)}, u32[]{:S(2)}, u32[]{:S(2)}) %collective-permute-start.5) | collective-permute-done | bytes 8224 | tf_op jit(solution)/shard_map/ppermute | solution.py:422
  63.5 9.4 %collective-permute-start.6 = (f32[32,64]{1,0:T(8,128)S(1)}, f32[32,64]{1,0:T(8,128)S(1)}, u32[]{:S(2)}, u32[]{:S(2)}) collective-permute-start(f32[32,64]{1,0:T(8,128)S(1)} %add.33), channel_id=1, source_target_pairs={{0,2},{1,3},{2,0},{3,1},{4,6},{5,7},{6,4},{7,5},{8,10},{9,11},{10,... | collective-permute-start | bytes 24584 | tf_op jit(solution)/shard_map/ppermute | solution.py:422
  72.9 0.7 maximum_maximum_fusion.spread_ref
  73.6 0.2 collective-permute-done.6
  73.8 1.4 %collective-permute-start.7 = (f32[32,64]{1,0:T(8,128)S(1)}, f32[32,64]{1,0:T(8,128)S(1)}, u32[]{:S(2)}, u32[]{:S(2)}) collective-permute-start(f32[32,64]{1,0:T(8,128)S(1)} %add.34), channel_id=1, source_target_pairs={{0,4},{1,5},{2,6},{3,7},{4,0},{5,1},{6,2},{7,3},{8,12},{9,13},{10,... | collective-permute-start | bytes 24584 | tf_op jit(solution)/shard_map/ppermute | solution.py:422
  75.2 0.6 collective-permute-start.10
  75.8 1.7 %collective-permute-done.7 = f32[32,64]{1,0:T(8,128)S(1)} collective-permute-done((f32[32,64]{1,0:T(8,128)S(1)}, f32[32,64]{1,0:T(8,128)S(1)}, u32[]{:S(2)}, u32[]{:S(2)}) %collective-permute-start.7) | collective-permute-done | bytes 8224 | tf_op jit(solution)/shard_map/ppermute | solution.py:422
  77.5 0.9 collective-permute-start.8
  78.5 2.8 %collective-permute-done.8 = f32[32,64]{1,0:T(8,128)S(1)} collective-permute-done((f32[32,64]{1,0:T(8,128)S(1)}, f32[32,64]{1,0:T(8,128)S(1)}, u32[]{:S(2)}, u32[]{:S(2)}) %collective-permute-start.8) | collective-permute-done | bytes 8224 | tf_op jit(solution)/shard_map/ppermute | solution.py:422
  81.2 2.0 %collective-permute-start.9 = (f32[32,64]{1,0:T(8,128)S(1)}, f32[32,64]{1,0:T(8,128)S(1)}, u32[]{:S(2)}, u32[]{:S(2)}) collective-permute-start(f32[32,64]{1,0:T(8,128)S(1)} %add.36), channel_id=1, source_target_pairs={{0,16},{1,17},{2,18},{3,19},{4,20},{5,21},{6,22},{7,23},{8,24},{9,... | collective-permute-start | bytes 24584 | tf_op jit(solution)/shard_map/ppermute | solution.py:422
  83.2 0.7 fusion.4.unit_ref
  83.9 0.7 concatenate.33.expand_ref
  84.5 1.4 %collective-permute-done.9 = f32[32,64]{1,0:T(8,128)S(1)} collective-permute-done((f32[32,64]{1,0:T(8,128)S(1)}, f32[32,64]{1,0:T(8,128)S(1)}, u32[]{:S(2)}, u32[]{:S(2)}) %collective-permute-start.9) | collective-permute-done | bytes 8224 | tf_op jit(solution)/shard_map/ppermute | solution.py:422
  85.9 0.6 add.37.left_ref
  86.5 8.5 %merge.1 = f32[32,16,2048]{2,1,0:T(8,128)} custom-call(f32[32,64]{1,0:T(8,128)} %add.37.left_ref, f32[64,128]{1,0:T(8,128)} %maximum_maximum_fusion.spread_ref, f32[32,128]{1,0:T(8,128)} %fusion.4.unit_ref, f32[128,256]{1,0:T(8,128)} %concatenate.33.expand_ref, f32[16,128,1024]{2,1,0:T(8,128)} %get-tuple-element.10.snap_ref), custom_call_target="tpu_custom_call" | custom-call | tf_op jit(solution)/shard_map/merge/pallas_call | solution.py:516
  95.0 0.0 collective-permute-done.10
  95.0 0.8 maximum_select_fusion
  (8 shorter events, 0.1 us)
Async XLA Ops:
  3.8 23.5 %collective-permute-start = (f32[7,16,2176]{2,1,0:T(8,128)}, f32[7,16,2176]{2,1,0:T(8,128)S(1)}, u32[]{:S(2)}, u32[]{:S(2)}) collective-permute-start(f32[7,16,2176]{2,1,0:T(8,128)} %get-tuple-element.7.refs_1_), channel_id=1, source_target_pairs={{0,2},{1,3},{2,4},{3,5},{4,6},{5,7},{6,8},{7,9},{8,10},{9,11},{10,... | collective-permute-start | bytes 2924552 | tf_op jit(solution)/shard_map/ppermute | solution.py:409
  4.3 23.0 %collective-permute-start.1 = (f32[7,16,2176]{2,1,0:T(8,128)}, f32[7,16,2176]{2,1,0:T(8,128)S(1)}, u32[]{:S(2)}, u32[]{:S(2)}) collective-permute-start(f32[7,16,2176]{2,1,0:T(8,128)} %get-tuple-element.7.refs_1_), channel_id=1, source_target_pairs={{0,30},{1,31},{2,0},{3,1},{4,2},{5,3},{6,4},{7,5},{8,6},{9,7},{10,... | collective-permute-start | bytes 2924552 | tf_op jit(solution)/shard_map/ppermute | solution.py:409
  9.2 16.5 %collective-permute-start.2 = (f32[2,16,2176]{2,1,0:T(8,128)}, f32[2,16,2176]{2,1,0:T(8,128)S(1)}, u32[]{:S(2)}, u32[]{:S(2)}) collective-permute-start(f32[2,16,2176]{2,1,0:T(8,128)} %get-tuple-element.8), channel_id=1, source_target_pairs={{0,3},{1,2},{2,5},{3,4},{4,7},{5,6},{6,9},{7,8},{8,11},{9,10},{10,... | collective-permute-start | bytes 835592 | tf_op jit(solution)/shard_map/ppermute | solution.py:409
  9.2 18.1 %collective-permute-start.3 = (f32[2,16,2176]{2,1,0:T(8,128)}, f32[2,16,2176]{2,1,0:T(8,128)S(1)}, u32[]{:S(2)}, u32[]{:S(2)}) collective-permute-start(f32[2,16,2176]{2,1,0:T(8,128)} %get-tuple-element.8), channel_id=1, source_target_pairs={{0,1},{1,0},{2,3},{3,2},{4,5},{5,4},{6,7},{7,6},{8,9},{9,8},{10,11... | collective-permute-start | bytes 835592 | tf_op jit(solution)/shard_map/ppermute | solution.py:409
  11.2 16.1 %collective-permute-start.4 = (f32[2,16,2176]{2,1,0:T(8,128)}, f32[2,16,2176]{2,1,0:T(8,128)S(1)}, u32[]{:S(2)}, u32[]{:S(2)}) collective-permute-start(f32[2,16,2176]{2,1,0:T(8,128)} %get-tuple-element.8), channel_id=1, source_target_pairs={{0,31},{1,30},{2,1},{3,0},{4,3},{5,2},{6,5},{7,4},{8,7},{9,6},{10,... | collective-permute-start | bytes 835592 | tf_op jit(solution)/shard_map/ppermute | solution.py:409
  27.3 1.2 %copy-start = (f32[7,16,2176]{2,1,0:T(8,128)S(1)}, f32[7,16,2176]{2,1,0:T(8,128)}, u32[]{:S(2)}) copy-start(f32[7,16,2176]{2,1,0:T(8,128)} %get-tuple-element.7.refs_1_) | copy-start | bytes 2924548
  59.7 3.8 %collective-permute-start.5 = (f32[32,64]{1,0:T(8,128)S(1)}, f32[32,64]{1,0:T(8,128)S(1)}, u32[]{:S(2)}, u32[]{:S(2)}) collective-permute-start(f32[32,64]{1,0:T(8,128)S(1)} %get-tuple-element.9), channel_id=1, source_target_pairs={{0,1},{1,0},{2,3},{3,2},{4,5},{5,4},{6,7},{7,6},{8,9},{9,8},{10,11... | collective-permute-start | bytes 24584 | tf_op jit(solution)/shard_map/ppermute | solution.py:422
  63.5 10.3 %collective-permute-start.6 = (f32[32,64]{1,0:T(8,128)S(1)}, f32[32,64]{1,0:T(8,128)S(1)}, u32[]{:S(2)}, u32[]{:S(2)}) collective-permute-start(f32[32,64]{1,0:T(8,128)S(1)} %add.33), channel_id=1, source_target_pairs={{0,2},{1,3},{2,0},{3,1},{4,6},{5,7},{6,4},{7,5},{8,10},{9,11},{10,... | collective-permute-start | bytes 24584 | tf_op jit(solution)/shard_map/ppermute | solution.py:422
  73.8 3.7 %collective-permute-start.7 = (f32[32,64]{1,0:T(8,128)S(1)}, f32[32,64]{1,0:T(8,128)S(1)}, u32[]{:S(2)}, u32[]{:S(2)}) collective-permute-start(f32[32,64]{1,0:T(8,128)S(1)} %add.34), channel_id=1, source_target_pairs={{0,4},{1,5},{2,6},{3,7},{4,0},{5,1},{6,2},{7,3},{8,12},{9,13},{10,... | collective-permute-start | bytes 24584 | tf_op jit(solution)/shard_map/ppermute | solution.py:422
  75.2 19.8 %collective-permute-start.10 = (f32[2,16,2048]{2,1,0:T(8,128)S(1)}, f32[2,16,2048]{2,1,0:T(8,128)S(1)}, u32[]{:S(2)}, u32[]{:S(2)}) collective-permute-start(f32[2,16,2048]{2,1,0:T(8,128)S(1)} %get-tuple-element.13), channel_id=1, source_target_pairs={{0,1},{1,0},{2,3},{3,2},{4,5},{5,4},{6,7},{7,6},{8,9},{9,8},{10,11... | collective-permute-start | bytes 786440 | tf_op jit(solution)/shard_map/ppermute | solution.py:409
  77.5 3.7 %collective-permute-start.8 = (f32[32,64]{1,0:T(8,128)S(1)}, f32[32,64]{1,0:T(8,128)S(1)}, u32[]{:S(2)}, u32[]{:S(2)}) collective-permute-start(f32[32,64]{1,0:T(8,128)S(1)} %add.35), channel_id=1, source_target_pairs={{0,8},{1,9},{2,10},{3,11},{4,12},{5,13},{6,14},{7,15},{8,0},{9,1},... | collective-permute-start | bytes 24584 | tf_op jit(solution)/shard_map/ppermute | solution.py:422
  81.2 4.6 %collective-permute-start.9 = (f32[32,64]{1,0:T(8,128)S(1)}, f32[32,64]{1,0:T(8,128)S(1)}, u32[]{:S(2)}, u32[]{:S(2)}) collective-permute-start(f32[32,64]{1,0:T(8,128)S(1)} %add.36), channel_id=1, source_target_pairs={{0,16},{1,17},{2,18},{3,19},{4,20},{5,21},{6,22},{7,23},{8,24},{9,... | collective-permute-start | bytes 24584 | tf_op jit(solution)/shard_map/ppermute | solution.py:422

commit v4 on v3

--- a/solution.py
+++ b/solution.py
@@ -16,6 +16,7 @@
 GUARD = 8
 BATCH = 4
 OWN = 8
+REACH = STEPS // 2
 VMEM = pl.BlockSpec(memory_space=pltpu.VMEM)
 HBM = pl.BlockSpec(memory_space=pltpu.HBM)
 SMEM = pl.BlockSpec(memory_space=pltpu.SMEM)
@@ -35,7 +36,7 @@
     return lax.broadcasted_iota(jnp.int32, shape, len(shape) - 1)
 
 
-def pack_kernel(groups, block, step_ref, state_ref, vx, vy, amp, freq, phase, own_ref, *peer_refs):
+def pack_kernel(groups, block, step_ref, state_ref, vx, vy, amp, freq, phase, *out_refs):
     full = vx.shape[1]
     me = lax.axis_index("tm")
     start = step_ref[0].astype(jnp.float32)
@@ -56,21 +57,22 @@
             halo = jnp.where((lane >= TILE // 4) & (lane < 3 * TILE // 4), start, halo)
         write(pl.ds(block, TILE), halo)
 
-    def writer(ref, index):
+    def writer(group, index):
+        low, every, high = out_refs[3 * group : 3 * group + 3]
+
         def write(columns, value):
-            ref[index, :, columns] = value
+            low[index, :, columns] = value[:REACH]
+            every[index, :, columns] = value
+            high[index, :, columns] = value[rows - REACH :]
 
         return write
 
     for index, ref in enumerate((vx, vy, amp, freq, phase)):
-        cut(lambda columns, ref=ref: ref[:, columns], me, writer(own_ref, index), False)
+        cut(lambda columns, ref=ref: ref[:, columns], me, writer(0, index), False)
     for shift in range(groups):
         target = lax.rem(me + shift, groups)
         for field in range(2):
-            if shift == 0:
-                write = writer(own_ref, 5 + field)
-            else:
-                write = writer(peer_refs[shift - 1], field)
+            write = writer(shift, 5 + field if shift == 0 else field)
             cut(lambda columns, field=field: state_ref[0, field, :, columns], target, write, True)
 
 
@@ -103,111 +105,15 @@
     return s, c
 
 
-def stencil_kernel(groups, halves, with_left, *refs):
-    count = 3 * groups
-    sources = [refs[3 * i : 3 * i + 3] for i in range(groups)]
-    refs = refs[count:]
-    if with_left:
-        select_ref, fold_ref = refs[:2]
-        refs = refs[2:]
-        snap_ref, end_ref, left_ref = refs[:3]
-        refs = refs[3:]
-    else:
-        snap_ref, end_ref = refs[:2]
-        refs = refs[2:]
-    qa, qb, xa, xb, twice, cw, ce, cs, cn, c0, snap, sems = refs
-    rows = sources[0][0].shape[1]
-    block = sources[0][0].shape[2] - TILE
-    length = block // halves
-    tiles = length // TILE + 1
-    subs = halves * groups * 2
-    total = 3 * rows
-    me = lax.axis_index("tm")
-
-    sub = lax.broadcasted_iota(jnp.int32, (1, subs, TILE), 1)
-    kappa = jnp.where((sub & 1) == 0, np.float32(KAPPA[0]), np.float32(KAPPA[1]))
-    half_of = sub // (2 * groups)
-    lane3 = lanes_of((1, subs, TILE))
-    lowest = (me == 0) & (half_of == 0) & (lane3 >= TILE // 2)
-    highest = (me == groups - 1) & (half_of == halves - 1) & (lane3 < TILE // 2)
-    inside = jnp.where(lowest | highest, 0.0, 1.0).astype(jnp.float32)
-    lane2 = lanes_of((8, TILE))
+def run_phase(grid, rows, snap, snap_ref, sems, keep_drift):
+    qa, qb, xa, xb, twice, cw, ce, cs, cn, c0 = grid
+    subs = qa.shape[1]
+    tiles = qa.shape[2] // TILE
+    total = rows + 2 * REACH
 
     for guard in (GUARD - 1, GUARD + total):
         qa[guard] = jnp.zeros(qa.shape[1:], jnp.float32)
         qb[guard] = jnp.zeros(qb.shape[1:], jnp.float32)
-
-    def turned(parts):
-        return jnp.swapaxes(jnp.stack(parts, axis=0), 0, 1)
-
-    def prepare(place, base, tile, halo):
-        def cut(ref, index, half):
-            line = pl.ds(base, 8)
-            if not halo:
-                return ref[index, line, pl.ds(pl.multiple_of(half * length + tile * TILE, TILE), TILE)]
-            above = (half + 1) * length
-            below = half * length - TILE if half > 0 else block
-            high = ref[index, line, above : above + TILE]
-            if above == below:
-                return high
-            low = ref[index, line, below : below + TILE]
-            return jnp.where(lane2 < TILE // 2, high, low)
-
-        own = sources[0][place]
-        starts, first, second, flow_x, flow_y, doubled = [], [], [], [], [], []
-        for half in range(halves):
-            vx, vy, amp, freq, phase = (cut(own, index, half) for index in range(5))
-            sin_f, cos_f = sin_cos(freq)
-            for group in range(groups):
-                ref, at = sources[group][place], 5 if group == 0 else 0
-                step = ref[at, pl.ds(base, 8), block : block + TILE][:, TILE // 2 : TILE // 2 + 1]
-                s, c = sin_cos(freq * step + phase)
-                s, c = amp * s, amp * c
-                for field in range(2):
-                    starts.append(cut(ref, at + field, half))
-                    x, y = (s, c) if field == 0 else (0.5 * c, -0.5 * s)
-                    first.append(x)
-                    second.append(x * cos_f + y * sin_f)
-                    flow_x.append(vx)
-                    flow_y.append(vy)
-                    doubled.append(2.0 * cos_f)
-        where = pl.ds(place * rows + base, 8)
-        columns = pl.ds(pl.multiple_of(tile * TILE, TILE), TILE)
-        vx, vy = turned(flow_x), turned(flow_y)
-        west = kappa + jnp.maximum(vx, 0.0)
-        east = kappa - jnp.minimum(vx, 0.0)
-        south = kappa + jnp.maximum(vy, 0.0)
-        north = kappa - jnp.minimum(vy, 0.0)
-        centre = 1.0 - (west + east + south + north)
-        state, x0, x1 = turned(starts), turned(first), turned(second)
-        if halo:
-            west, east, south, north, centre, state, x0, x1 = (
-                v * inside for v in (west, east, south, north, centre, state, x0, x1)
-            )
-        cw[where, :, columns] = west
-        ce[where, :, columns] = east
-        cs[where, :, columns] = south
-        cn[where, :, columns] = north
-        c0[where, :, columns] = centre
-        xa[where, :, columns] = x0
-        xb[where, :, columns] = x1
-        twice[where, :, columns] = turned(doubled)
-        qa[pl.ds(GUARD + place * rows + base, 8), :, columns] = state
-
-    for place in range(3):
-
-        def by_rows(number, carry, place=place):
-            base = pl.multiple_of(number * 8, 8)
-
-            def by_tiles(tile, inner):
-                prepare(place, base, tile, False)
-                return inner
-
-            lax.fori_loop(0, tiles - 1, by_tiles, 0)
-            prepare(place, base, tiles - 1, True)
-            return carry
-
-        lax.fori_loop(0, rows // 8, by_rows, 0)
 
     lane2s = lanes_of((subs, TILE))
     first_lane, last_lane = lane2s == 0, lane2s == TILE - 1
@@ -246,7 +152,11 @@
                 target[GUARD + x, :, cols] = fresh
                 now[x, :, cols] = twice[x, :, cols] * later[x, :, cols] - drive
                 if keep and t < tiles - 1:
-                    snap[x - rows, pl.ds(pl.multiple_of(step * subs, subs), subs), cols] = fresh
+                    snap[x - REACH, pl.ds(pl.multiple_of(step * subs, subs), subs), cols] = fresh
+
+    def copy_out(step):
+        part = pl.ds(pl.multiple_of(step * subs, subs), subs)
+        return pltpu.make_async_copy(snap.at[:, part, :], snap_ref.at[:, part, :], sems.at[step])
 
     def one(source, target, now, later, step):
         low = (step + 1) // BATCH
@@ -257,29 +167,212 @@
             return carry
 
         def own_rows(i, carry):
-            advance(source, target, now, later, i * OWN, OWN, step, True)
+            advance(source, target, now, later, REACH + i * OWN, OWN, step, True)
             return carry
 
-        lax.fori_loop(low, rows // BATCH, halo_rows, 0)
-        lax.fori_loop(rows // OWN, 2 * rows // OWN, own_rows, 0)
+        def drift_rows(i, carry):
+            part = pl.ds(i * BATCH, BATCH)
+            now[part] = twice[part] * later[part] - now[part]
+            return carry
+
+        lax.fori_loop(0, rows // OWN, own_rows, 0)
         copy_out(step).start()
-        lax.fori_loop(2 * rows // BATCH, high, halo_rows, 0)
-
-    def copy_out(step):
-        part = pl.ds(pl.multiple_of(step * subs, subs), subs)
-        return pltpu.make_async_copy(snap.at[:, part, :], snap_ref.at[:, part, :], sems.at[step])
+        lax.fori_loop(low, REACH // BATCH, halo_rows, 0)
+        lax.fori_loop((REACH + rows) // BATCH, high, halo_rows, 0)
+        if keep_drift:
+            lax.fori_loop(0, low, drift_rows, 0)
+            lax.fori_loop(high, total // BATCH, drift_rows, 0)
 
     def pair(i, carry):
         one(qa, qb, xa, xb, 2 * i)
         one(qb, qa, xb, xa, 2 * i + 1)
         return carry
 
-    lax.fori_loop(0, STEPS // 2, pair, 0)
+    lax.fori_loop(0, REACH // 2, pair, 0)
+
+    def drain():
+        def drained(step, carry):
+            copy_out(step).wait()
+            return carry
+
+        lax.fori_loop(0, REACH, drained, 0)
+
+    return drain
+
+
+def first_kernel(groups, halves, *refs):
+    sources = [refs[3 * i : 3 * i + 3] for i in range(groups)]
+    snap_ref, carry_ref, low_ref, own_ref, high_ref = refs[3 * groups : 3 * groups + 5]
+    refs = refs[3 * groups + 5 :]
+    grid, (snap, sems, carry_sems) = refs[:10], refs[10:]
+    qa, qb, xa, xb, twice, cw, ce, cs, cn, c0 = grid
+    rows = sources[0][1].shape[1]
+    block = sources[0][1].shape[2] - TILE
+    length = block // halves
+    tiles = length // TILE + 1
+    subs = halves * groups * 2
+    me = lax.axis_index("tm")
+    offsets = (0, REACH, REACH + rows)
+
+    sub = lax.broadcasted_iota(jnp.int32, (1, subs, TILE), 1)
+    kappa = jnp.where((sub & 1) == 0, np.float32(KAPPA[0]), np.float32(KAPPA[1]))
+    half_of = sub // (2 * groups)
+    lane3 = lanes_of((1, subs, TILE))
+    lowest = (me == 0) & (half_of == 0) & (lane3 >= TILE // 2)
+    highest = (me == groups - 1) & (half_of == halves - 1) & (lane3 < TILE // 2)
+    inside = jnp.where(lowest | highest, 0.0, 1.0).astype(jnp.float32)
+    lane2 = lanes_of((8, TILE))
+
+    def turned(parts):
+        return jnp.swapaxes(jnp.stack(parts, axis=0), 0, 1)
+
+    def prepare(place, base, tile, halo):
+        def cut(ref, index, half):
+            line = pl.ds(base, 8)
+            if not halo:
+                return ref[index, line, pl.ds(pl.multiple_of(half * length + tile * TILE, TILE), TILE)]
+            above = (half + 1) * length
+            below = half * length - TILE if half > 0 else block
+            high = ref[index, line, above : above + TILE]
+            if above == below:
+                return high
+            low = ref[index, line, below : below + TILE]
+            return jnp.where(lane2 < TILE // 2, high, low)
+
+        own = sources[0][place]
+        starts, first, second, flow_x, flow_y, doubled = [], [], [], [], [], []
+        for half in range(halves):
+            vx, vy, amp, freq, phase = (cut(own, index, half) for index in range(5))
+            sin_f, cos_f = sin_cos(freq)
+            for group in range(groups):
+                ref, at = sources[group][place], 5 if group == 0 else 0
+                step = ref[at, pl.ds(base, 8), block : block + TILE][:, TILE // 2 : TILE // 2 + 1]
+                s, c = sin_cos(freq * step + phase)
+                s, c = amp * s, amp * c
+                for field in range(2):
+                    starts.append(cut(ref, at + field, half))
+                    x, y = (s, c) if field == 0 else (0.5 * c, -0.5 * s)
+                    first.append(x)
+                    second.append(x * cos_f + y * sin_f)
+                    flow_x.append(vx)
+                    flow_y.append(vy)
+                    doubled.append(2.0 * cos_f)
+        where = pl.ds(offsets[place] + base, 8)
+        columns = pl.ds(pl.multiple_of(tile * TILE, TILE), TILE)
+        vx, vy = turned(flow_x), turned(flow_y)
+        west = kappa + jnp.maximum(vx, 0.0)
+        east = kappa - jnp.minimum(vx, 0.0)
+        south = kappa + jnp.maximum(vy, 0.0)
+        north = kappa - jnp.minimum(vy, 0.0)
+        centre = 1.0 - (west + east + south + north)
+        state, x0, x1 = turned(starts), turned(first), turned(second)
+        if halo:
+            west, east, south, north, centre, state, x0, x1 = (
+                v * inside for v in (west, east, south, north, centre, state, x0, x1)
+            )
+        cw[where, :, columns] = west
+        ce[where, :, columns] = east
+        cs[where, :, columns] = south
+        cn[where, :, columns] = north
+        c0[where, :, columns] = centre
+        xa[where, :, columns] = x0
+        xb[where, :, columns] = x1
+        twice[where, :, columns] = turned(doubled)
+        qa[pl.ds(GUARD + offsets[place] + base, 8), :, columns] = state
+
+    for place, count in ((0, REACH), (1, rows), (2, REACH)):
+
+        def by_rows(number, carry, place=place):
+            base = pl.multiple_of(number * 8, 8)
+
+            def by_tiles(tile, inner):
+                prepare(place, base, tile, False)
+                return inner
+
+            lax.fori_loop(0, tiles - 1, by_tiles, 0)
+            prepare(place, base, tiles - 1, True)
+            return carry
+
+        lax.fori_loop(0, count // 8, by_rows, 0)
+
+    def keep(i):
+        return pltpu.make_async_copy(grid[2 + i], carry_ref.at[i], carry_sems.at[i])
+
+    for i in range(2, 8):
+        keep(i).start()
+    drain = run_phase(grid, rows, snap, snap_ref, sems, True)
+    for i in range(2):
+        keep(i).start()
+    low_ref[...] = qa[GUARD + REACH : GUARD + 2 * REACH]
+    own_ref[...] = qa[GUARD + REACH : GUARD + REACH + rows]
+    high_ref[...] = qa[GUARD + rows : GUARD + rows + REACH]
+    drain()
+    for i in range(8):
+        keep(i).wait()
+
+
+def split_rows(a):
+    high = a.astype(jnp.bfloat16)
+    return jnp.concatenate([high, (a - high.astype(jnp.float32)).astype(jnp.bfloat16)], axis=0)
+
+
+def outer_of(a, b):
+    return lax.dot_general(a, b, (((1,), (1,)), ((), ())), preferred_element_type=jnp.float32)
+
+
+def joined(g):
+    m, n = g.shape[0] // 2, g.shape[1] // 2
+    return (g[:m, :n] + g[m:, n:]) + (g[:m, n:] + g[m:, :n])
+
+
+def gram_kernel(snap_ref, gram_ref):
+    width = snap_ref.shape[1]
+
+    @pl.when(pl.program_id(0) == 0)
+    def _():
+        gram_ref[...] = jnp.zeros_like(gram_ref)
+
+    total = jnp.zeros((2 * width, 2 * width), jnp.float32)
+    for x in range(snap_ref.shape[0]):
+        both = split_rows(snap_ref[x])
+        total = total + outer_of(both, both)
+    gram_ref[...] += joined(total)
+
+
+def second_kernel(groups, halves, with_left, left_halo, own, right_halo, carry_ref, earlier_ref, *refs):
+    if with_left:
+        gram_ref, select_ref, fold_ref = refs[:3]
+        refs = refs[3:]
+        snap_ref, end_ref, left_ref = refs[:3]
+        refs = refs[3:]
+    else:
+        snap_ref, end_ref = refs[:2]
+        refs = refs[2:]
+    grid, (snap, earlier, sems, carry_sems, more_sems) = refs[:10], refs[10:]
+    qa = grid[0]
+    rows, width, length = snap.shape
+    subs = qa.shape[1]
+    tiles = length // TILE + 1
+
+    def bring(i):
+        return pltpu.make_async_copy(carry_ref.at[i], grid[2 + i], carry_sems.at[i])
+
+    late = pltpu.make_async_copy(earlier_ref, earlier, more_sems.at[0])
+    for i in range(8):
+        bring(i).start()
+    if with_left:
+        late.start()
+    qa[GUARD : GUARD + REACH] = left_halo[...]
+    qa[GUARD + REACH : GUARD + REACH + rows] = own[...]
+    qa[GUARD + REACH + rows : GUARD + 2 * REACH + rows] = right_halo[...]
+    for i in range(8):
+        bring(i).wait()
+    drain = run_phase(grid, rows, snap, snap_ref, sems, False)
 
     for base in range(0, rows, 8):
         for t in range(tiles - 1):
             cols = slice(t * TILE, (t + 1) * TILE)
-            value = jnp.swapaxes(qa[GUARD + rows + base : GUARD + rows + base + 8, :, cols], 0, 1)
+            value = jnp.swapaxes(qa[GUARD + REACH + base : GUARD + REACH + base + 8, :, cols], 0, 1)
             for half in range(halves):
                 for group in range(groups):
                     for field in range(2):
@@ -288,31 +381,27 @@
                         ] = value[half * groups * 2 + group * 2 + field]
 
     if with_left:
-        width = STEPS * subs
+        late.wait()
 
         def add(x, total):
-            a = snap[x]
-            high = a.astype(jnp.bfloat16)
-            low = (a - high.astype(jnp.float32)).astype(jnp.bfloat16)
-            both = jnp.concatenate([high, low], axis=0)
-            return total + lax.dot_general(
-                both, both, (((1,), (1,)), ((), ())), preferred_element_type=jnp.float32
-            )
-
-        gram = lax.fori_loop(0, rows, add, jnp.zeros((2 * width, 2 * width), jnp.float32))
-        gram = (gram[:width, :width] + gram[width:, width:]) + (gram[:width, width:] + gram[width:, :width])
+            now = split_rows(snap[x])
+            every = jnp.concatenate([now, split_rows(earlier[x])], axis=0)
+            return total + outer_of(now, every)
+
+        both = lax.fori_loop(0, rows, add, jnp.zeros((2 * width, 4 * width), jnp.float32))
+        late_late, late_early = joined(both[:, : 2 * width]), joined(both[:, 2 * width :])
         lane = lanes_of((1, width))
-        left = jnp.zeros((select_ref.shape[0], width), jnp.float32)
+        result = jnp.zeros(left_ref.shape, jnp.float32)
         for half in range(halves):
-            part = mm(select_ref[:, half * width : (half + 1) * width], gram)
-            left = left + jnp.where((lane % subs) // (2 * groups) == half, part, 0.0)
-        left_ref[...] = mm(left, fold_ref[...])
-
-    def drained(step, carry):
-        copy_out(step).wait()
-        return carry
-
-    lax.fori_loop(0, STEPS, drained, 0)
+            inside = (lane % subs) // (2 * groups) == half
+            at = half * 2 * width
+            early, later = select_ref[:, at : at + width], select_ref[:, at + width : at + 2 * width]
+            part = mm(early, gram_ref[...]) + mm(later, late_early)
+            result = result + mm(jnp.where(inside, part, 0.0), fold_ref[:width])
+            part = mm_nt(early, late_early) + mm(later, late_late)
+            result = result + mm(jnp.where(inside, part, 0.0), fold_ref[width:])
+        left_ref[...] = result
+    drain()
 
 
 def eliminate(m, rank):
@@ -345,22 +434,25 @@
 CHUNK = 256
 
 
-def merge_kernel(halves, left_ref, spread_ref, unit_ref, expand_ref, snap_ref, out_ref, snap, out, arrived, left_sems):
+def merge_kernel(halves, left_ref, spread_ref, unit_ref, expand_ref, early_ref, late_ref, out_ref, snap, out, arrived, left_sems):
     rank = left_ref.shape[0]
     wide = left_ref.shape[1]
     rows, width, length = snap.shape
     parts = length // CHUNK
 
-    def fetch(i):
+    def fetch(i, part):
         at = pl.ds(i * CHUNK, CHUNK)
-        return pltpu.make_async_copy(snap_ref.at[:, :, at], snap.at[:, :, at], arrived.at[i])
+        ref = (early_ref, late_ref)[part]
+        columns = pl.ds(part * (width // 2), width // 2)
+        return pltpu.make_async_copy(ref.at[:, :, at], snap.at[:, columns, at], arrived.at[i, part])
 
     def store(i, half):
         at = pl.ds(half * length + i * CHUNK, CHUNK)
         return pltpu.make_async_copy(out.at[:, :, at], out_ref.at[:, :, at], left_sems.at[i, half])
 
     for i in range(parts):
-        fetch(i).start()
+        fetch(i, 0).start()
+        fetch(i, 1).start()
     lane = lanes_of((rank, 128))
     whole = eliminate(mm(left_ref[...], spread_ref[...]) + unit_ref[...], rank)
     proj = jnp.where((lane >= rank) & (lane < rank + wide), whole, 0.0)
@@ -379,7 +471,8 @@
         [jnp.concatenate([high, high], axis=1), jnp.concatenate([low, low], axis=1)], axis=0
     )
     for i in range(parts):
-        fetch(i).wait()
+        fetch(i, 0).wait()
+        fetch(i, 1).wait()
         for base in range(0, rows, 8):
             made = []
             for x in range(base, base + 8):
@@ -459,17 +552,21 @@
     fast = groups == 2
     f32 = jnp.float32
 
+    total = rows + 2 * REACH
+    shapes = [jax.ShapeDtypeStruct((7, count, block + TILE), f32) for count in (REACH, rows, REACH)]
+    for _ in range(groups - 1):
+        shapes += [jax.ShapeDtypeStruct((2, count, block + TILE), f32) for count in (REACH, rows, REACH)]
     packed = pl.pallas_call(
         functools.partial(pack_kernel, groups, block),
-        out_shape=[jax.ShapeDtypeStruct((7, rows, block + TILE), f32)]
-        + [jax.ShapeDtypeStruct((2, rows, block + TILE), f32)] * (groups - 1),
+        out_shape=shapes,
         in_specs=[SMEM] + [VMEM] * 6,
-        out_specs=[VMEM] * groups,
+        out_specs=[VMEM] * len(shapes),
         name="pack",
     )(start_step, start_state, velocity_x, velocity_y, amplitude, frequency, phase)
-    sources = [shifted(packed[0], 1, 0), packed[0], shifted(packed[0], -1, 0)]
+    sources = [shifted(packed[2], 1, 0), packed[1], shifted(packed[0], -1, 0)]
     for shift in range(1, groups):
-        sources += [shifted(packed[shift], move, shift) for move in (1, 0, -1)]
+        low, every, high = packed[3 * shift : 3 * shift + 3]
+        sources += [shifted(high, 1, shift), shifted(every, 0, shift), shifted(low, -1, shift)]
 
     extra = []
     if fast:
@@ -492,43 +589,69 @@
         expand = jnp.concatenate([jnp.zeros((128 - rank, halves * width), f32), select], axis=0)
         extra = [select, fold]
 
-    outs = [
-        pltpu.HBM((rows, width, length), f32),
-        jax.ShapeDtypeStruct((groups, 2, rows, block), f32),
-    ]
+    grid = [pltpu.VMEM((total + 2 * GUARD, subs, span), f32)] * 2 + [pltpu.VMEM((total, subs, span), f32)] * 8
+    half_snap = (rows, width // 2, length)
+    early, carry, low, own, high = pl.pallas_call(
+        functools.partial(first_kernel, groups, halves),
+        out_shape=[
+            pltpu.HBM(half_snap, f32),
+            pltpu.HBM((8, total, subs, span), f32),
+            jax.ShapeDtypeStruct((REACH, subs, span), f32),
+            jax.ShapeDtypeStruct((rows, subs, span), f32),
+            jax.ShapeDtypeStruct((REACH, subs, span), f32),
+        ],
+        in_specs=[VMEM] * len(sources),
+        out_specs=[HBM] * 2 + [VMEM] * 3,
+        scratch_shapes=grid
+        + [pltpu.VMEM(half_snap, f32), pltpu.SemaphoreType.DMA((REACH,)), pltpu.SemaphoreType.DMA((8,))],
+        compiler_params=pltpu.CompilerParams(vmem_limit_bytes=36 * 2**20),
+        name="first",
+    )(*sources)
+    beside = [shifted(high, 1, 0), own, shifted(low, -1, 0)]
+    outs = [pltpu.HBM(half_snap, f32), jax.ShapeDtypeStruct((groups, 2, rows, block), f32)]
     if fast:
         outs.append(jax.ShapeDtypeStruct((sketch.shape[1], sketch.shape[0]), f32))
-    grid_of = (3 * rows, subs, span)
+        gram = pl.pallas_call(
+            gram_kernel,
+            out_shape=jax.ShapeDtypeStruct((width // 2, width // 2), f32),
+            grid=(4,),
+            in_specs=[pl.BlockSpec((rows // 4, width // 2, length), lambda i: (i, 0, 0))],
+            out_specs=pl.BlockSpec((width // 2, width // 2), lambda i: (0, 0)),
+            cost_estimate=pl.CostEstimate(flops=2 * rows * width * width * length, bytes_accessed=2 * rows * width * length, transcendentals=0),
+            compiler_params=pltpu.CompilerParams(vmem_limit_bytes=16 * 2**20),
+            name="gram",
+        )(early)
+        extra = [gram] + extra
     made = pl.pallas_call(
-        functools.partial(stencil_kernel, groups, halves, fast),
+        functools.partial(second_kernel, groups, halves, fast),
         out_shape=outs,
-        in_specs=[VMEM] * (len(sources) + len(extra)),
+        in_specs=[VMEM] * 3 + [HBM] * 2 + [VMEM] * len(extra),
         out_specs=[HBM] + [VMEM] * (len(outs) - 1),
-        scratch_shapes=[pltpu.VMEM((3 * rows + 2 * GUARD, subs, span), f32)] * 2
-        + [pltpu.VMEM(grid_of, f32)] * 8
-        + [pltpu.VMEM((rows, width, length), f32), pltpu.SemaphoreType.DMA((STEPS,))],
-        compiler_params=pltpu.CompilerParams(vmem_limit_bytes=36 * 2**20),
-        name="stencil",
-    )(*sources, *extra)
+        scratch_shapes=grid
+        + [pltpu.VMEM(half_snap, f32)] * 2
+        + [pltpu.SemaphoreType.DMA((REACH,)), pltpu.SemaphoreType.DMA((8,)), pltpu.SemaphoreType.DMA((1,))],
+        compiler_params=pltpu.CompilerParams(vmem_limit_bytes=40 * 2**20),
+        name="second",
+    )(*beside, carry, early, *extra)
 
     if fast:
         left = total_of(made[2])
         piece = pl.pallas_call(
             functools.partial(merge_kernel, halves),
             out_shape=jax.ShapeDtypeStruct((rank, rows, block), f32),
-            in_specs=[VMEM] * 4 + [HBM],
+            in_specs=[VMEM] * 4 + [HBM] * 2,
             out_specs=HBM,
             scratch_shapes=[
                 pltpu.VMEM((rows, width, length), f32),
                 pltpu.VMEM((rank, rows, block), f32),
-                pltpu.SemaphoreType.DMA((length // CHUNK,)),
+                pltpu.SemaphoreType.DMA((length // CHUNK, 2)),
                 pltpu.SemaphoreType.DMA((length // CHUNK, halves)),
             ],
             compiler_params=pltpu.CompilerParams(vmem_limit_bytes=54 * 2**20),
             name="merge",
-        )(left, spread, unit, expand, made[0])
+        )(left, spread, unit, expand, early, made[0])
     else:
-        snaps = made[0].reshape(rows, STEPS, halves, groups, 2, length)
+        snaps = jnp.concatenate([early, made[0]], axis=1).reshape(rows, STEPS, halves, groups, 2, length)
         snaps = jnp.transpose(snaps, (3, 4, 1, 0, 2, 5)).reshape(groups, 2 * STEPS, rows, block)
         snaps = turn(jnp.flip(snaps, 0), groups - 1 - me)
         piece = merge_levels(snaps, sketch)

time: 96.3 us -> 90.8 us (0.943)
  waiting for transfers between devices: 16.6 us -> 8.81 us
  Pallas kernels: 42.2 us -> 43.8 us
  local copies, waits for them, and re-layouts: 3.65 us -> 5.13 us
    ppermute x6 -> x8, waiting for transfers between devices: 8.27 us -> 2.23 us  [shifted(): return lax.ppermute(value, AXES, moves)]
    ppermute x6 -> x8, starting transfers between devices: 13 us -> 18.2 us  [shifted(): return lax.ppermute(value, AXES, moves)]
    ppermute x5, starting transfers between devices: 14.3 us -> 10.1 us  [total_of(): lax.ppermute(value, AXES, [(i, i ^ bit) for i in range(size)])]
    ppermute x5, waiting for transfers between devices: 8.38 us -> 6.57 us  [total_of(): lax.ppermute(value, AXES, [(i, i ^ bit) for i in range(size)])]
    pallas_call x2 -> x4, Pallas kernels: 33.7 us -> 35.2 us  [the longest x1 16.9 us: body(): pl.pallas_call(functools.partial(second_kernel, groups, halves, fast), ou...]
    unnamed x3 -> x11, local copies, waits for them, and re-layouts: 1.99 us -> 3.47 us
  transfers between devices with their start and end apart: 11 -> 13, of which waited for: 7 -> 6; matrix products, arithmetic and copies ran while one was open for 7% -> 4% of each run, Pallas kernels for 9% -> 12%
where the time goes in v4:
time: 90.8 us; the launch traced here: 90.5 us
  Pallas kernels  43.8 us (48%)
  starting transfers between devices  28.2 us (31%)
  waiting for transfers between devices  8.81 us (10%)
  local copies, waits for them, and re-layouts  5.13 us (6%)
  other arithmetic  2.83 us (3%)
  between operations  1.47 us (2%)
    ppermute x8, starting transfers between devices, shifted(): return lax.ppermute(value, AXES, moves)  18.2 us
    pallas_call x1, Pallas kernels, body(): pl.pallas_call(functools.partial(second_kernel, groups, halves, fast), ou...  16.9 us
    pallas_call x1, Pallas kernels, body(): pl.pallas_call(functools.partial(first_kernel, groups, halves), out_shape...  13 us
    ppermute x5, starting transfers between devices, total_of(): lax.ppermute(value, AXES, [(i, i ^ bit) for i in range(size)])  10.1 us
    pallas_call x1, Pallas kernels, body(): pl.pallas_call(functools.partial(merge_kernel, halves), out_shape=jax.Sha...  8.56 us
    ppermute x5, waiting for transfers between devices, total_of(): lax.ppermute(value, AXES, [(i, i ^ bit) for i in range(size)])  6.57 us
    unnamed x11, local copies, waits for them, and re-layouts  3.47 us
    pallas_call x1, Pallas kernels, body(): pl.pallas_call(functools.partial(pack_kernel, groups, block), out_shape=s...  2.99 us
  transfers between devices with their start and end apart: 13, of which 6 were waited for; matrix products, arithmetic and copies ran while one was open for 4% of the time, Pallas kernels for 12%

profile of v4, /device:TPU:0, one launch (start us, length us, event | category | flops | bytes accessed | tf_op | source)
XLA Modules:
  0.0 90.5 jit_solution(7033621154700014677)
XLA Ops:
  0.6 0.0 copy-start.3
  0.6 0.0 copy-start.4
  1.3 3.0 %pack.1 = (f32[7,8,2176]{2,1,0:T(8,128)}, f32[7,16,2176]{2,1,0:T(8,128)}, f32[7,8,2176]{2,1,0:T(8,128)}, f32[2,8,2176]{2,1,0:T(8,128)}, f32[2,16,2176]{2,1,0:T(8,128)}, /*index=5*/f32[2,8,2176]{2,1,0:T(8,128)}) custom-call(s32[1]{0:T(128)S(6)} %copy.12.step_ref, f32[1,2,16,4096]{3,2,1,0:T(8,128)} %state_ref.1, f32[16,4096]{1,0:T(8,128)} %vx.1, ...), custom_call_target="tpu_custom_call" | custom-call | tf_op jit(solution)/shard_map/pack/pallas_call | solution.py:559
  4.3 0.5 collective-permute-start
  4.8 5.0 %collective-permute-start.1 = (f32[7,8,2176]{2,1,0:T(8,128)}, f32[7,8,2176]{2,1,0:T(8,128)S(1)}, u32[]{:S(2)}, u32[]{:S(2)}) collective-permute-start(f32[7,8,2176]{2,1,0:T(8,128)} %get-tuple-element.18), channel_id=1, source_target_pairs={{0,30},{1,31},{2,0},{3,1},{4,2},{5,3},{6,4},{7,5},{8,6},{9,7},{10,... | collective-permute-start | bytes 1462280 | tf_op jit(solution)/shard_map/ppermute | solution.py:502
  9.8 2.0 %collective-permute-start.3 = (f32[2,16,2176]{2,1,0:T(8,128)}, f32[2,16,2176]{2,1,0:T(8,128)S(1)}, u32[]{:S(2)}, u32[]{:S(2)}) collective-permute-start(f32[2,16,2176]{2,1,0:T(8,128)} %get-tuple-element.20), channel_id=1, source_target_pairs={{0,1},{1,0},{2,3},{3,2},{4,5},{5,4},{6,7},{7,6},{8,9},{9,8},{10,11... | collective-permute-start | bytes 835592 | tf_op jit(solution)/shard_map/ppermute | solution.py:502
  11.7 0.0 collective-permute-start.2
  11.7 5.3 %collective-permute-start.4 = (f32[2,8,2176]{2,1,0:T(8,128)}, f32[2,8,2176]{2,1,0:T(8,128)S(1)}, u32[]{:S(2)}, u32[]{:S(2)}) collective-permute-start(f32[2,8,2176]{2,1,0:T(8,128)} %get-tuple-element.21), channel_id=1, source_target_pairs={{0,31},{1,30},{2,1},{3,0},{4,3},{5,2},{6,5},{7,4},{8,7},{9,6},{10,... | collective-permute-start | bytes 417800 | tf_op jit(solution)/shard_map/ppermute | solution.py:502
  17.1 0.9 dynamic-slice_bitcast_fusion.1
  18.0 2.2 %collective-permute-done.2.refs_3_ = f32[2,8,2176]{2,1,0:T(8,128)S(1)} collective-permute-done((f32[2,8,2176]{2,1,0:T(8,128)}, f32[2,8,2176]{2,1,0:T(8,128)S(1)}, u32[]{:S(2)}, u32[]{:S(2)}) %collective-permute-start.2) | collective-permute-done | bytes 139296 | tf_op jit(solution)/shard_map/ppermute | solution.py:502
  20.2 0.0 collective-permute-done.4.refs_5_
  20.2 0.0 collective-permute-done.3.refs_4_
  20.2 0.0 collective-permute-done.refs_0_
  20.2 0.0 collective-permute-done.1.refs_2_
  20.2 0.0 copy-start.2
  20.2 1.2 %copy-done.2 = f32[7,16,2176]{2,1,0:T(8,128)S(1)} copy-done((f32[7,16,2176]{2,1,0:T(8,128)S(1)}, f32[7,16,2176]{2,1,0:T(8,128)}, u32[]{:S(2)}) %copy-start.2) | copy-done | bytes 974872
  21.4 13.0 %first.1 = (f32[16,64,1024]{2,1,0:T(8,128)}, f32[8,32,8,1152]{3,2,1,0:T(8,128)}, f32[8,8,1152]{2,1,0:T(8,128)S(1)}, f32[16,8,1152]{2,1,0:T(8,128)S(1)}, f32[8,8,1152]{2,1,0:T(8,128)S(1)}) custom-call(f32[7,8,2176]{2,1,0:T(8,128)S(1)} %collective-permute-done.refs_0_, f32[7,16,2176]{2,1,0:T(8,128)S(1)} %copy-done.2, ...), custom_call_target="tpu_custom_call" | custom-call | tf_op jit(solution)/shard_map/first/pallas_call | solution.py:594
  34.5 4.8 %collective-permute-start.5 = (f32[8,8,1152]{2,1,0:T(8,128)S(1)}, f32[8,8,1152]{2,1,0:T(8,128)S(1)}, u32[]{:S(2)}, u32[]{:S(2)}) collective-permute-start(f32[8,8,1152]{2,1,0:T(8,128)S(1)} %get-tuple-element.22), channel_id=1, source_target_pairs={{0,2},{1,3},{2,4},{3,5},{4,6},{5,7},{6,8},{7,9},{8,10},{9,11},{10,... | collective-permute-start | bytes 884744 | tf_op jit(solution)/shard_map/ppermute | solution.py:502
  39.3 0.0 collective-permute-start.6
  39.3 0.0 copy-done.3
  39.3 0.0 copy-done.4
  39.3 0.2 convolution_bitcast_fusion.refs_1_
  39.6 0.0 copy-start
  39.6 2.2 %copy-done = f32[16,64,1024]{2,1,0:T(8,128)S(1)} copy-done((f32[16,64,1024]{2,1,0:T(8,128)S(1)}, f32[16,64,1024]{2,1,0:T(8,128)}, u32[]{:S(2)}) %copy-start) | copy-done | bytes 4194328
  41.8 2.3 %gram.1.refs_0_ = f32[64,64]{1,0:T(8,128)S(1)} custom-call(f32[16,64,1024]{2,1,0:T(8,128)S(1)} %copy-done), custom_call_target="tpu_custom_call" | custom-call | flops 536870912 | bytes 4194304 | tf_op jit(solution)/shard_map/gram/pallas_call | solution.py:614
  44.1 0.0 collective-permute-done.5.left_halo
  44.1 0.0 collective-permute-done.6.right_halo
  44.1 16.9 %second.1 = (f32[16,64,1024]{2,1,0:T(8,128)}, f32[2,2,16,2048]{3,2,1,0:T(8,128)S(1)}, f32[32,64]{1,0:T(8,128)S(1)}) custom-call(f32[8,8,1152]{2,1,0:T(8,128)S(1)} %collective-permute-done.5.left_halo, f32[16,8,1152]{2,1,0:T(8,128)S(1)} %get-tuple-element.23.own, f32[8,8,1152]{2,1,0:T(8,128)S(1)} %collective-permute-done.6.right_halo, ...), custom_call_target="tpu_custom_call" | custom-call | tf_op jit(solution)/shard_map/second/pallas_call | solution.py:625
  61.0 1.2 %collective-permute-start.7 = (f32[32,64]{1,0:T(8,128)S(1)}, f32[32,64]{1,0:T(8,128)S(1)}, u32[]{:S(2)}, u32[]{:S(2)}) collective-permute-start(f32[32,64]{1,0:T(8,128)S(1)} %get-tuple-element.27), channel_id=1, source_target_pairs={{0,1},{1,0},{2,3},{3,2},{4,5},{5,4},{6,7},{7,6},{8,9},{9,8},{10,11... | collective-permute-start | bytes 24584 | tf_op jit(solution)/shard_map/ppermute | solution.py:515
  62.2 0.1 copy.11
  62.3 0.1 pad.7.clone
  62.4 2.4 %collective-permute-done.7 = f32[32,64]{1,0:T(8,128)S(1)} collective-permute-done((f32[32,64]{1,0:T(8,128)S(1)}, f32[32,64]{1,0:T(8,128)S(1)}, u32[]{:S(2)}, u32[]{:S(2)}) %collective-permute-start.7) | collective-permute-done | bytes 8224 | tf_op jit(solution)/shard_map/ppermute | solution.py:515
  64.8 1.1 %collective-permute-start.8 = (f32[32,64]{1,0:T(8,128)S(1)}, f32[32,64]{1,0:T(8,128)S(1)}, u32[]{:S(2)}, u32[]{:S(2)}) collective-permute-start(f32[32,64]{1,0:T(8,128)S(1)} %add.33), channel_id=1, source_target_pairs={{0,2},{1,3},{2,0},{3,1},{4,6},{5,7},{6,4},{7,5},{8,10},{9,11},{10,... | collective-permute-start | bytes 24584 | tf_op jit(solution)/shard_map/ppermute | solution.py:515
  65.9 0.7 maximum_maximum_fusion.spread_ref
  66.6 0.2 collective-permute-done.8
  66.7 3.6 %collective-permute-start.9 = (f32[32,64]{1,0:T(8,128)S(1)}, f32[32,64]{1,0:T(8,128)S(1)}, u32[]{:S(2)}, u32[]{:S(2)}) collective-permute-start(f32[32,64]{1,0:T(8,128)S(1)} %add.34), channel_id=1, source_target_pairs={{0,4},{1,5},{2,6},{3,7},{4,0},{5,1},{6,2},{7,3},{8,12},{9,13},{10,... | collective-permute-start | bytes 24584 | tf_op jit(solution)/shard_map/ppermute | solution.py:515
  70.4 0.6 collective-permute-start.12
  71.0 1.1 %collective-permute-done.9 = f32[32,64]{1,0:T(8,128)S(1)} collective-permute-done((f32[32,64]{1,0:T(8,128)S(1)}, f32[32,64]{1,0:T(8,128)S(1)}, u32[]{:S(2)}, u32[]{:S(2)}) %collective-permute-start.9) | collective-permute-done | bytes 8224 | tf_op jit(solution)/shard_map/ppermute | solution.py:515
  72.1 1.6 %collective-permute-start.10 = (f32[32,64]{1,0:T(8,128)S(1)}, f32[32,64]{1,0:T(8,128)S(1)}, u32[]{:S(2)}, u32[]{:S(2)}) collective-permute-start(f32[32,64]{1,0:T(8,128)S(1)} %add.35), channel_id=1, source_target_pairs={{0,8},{1,9},{2,10},{3,11},{4,12},{5,13},{6,14},{7,15},{8,0},{9,1},... | collective-permute-start | bytes 24584 | tf_op jit(solution)/shard_map/ppermute | solution.py:515
  73.7 2.2 %collective-permute-done.10 = f32[32,64]{1,0:T(8,128)S(1)} collective-permute-done((f32[32,64]{1,0:T(8,128)S(1)}, f32[32,64]{1,0:T(8,128)S(1)}, u32[]{:S(2)}, u32[]{:S(2)}) %collective-permute-start.10) | collective-permute-done | bytes 8224 | tf_op jit(solution)/shard_map/ppermute | solution.py:515
  75.8 2.6 %collective-permute-start.11 = (f32[32,64]{1,0:T(8,128)S(1)}, f32[32,64]{1,0:T(8,128)S(1)}, u32[]{:S(2)}, u32[]{:S(2)}) collective-permute-start(f32[32,64]{1,0:T(8,128)S(1)} %add.36), channel_id=1, source_target_pairs={{0,16},{1,17},{2,18},{3,19},{4,20},{5,21},{6,22},{7,23},{8,24},{9,... | collective-permute-start | bytes 24584 | tf_op jit(solution)/shard_map/ppermute | solution.py:515
  78.4 0.7 fusion.4.unit_ref
  79.1 0.7 concatenate.33.expand_ref
  79.8 0.7 collective-permute-done.11
  80.5 0.6 add.37.left_ref
  81.1 8.6 %merge.1 = f32[32,16,2048]{2,1,0:T(8,128)} custom-call(f32[32,64]{1,0:T(8,128)} %add.37.left_ref, f32[64,128]{1,0:T(8,128)} %maximum_maximum_fusion.spread_ref, f32[32,128]{1,0:T(8,128)} %fusion.4.unit_ref, f32[128,256]{1,0:T(8,128)} %concatenate.33.expand_ref, f32[16,64,1024]{2,1,0:T(8,128)} %get-tuple-element.26.snap_ref.earlier_ref.early_ref, ...), custom_call_target="tpu_custom_call" | custom-call | tf_op jit(solution)/shard_map/merge/pallas_call | solution.py:639
  89.6 0.0 collective-permute-done.12
  89.6 0.8 maximum_select_fusion
  (11 shorter events, 0.1 us)
Async XLA Ops:
  0.6 38.7 %copy-start.3 = (f32[2,2,64,128]{2,3,1,0:T(8,128)S(1)}, f32[2,2,64,128]{2,3,1,0:T(8,128)}, u32[]{:S(2)}) copy-start(f32[2,2,64,128]{2,3,1,0:T(8,128)} %constant.18.clone) | copy-start | bytes 393220
  0.6 38.7 %copy-start.4 = (f32[64,32]{0,1:T(8,128)S(1)}, f32[64,32]{0,1:T(8,128)}, u32[]{:S(2)}) copy-start(f32[64,32]{0,1:T(8,128)} %param.16) | copy-start | bytes 24580
  4.3 15.9 %collective-permute-start = (f32[7,8,2176]{2,1,0:T(8,128)}, f32[7,8,2176]{2,1,0:T(8,128)S(1)}, u32[]{:S(2)}, u32[]{:S(2)}) collective-permute-start(f32[7,8,2176]{2,1,0:T(8,128)} %get-tuple-element.16), channel_id=1, source_target_pairs={{0,2},{1,3},{2,4},{3,5},{4,6},{5,7},{6,8},{7,9},{8,10},{9,11},{10,... | collective-permute-start | bytes 1462280 | tf_op jit(solution)/shard_map/ppermute | solution.py:502
  4.8 15.4 %collective-permute-start.1 = (f32[7,8,2176]{2,1,0:T(8,128)}, f32[7,8,2176]{2,1,0:T(8,128)S(1)}, u32[]{:S(2)}, u32[]{:S(2)}) collective-permute-start(f32[7,8,2176]{2,1,0:T(8,128)} %get-tuple-element.18), channel_id=1, source_target_pairs={{0,30},{1,31},{2,0},{3,1},{4,2},{5,3},{6,4},{7,5},{8,6},{9,7},{10,... | collective-permute-start | bytes 1462280 | tf_op jit(solution)/shard_map/ppermute | solution.py:502
  9.8 10.4 %collective-permute-start.3 = (f32[2,16,2176]{2,1,0:T(8,128)}, f32[2,16,2176]{2,1,0:T(8,128)S(1)}, u32[]{:S(2)}, u32[]{:S(2)}) collective-permute-start(f32[2,16,2176]{2,1,0:T(8,128)} %get-tuple-element.20), channel_id=1, source_target_pairs={{0,1},{1,0},{2,3},{3,2},{4,5},{5,4},{6,7},{7,6},{8,9},{9,8},{10,11... | collective-permute-start | bytes 835592 | tf_op jit(solution)/shard_map/ppermute | solution.py:502
  11.7 8.4 %collective-permute-start.2 = (f32[2,8,2176]{2,1,0:T(8,128)}, f32[2,8,2176]{2,1,0:T(8,128)S(1)}, u32[]{:S(2)}, u32[]{:S(2)}) collective-permute-start(f32[2,8,2176]{2,1,0:T(8,128)} %get-tuple-element.19), channel_id=1, source_target_pairs={{0,3},{1,2},{2,5},{3,4},{4,7},{5,6},{6,9},{7,8},{8,11},{9,10},{10,... | collective-permute-start | bytes 417800 | tf_op jit(solution)/shard_map/ppermute | solution.py:502
  11.7 8.4 %collective-permute-start.4 = (f32[2,8,2176]{2,1,0:T(8,128)}, f32[2,8,2176]{2,1,0:T(8,128)S(1)}, u32[]{:S(2)}, u32[]{:S(2)}) collective-permute-start(f32[2,8,2176]{2,1,0:T(8,128)} %get-tuple-element.21), channel_id=1, source_target_pairs={{0,31},{1,30},{2,1},{3,0},{4,3},{5,2},{6,5},{7,4},{8,7},{9,6},{10,... | collective-permute-start | bytes 417800 | tf_op jit(solution)/shard_map/ppermute | solution.py:502
  20.2 1.2 %copy-start.2 = (f32[7,16,2176]{2,1,0:T(8,128)S(1)}, f32[7,16,2176]{2,1,0:T(8,128)}, u32[]{:S(2)}) copy-start(f32[7,16,2176]{2,1,0:T(8,128)} %get-tuple-element.17.refs_1_) | copy-start | bytes 2924548
  34.5 9.7 %collective-permute-start.5 = (f32[8,8,1152]{2,1,0:T(8,128)S(1)}, f32[8,8,1152]{2,1,0:T(8,128)S(1)}, u32[]{:S(2)}, u32[]{:S(2)}) collective-permute-start(f32[8,8,1152]{2,1,0:T(8,128)S(1)} %get-tuple-element.22), channel_id=1, source_target_pairs={{0,2},{1,3},{2,4},{3,5},{4,6},{5,7},{6,8},{7,9},{8,10},{9,11},{10,... | collective-permute-start | bytes 884744 | tf_op jit(solution)/shard_map/ppermute | solution.py:502
  39.3 4.8 %collective-permute-start.6 = (f32[8,8,1152]{2,1,0:T(8,128)S(1)}, f32[8,8,1152]{2,1,0:T(8,128)S(1)}, u32[]{:S(2)}, u32[]{:S(2)}) collective-permute-start(f32[8,8,1152]{2,1,0:T(8,128)S(1)} %get-tuple-element.24), channel_id=1, source_target_pairs={{0,30},{1,31},{2,0},{3,1},{4,2},{5,3},{6,4},{7,5},{8,6},{9,7},{10,... | collective-permute-start | bytes 884744 | tf_op jit(solution)/shard_map/ppermute | solution.py:502
  39.6 2.2 %copy-start = (f32[16,64,1024]{2,1,0:T(8,128)S(1)}, f32[16,64,1024]{2,1,0:T(8,128)}, u32[]{:S(2)}) copy-start(f32[16,64,1024]{2,1,0:T(8,128)} %get-tuple-element.26.snap_ref.earlier_ref.early_ref) | copy-start | bytes 12582916
  41.8 2.4 %copy-start.1 = (f32[16,64,1024]{2,1,0:T(8,128)S(1)}, f32[16,64,1024]{2,1,0:T(8,128)}, u32[]{:S(2)}) copy-start(f32[16,64,1024]{2,1,0:T(8,128)} %get-tuple-element.26.snap_ref.earlier_ref.early_ref) | copy-start | bytes 12582916
  61.0 3.8 %collective-permute-start.7 = (f32[32,64]{1,0:T(8,128)S(1)}, f32[32,64]{1,0:T(8,128)S(1)}, u32[]{:S(2)}, u32[]{:S(2)}) collective-permute-start(f32[32,64]{1,0:T(8,128)S(1)} %get-tuple-element.27), channel_id=1, source_target_pairs={{0,1},{1,0},{2,3},{3,2},{4,5},{5,4},{6,7},{7,6},{8,9},{9,8},{10,11... | collective-permute-start | bytes 24584 | tf_op jit(solution)/shard_map/ppermute | solution.py:515
  64.8 1.9 %collective-permute-start.8 = (f32[32,64]{1,0:T(8,128)S(1)}, f32[32,64]{1,0:T(8,128)S(1)}, u32[]{:S(2)}, u32[]{:S(2)}) collective-permute-start(f32[32,64]{1,0:T(8,128)S(1)} %add.33), channel_id=1, source_target_pairs={{0,2},{1,3},{2,0},{3,1},{4,6},{5,7},{6,4},{7,5},{8,10},{9,11},{10,... | collective-permute-start | bytes 24584 | tf_op jit(solution)/shard_map/ppermute | solution.py:515
  66.7 5.4 %collective-permute-start.9 = (f32[32,64]{1,0:T(8,128)S(1)}, f32[32,64]{1,0:T(8,128)S(1)}, u32[]{:S(2)}, u32[]{:S(2)}) collective-permute-start(f32[32,64]{1,0:T(8,128)S(1)} %add.34), channel_id=1, source_target_pairs={{0,4},{1,5},{2,6},{3,7},{4,0},{5,1},{6,2},{7,3},{8,12},{9,13},{10,... | collective-permute-start | bytes 24584 | tf_op jit(solution)/shard_map/ppermute | solution.py:515
  70.4 19.2 %collective-permute-start.12 = (f32[2,16,2048]{2,1,0:T(8,128)S(1)}, f32[2,16,2048]{2,1,0:T(8,128)S(1)}, u32[]{:S(2)}, u32[]{:S(2)}) collective-permute-start(f32[2,16,2048]{2,1,0:T(8,128)S(1)} %get-tuple-element.31), channel_id=1, source_target_pairs={{0,1},{1,0},{2,3},{3,2},{4,5},{5,4},{6,7},{7,6},{8,9},{9,8},{10,11... | collective-permute-start | bytes 786440 | tf_op jit(solution)/shard_map/ppermute | solution.py:502
  72.1 3.7 %collective-permute-start.10 = (f32[32,64]{1,0:T(8,128)S(1)}, f32[32,64]{1,0:T(8,128)S(1)}, u32[]{:S(2)}, u32[]{:S(2)}) collective-permute-start(f32[32,64]{1,0:T(8,128)S(1)} %add.35), channel_id=1, source_target_pairs={{0,8},{1,9},{2,10},{3,11},{4,12},{5,13},{6,14},{7,15},{8,0},{9,1},... | collective-permute-start | bytes 24584 | tf_op jit(solution)/shard_map/ppermute | solution.py:515
  75.8 4.6 %collective-permute-start.11 = (f32[32,64]{1,0:T(8,128)S(1)}, f32[32,64]{1,0:T(8,128)S(1)}, u32[]{:S(2)}, u32[]{:S(2)}) collective-permute-start(f32[32,64]{1,0:T(8,128)S(1)} %add.36), channel_id=1, source_target_pairs={{0,16},{1,17},{2,18},{3,19},{4,20},{5,21},{6,22},{7,23},{8,24},{9,... | collective-permute-start | bytes 24584 | tf_op jit(solution)/shard_map/ppermute | solution.py:515

commit v5 on v4

--- a/solution.py
+++ b/solution.py
@@ -18,6 +18,7 @@
 OWN = 8
 REACH = STEPS // 2
 VMEM = pl.BlockSpec(memory_space=pltpu.VMEM)
+ANY = pl.BlockSpec(memory_space=pl.ANY)
 HBM = pl.BlockSpec(memory_space=pltpu.HBM)
 SMEM = pl.BlockSpec(memory_space=pltpu.SMEM)
 
@@ -36,7 +37,12 @@
     return lax.broadcasted_iota(jnp.int32, shape, len(shape) - 1)
 
 
-def pack_kernel(groups, block, step_ref, state_ref, vx, vy, amp, freq, phase, *out_refs):
+def pack_kernel(groups, block, step_ref, *refs):
+    out_refs, scratch, sems = refs[6:-7], refs[-7:-1], refs[-1]
+    brought = [pltpu.make_async_copy(refs[i], scratch[i], sems.at[i]) for i in range(6)]
+    for copy in brought:
+        copy.start()
+    state_ref, vx, vy, amp, freq, phase = scratch
     full = vx.shape[1]
     me = lax.axis_index("tm")
     start = step_ref[0].astype(jnp.float32)
@@ -68,7 +74,9 @@
         return write
 
     for index, ref in enumerate((vx, vy, amp, freq, phase)):
+        brought[1 + index].wait()
         cut(lambda columns, ref=ref: ref[:, columns], me, writer(0, index), False)
+    brought[0].wait()
     for shift in range(groups):
         target = lax.rem(me + shift, groups)
         for field in range(2):
@@ -204,8 +212,9 @@
     sources = [refs[3 * i : 3 * i + 3] for i in range(groups)]
     snap_ref, carry_ref, low_ref, own_ref, high_ref = refs[3 * groups : 3 * groups + 5]
     refs = refs[3 * groups + 5 :]
-    grid, (snap, sems, carry_sems) = refs[:10], refs[10:]
-    qa, qb, xa, xb, twice, cw, ce, cs, cn, c0 = grid
+    qa, qb, snap, sems = refs
+    xa, xb, twice, cw, ce, cs, cn, c0 = (carry_ref.at[i] for i in range(8))
+    grid = (qa, qb, xa, xb, twice, cw, ce, cs, cn, c0)
     rows = sources[0][1].shape[1]
     block = sources[0][1].shape[2] - TILE
     length = block // halves
@@ -295,20 +304,11 @@
 
         lax.fori_loop(0, count // 8, by_rows, 0)
 
-    def keep(i):
-        return pltpu.make_async_copy(grid[2 + i], carry_ref.at[i], carry_sems.at[i])
-
-    for i in range(2, 8):
-        keep(i).start()
     drain = run_phase(grid, rows, snap, snap_ref, sems, True)
-    for i in range(2):
-        keep(i).start()
     low_ref[...] = qa[GUARD + REACH : GUARD + 2 * REACH]
     own_ref[...] = qa[GUARD + REACH : GUARD + REACH + rows]
     high_ref[...] = qa[GUARD + rows : GUARD + rows + REACH]
     drain()
-    for i in range(8):
-        keep(i).wait()
 
 
 def split_rows(a):
@@ -325,48 +325,46 @@
     return (g[:m, :n] + g[m:, n:]) + (g[:m, n:] + g[m:, :n])
 
 
-def gram_kernel(snap_ref, gram_ref):
-    width = snap_ref.shape[1]
-
-    @pl.when(pl.program_id(0) == 0)
-    def _():
-        gram_ref[...] = jnp.zeros_like(gram_ref)
-
+def gram_kernel(snap_ref, gram_ref, snap, sems):
+    rows, width, _ = snap.shape
+    parts = sems.shape[0]
+    depth = rows // parts
+
+    def fetch(i):
+        at = pl.ds(i * depth, depth)
+        return pltpu.make_async_copy(snap_ref.at[at], snap.at[at], sems.at[i])
+
+    for i in range(parts):
+        fetch(i).start()
     total = jnp.zeros((2 * width, 2 * width), jnp.float32)
-    for x in range(snap_ref.shape[0]):
-        both = split_rows(snap_ref[x])
-        total = total + outer_of(both, both)
-    gram_ref[...] += joined(total)
-
-
-def second_kernel(groups, halves, with_left, left_halo, own, right_halo, carry_ref, earlier_ref, *refs):
+    for i in range(parts):
+        fetch(i).wait()
+        for x in range(i * depth, (i + 1) * depth):
+            both = split_rows(snap[x])
+            total = total + outer_of(both, both)
+    gram_ref[...] = joined(total)
+
+
+def second_kernel(groups, halves, with_left, left_halo, own, right_halo, carry_ref, earlier, *refs):
     if with_left:
         gram_ref, select_ref, fold_ref = refs[:3]
         refs = refs[3:]
-        snap_ref, end_ref, left_ref = refs[:3]
+        snap_ref, kept_ref, sent_ref, left_ref = refs[:4]
+        refs = refs[4:]
+    else:
+        snap_ref, kept_ref, sent_ref = refs[:3]
         refs = refs[3:]
-    else:
-        snap_ref, end_ref = refs[:2]
-        refs = refs[2:]
-    grid, (snap, earlier, sems, carry_sems, more_sems) = refs[:10], refs[10:]
-    qa = grid[0]
+    qa, qb, xa, xb, snap, sems = refs
+    grid = [qa, qb, xa, xb] + [carry_ref.at[i] for i in range(2, 8)]
     rows, width, length = snap.shape
     subs = qa.shape[1]
     tiles = length // TILE + 1
 
-    def bring(i):
-        return pltpu.make_async_copy(carry_ref.at[i], grid[2 + i], carry_sems.at[i])
-
-    late = pltpu.make_async_copy(earlier_ref, earlier, more_sems.at[0])
-    for i in range(8):
-        bring(i).start()
-    if with_left:
-        late.start()
+    xa[...] = carry_ref[0]
+    xb[...] = carry_ref[1]
     qa[GUARD : GUARD + REACH] = left_halo[...]
     qa[GUARD + REACH : GUARD + REACH + rows] = own[...]
     qa[GUARD + REACH + rows : GUARD + 2 * REACH + rows] = right_halo[...]
-    for i in range(8):
-        bring(i).wait()
     drain = run_phase(grid, rows, snap, snap_ref, sems, False)
 
     for base in range(0, rows, 8):
@@ -376,13 +374,10 @@
             for half in range(halves):
                 for group in range(groups):
                     for field in range(2):
-                        end_ref[
-                            group, field, base : base + 8, half * length + t * TILE : half * length + (t + 1) * TILE
-                        ] = value[half * groups * 2 + group * 2 + field]
+                        end_ref = kept_ref if group == 0 else sent_ref.at[group - 1]
+                        end_ref[field, base : base + 8, half * length + t * TILE : half * length + (t + 1) * TILE] = value[half * groups * 2 + group * 2 + field]
 
     if with_left:
-        late.wait()
-
         def add(x, total):
             now = split_rows(snap[x])
             every = jnp.concatenate([now, split_rows(earlier[x])], axis=0)
@@ -434,7 +429,33 @@
 CHUNK = 256
 
 
-def merge_kernel(halves, left_ref, spread_ref, unit_ref, expand_ref, early_ref, late_ref, out_ref, snap, out, arrived, left_sems):
+def merge_kernel(
+    halves,
+    left_ref,
+    other_ref,
+    spread_ref,
+    unit_ref,
+    expand_ref,
+    kept_ref,
+    came_ref,
+    early_ref,
+    late_ref,
+    out_ref,
+    end_ref,
+    snap,
+    out,
+    arrived,
+    left_sems,
+    end_sems,
+):
+    me = lax.axis_index("tm")
+    block = kept_ref.shape[2]
+    ends = [
+        pltpu.make_async_copy(
+            ref, end_ref.at[:, :, pl.ds(pl.multiple_of(member * block, TILE), block)], end_sems.at[i]
+        )
+        for i, (ref, member) in enumerate(((kept_ref, me), (came_ref, 1 - me)))
+    ]
     rank = left_ref.shape[0]
     wide = left_ref.shape[1]
     rows, width, length = snap.shape
@@ -453,8 +474,10 @@
     for i in range(parts):
         fetch(i, 0).start()
         fetch(i, 1).start()
+    for copy in ends:
+        copy.start()
     lane = lanes_of((rank, 128))
-    whole = eliminate(mm(left_ref[...], spread_ref[...]) + unit_ref[...], rank)
+    whole = eliminate(mm(left_ref[...] + other_ref[...], spread_ref[...]) + unit_ref[...], rank)
     proj = jnp.where((lane >= rank) & (lane < rank + wide), whole, 0.0)
     outer = mm_nt(proj, proj)
     factor = eliminate(outer, rank)
@@ -490,6 +513,8 @@
     for i in range(parts):
         for half in range(halves):
             store(i, half).wait()
+    for copy in ends:
+        copy.wait()
 
 
 def shifted(value, along_space, along_tm):
@@ -502,6 +527,10 @@
     return lax.ppermute(value, AXES, moves)
 
 
+def in_hbm(value):
+    return pltpu.with_memory_space_constraint(value, pltpu.HBM)
+
+
 def turn(value, start):
     return lax.dynamic_slice_in_dim(jnp.concatenate([value, value]), start, value.shape[0], 0)
 
@@ -509,12 +538,14 @@
 def total_of(value):
     size = lax.axis_size("space") * lax.axis_size("tm")
     if size & (size - 1):
-        return lax.psum(value, AXES)
+        return lax.psum(value, AXES), jnp.zeros_like(value)
+    other = jnp.zeros_like(value)
     bit = 1
     while bit < size:
-        value = value + lax.ppermute(value, AXES, [(i, i ^ bit) for i in range(size)])
+        value = value if bit == 1 else value + other
+        other = lax.ppermute(value, AXES, [(i, i ^ bit) for i in range(size)])
         bit *= 2
-    return value
+    return value, other
 
 
 def coefficients(gram, sketch):
@@ -559,10 +590,14 @@
     packed = pl.pallas_call(
         functools.partial(pack_kernel, groups, block),
         out_shape=shapes,
-        in_specs=[SMEM] + [VMEM] * 6,
+        in_specs=[SMEM] + [HBM] * 6,
         out_specs=[VMEM] * len(shapes),
+        scratch_shapes=[pltpu.VMEM(start_state.shape, f32)]
+        + [pltpu.VMEM((rows, full), f32)] * 5
+        + [pltpu.SemaphoreType.DMA((6,))],
+        compiler_params=pltpu.CompilerParams(vmem_limit_bytes=16 * 2**20),
         name="pack",
-    )(start_step, start_state, velocity_x, velocity_y, amplitude, frequency, phase)
+    )(start_step, *map(in_hbm, (start_state, velocity_x, velocity_y, amplitude, frequency, phase)))
     sources = [shifted(packed[2], 1, 0), packed[1], shifted(packed[0], -1, 0)]
     for shift in range(1, groups):
         low, every, high = packed[3 * shift : 3 * shift + 3]
@@ -589,85 +624,83 @@
         expand = jnp.concatenate([jnp.zeros((128 - rank, halves * width), f32), select], axis=0)
         extra = [select, fold]
 
-    grid = [pltpu.VMEM((total + 2 * GUARD, subs, span), f32)] * 2 + [pltpu.VMEM((total, subs, span), f32)] * 8
+    grid = [pltpu.VMEM((total + 2 * GUARD, subs, span), f32)] * 2 + [pltpu.VMEM((total, subs, span), f32)] * 2
     half_snap = (rows, width // 2, length)
     early, carry, low, own, high = pl.pallas_call(
         functools.partial(first_kernel, groups, halves),
         out_shape=[
             pltpu.HBM(half_snap, f32),
-            pltpu.HBM((8, total, subs, span), f32),
+            jax.ShapeDtypeStruct((8, total, subs, span), f32),
             jax.ShapeDtypeStruct((REACH, subs, span), f32),
             jax.ShapeDtypeStruct((rows, subs, span), f32),
             jax.ShapeDtypeStruct((REACH, subs, span), f32),
         ],
         in_specs=[VMEM] * len(sources),
-        out_specs=[HBM] * 2 + [VMEM] * 3,
-        scratch_shapes=grid
-        + [pltpu.VMEM(half_snap, f32), pltpu.SemaphoreType.DMA((REACH,)), pltpu.SemaphoreType.DMA((8,))],
-        compiler_params=pltpu.CompilerParams(vmem_limit_bytes=36 * 2**20),
+        out_specs=[HBM] + [VMEM] * 4,
+        scratch_shapes=grid[:2] + [pltpu.VMEM(half_snap, f32), pltpu.SemaphoreType.DMA((REACH,))],
+        compiler_params=pltpu.CompilerParams(vmem_limit_bytes=28 * 2**20),
         name="first",
     )(*sources)
     beside = [shifted(high, 1, 0), own, shifted(low, -1, 0)]
-    outs = [pltpu.HBM(half_snap, f32), jax.ShapeDtypeStruct((groups, 2, rows, block), f32)]
+    outs = [
+        pltpu.HBM(half_snap, f32),
+        jax.ShapeDtypeStruct((2, rows, block), f32),
+        jax.ShapeDtypeStruct((groups - 1, 2, rows, block), f32),
+    ]
     if fast:
         outs.append(jax.ShapeDtypeStruct((sketch.shape[1], sketch.shape[0]), f32))
         gram = pl.pallas_call(
             gram_kernel,
             out_shape=jax.ShapeDtypeStruct((width // 2, width // 2), f32),
-            grid=(4,),
-            in_specs=[pl.BlockSpec((rows // 4, width // 2, length), lambda i: (i, 0, 0))],
-            out_specs=pl.BlockSpec((width // 2, width // 2), lambda i: (0, 0)),
+            in_specs=[HBM],
+            out_specs=VMEM,
+            scratch_shapes=[pltpu.VMEM(half_snap, f32), pltpu.SemaphoreType.DMA((4,))],
             cost_estimate=pl.CostEstimate(flops=2 * rows * width * width * length, bytes_accessed=2 * rows * width * length, transcendentals=0),
-            compiler_params=pltpu.CompilerParams(vmem_limit_bytes=16 * 2**20),
+            compiler_params=pltpu.CompilerParams(vmem_limit_bytes=12 * 2**20),
             name="gram",
-        )(early)
+        )(in_hbm(early))
         extra = [gram] + extra
     made = pl.pallas_call(
         functools.partial(second_kernel, groups, halves, fast),
         out_shape=outs,
-        in_specs=[VMEM] * 3 + [HBM] * 2 + [VMEM] * len(extra),
+        in_specs=[VMEM] * (5 + len(extra)),
         out_specs=[HBM] + [VMEM] * (len(outs) - 1),
-        scratch_shapes=grid
-        + [pltpu.VMEM(half_snap, f32)] * 2
-        + [pltpu.SemaphoreType.DMA((REACH,)), pltpu.SemaphoreType.DMA((8,)), pltpu.SemaphoreType.DMA((1,))],
-        compiler_params=pltpu.CompilerParams(vmem_limit_bytes=40 * 2**20),
+        scratch_shapes=grid[:4] + [pltpu.VMEM(half_snap, f32), pltpu.SemaphoreType.DMA((REACH,))],
+        compiler_params=pltpu.CompilerParams(vmem_limit_bytes=32 * 2**20),
         name="second",
     )(*beside, carry, early, *extra)
 
+    ends = [made[1]]
+    for shift in range(1, groups):
+        ends.append(shifted(made[2][shift - 1], 0, groups - shift))
     if fast:
-        left = total_of(made[2])
-        piece = pl.pallas_call(
+        left, other = total_of(made[3])
+        piece, end_state = pl.pallas_call(
             functools.partial(merge_kernel, halves),
-            out_shape=jax.ShapeDtypeStruct((rank, rows, block), f32),
-            in_specs=[VMEM] * 4 + [HBM] * 2,
-            out_specs=HBM,
+            out_shape=[
+                jax.ShapeDtypeStruct((rank, rows, block), f32),
+                jax.ShapeDtypeStruct((2, rows, full), f32),
+            ],
+            in_specs=[VMEM] * 5 + [ANY] * 2 + [HBM] * 2,
+            out_specs=[HBM] * 2,
             scratch_shapes=[
                 pltpu.VMEM((rows, width, length), f32),
                 pltpu.VMEM((rank, rows, block), f32),
                 pltpu.SemaphoreType.DMA((length // CHUNK, 2)),
                 pltpu.SemaphoreType.DMA((length // CHUNK, halves)),
+                pltpu.SemaphoreType.DMA((2,)),
             ],
-            compiler_params=pltpu.CompilerParams(vmem_limit_bytes=54 * 2**20),
+            compiler_params=pltpu.CompilerParams(vmem_limit_bytes=28 * 2**20),
             name="merge",
-        )(left, spread, unit, expand, early, made[0])
-    else:
-        snaps = jnp.concatenate([early, made[0]], axis=1).reshape(rows, STEPS, halves, groups, 2, length)
-        snaps = jnp.transpose(snaps, (3, 4, 1, 0, 2, 5)).reshape(groups, 2 * STEPS, rows, block)
-        snaps = turn(jnp.flip(snaps, 0), groups - 1 - me)
-        piece = merge_levels(snaps, sketch)
-
-    ends = [made[1][0]]
-    for shift in range(1, groups):
-        ends.append(shifted(made[1][shift], 0, groups - shift))
-    if groups == 2:
-        end_state = jnp.where(
-            me == 0,
-            jnp.concatenate([ends[0], ends[1]], axis=-1),
-            jnp.concatenate([ends[1], ends[0]], axis=-1),
-        )
-    else:
-        stacked = turn(jnp.stack(ends), groups - me)
-        end_state = jnp.moveaxis(stacked, 0, -2).reshape(2, rows, full)
+        )(left, other, spread, unit, expand, ends[0], ends[1], in_hbm(early), in_hbm(made[0]))
+        return (piece, end_state[None])
+
+    snaps = jnp.concatenate([early, made[0]], axis=1).reshape(rows, STEPS, halves, groups, 2, length)
+    snaps = jnp.transpose(snaps, (3, 4, 1, 0, 2, 5)).reshape(groups, 2 * STEPS, rows, block)
+    snaps = turn(jnp.flip(snaps, 0), groups - 1 - me)
+    piece = merge_levels(snaps, sketch)
+    stacked = turn(jnp.stack(ends), groups - me)
+    end_state = jnp.moveaxis(stacked, 0, -2).reshape(2, rows, full)
     return (piece, end_state[None])
 
 

time: 90.8 us -> 81.9 us (0.902)
  Pallas kernels: 43.8 us -> 39.6 us
  local copies, waits for them, and re-layouts: 5.13 us -> 1.06 us
  other arithmetic: 2.83 us -> 1.06 us
  waiting for transfers between devices: 8.81 us -> 10.5 us
    pallas_call x1, Pallas kernels: 16.9 us -> 13.3 us  [body(): pl.pallas_call(functools.partial(second_kernel, groups, halves, fast), ou...]
    unnamed x11 -> x5, local copies, waits for them, and re-layouts: 3.47 us -> 0.09 us
    pallas_call x1, Pallas kernels: 2.34 us -> 4.15 us  [body(): pl.pallas_call(gram_kernel, out_shape=jax.ShapeDtypeStruct((width // 2, w...]
    ppermute x5, waiting for transfers between devices: 6.57 us -> 8.26 us  [total_of(): other = lax.ppermute(value, AXES, [(i, i ^ bit) for i in range(size)])]
    pallas_call x1, Pallas kernels: 8.56 us -> 7.63 us  [body(): pl.pallas_call(functools.partial(merge_kernel, halves), out_shape=[jax.Sh...]
  transfers between devices with their start and end apart: 13 -> 13, of which waited for: 6 -> 6; matrix products, arithmetic and copies ran while one was open for 4% -> 3% of each run, Pallas kernels for 12% -> 5%
where the time goes in v5:
time: 81.9 us; the launch traced here: 81.6 us
  Pallas kernels  39.6 us (48%)
  starting transfers between devices  27.8 us (34%)
  waiting for transfers between devices  10.5 us (13%)
  between operations  1.42 us (2%)
  local copies, waits for them, and re-layouts  1.06 us (1%)
  other arithmetic  1.06 us (1%)
    ppermute x8, starting transfers between devices, shifted(): return lax.ppermute(value, AXES, moves)  18 us
    pallas_call x1, Pallas kernels, body(): pl.pallas_call(functools.partial(second_kernel, groups, halves, fast), ou...  13.3 us
    pallas_call x1, Pallas kernels, body(): pl.pallas_call(functools.partial(first_kernel, groups, halves), out_shape...  12.2 us
    ppermute x5, starting transfers between devices, total_of(): other = lax.ppermute(value, AXES, [(i, i ^ bit) for i in range(size)])  9.8 us
    ppermute x5, waiting for transfers between devices, total_of(): other = lax.ppermute(value, AXES, [(i, i ^ bit) for i in range(size)])  8.26 us
    pallas_call x1, Pallas kernels, body(): pl.pallas_call(functools.partial(merge_kernel, halves), out_shape=[jax.Sh...  7.63 us
    pallas_call x1, Pallas kernels, body(): pl.pallas_call(gram_kernel, out_shape=jax.ShapeDtypeStruct((width // 2, w...  4.15 us
    pallas_call x1, Pallas kernels, body(): pl.pallas_call(functools.partial(pack_kernel, groups, block), out_shape=s...  2.32 us
  transfers between devices with their start and end apart: 13, of which 6 were waited for; matrix products, arithmetic and copies ran while one was open for 3% of the time, Pallas kernels for 5%

profile of v5, /device:TPU:0, one launch (start us, length us, event | category | flops | bytes accessed | tf_op | source)
XLA Modules:
  0.0 81.6 jit_solution(18237092688965331134)
XLA Ops:
  0.6 0.0 copy-start.1
  1.3 2.3 %pack.1 = (f32[7,8,2176]{2,1,0:T(8,128)S(1)}, f32[7,16,2176]{2,1,0:T(8,128)S(1)}, f32[7,8,2176]{2,1,0:T(8,128)S(1)}, f32[2,8,2176]{2,1,0:T(8,128)}, f32[2,16,2176]{2,1,0:T(8,128)}, /*index=5*/f32[2,8,2176]{2,1,0:T(8,128)}) custom-call(s32[1]{0:T(128)S(6)} %copy.12.step_ref, f32[1,2,16,4096]{3,2,1,0:T(8,128)} %refs_0_.1, f32[16,4096]{1,0:T(8,128)} %refs_1_.1, ...), custom_call_target="tpu_custom_call" | custom-call | tf_op jit(solution)/shard_map/pack/pallas_call | solution.py:590
  3.6 0.5 collective-permute-start
  4.1 5.0 %collective-permute-start.1 = (f32[7,8,2176]{2,1,0:T(8,128)S(1)}, f32[7,8,2176]{2,1,0:T(8,128)S(1)}, u32[]{:S(2)}, u32[]{:S(2)}) collective-permute-start(f32[7,8,2176]{2,1,0:T(8,128)S(1)} %get-tuple-element.21), channel_id=1, source_target_pairs={{0,30},{1,31},{2,0},{3,1},{4,2},{5,3},{6,4},{7,5},{8,6},{9,7},{10,... | collective-permute-start | bytes 1462280 | tf_op jit(solution)/shard_map/ppermute | solution.py:527
  9.2 1.9 %collective-permute-start.3 = (f32[2,16,2176]{2,1,0:T(8,128)}, f32[2,16,2176]{2,1,0:T(8,128)S(1)}, u32[]{:S(2)}, u32[]{:S(2)}) collective-permute-start(f32[2,16,2176]{2,1,0:T(8,128)} %get-tuple-element.23), channel_id=1, source_target_pairs={{0,1},{1,0},{2,3},{3,2},{4,5},{5,4},{6,7},{7,6},{8,9},{9,8},{10,11... | collective-permute-start | bytes 835592 | tf_op jit(solution)/shard_map/ppermute | solution.py:527
  11.1 0.0 collective-permute-start.2
  11.1 5.3 %collective-permute-start.4 = (f32[2,8,2176]{2,1,0:T(8,128)}, f32[2,8,2176]{2,1,0:T(8,128)S(1)}, u32[]{:S(2)}, u32[]{:S(2)}) collective-permute-start(f32[2,8,2176]{2,1,0:T(8,128)} %get-tuple-element.24), channel_id=1, source_target_pairs={{0,31},{1,30},{2,1},{3,0},{4,3},{5,2},{6,5},{7,4},{8,7},{9,6},{10,... | collective-permute-start | bytes 417800 | tf_op jit(solution)/shard_map/ppermute | solution.py:527
  16.4 0.9 %dynamic-slice_bitcast_fusion.1 = (f32[64,128]{0,1:T(8,128)S(1)}, f32[64,128]{0,1:T(8,128)S(1)}) fusion(f32[2,2,64,128]{2,3,1,0:T(8,128)} %constant.17.clone, s32[]{:T(128)S(6)} %select_n.4, s32[]{:T(128)S(6)} %add.36), kind=kLoop, calls=%fused_computation.5 | loop fusion | bytes 131080 | tf_op jit(solution)/shard_map/squeeze | solution.py:616
  17.3 2.2 %collective-permute-done.2.refs_3_ = f32[2,8,2176]{2,1,0:T(8,128)S(1)} collective-permute-done((f32[2,8,2176]{2,1,0:T(8,128)}, f32[2,8,2176]{2,1,0:T(8,128)S(1)}, u32[]{:S(2)}, u32[]{:S(2)}) %collective-permute-start.2) | collective-permute-done | bytes 139296 | tf_op jit(solution)/shard_map/ppermute | solution.py:527
  19.5 0.0 collective-permute-done.4.refs_5_
  19.5 0.0 collective-permute-done.3.refs_4_
  19.5 0.0 collective-permute-done.refs_0_
  19.6 0.0 collective-permute-done.1.refs_2_
  19.6 12.2 %first.1 = (f32[16,64,1024]{2,1,0:T(8,128)}, f32[8,32,8,1152]{3,2,1,0:T(8,128)S(1)}, f32[8,8,1152]{2,1,0:T(8,128)S(1)}, f32[16,8,1152]{2,1,0:T(8,128)S(1)}, f32[8,8,1152]{2,1,0:T(8,128)S(1)}) custom-call(f32[7,8,2176]{2,1,0:T(8,128)S(1)} %collective-permute-done.refs_0_, f32[7,16,2176]{2,1,0:T(8,128)S(1)} %get-tuple-element.20.refs_1_, ...), custom_call_target="tpu_custom_call" | custom-call | tf_op jit(solution)/shard_map/first/pallas_call | solution.py:629
  31.7 0.0 copy-start
  31.8 4.6 %collective-permute-start.5 = (f32[8,8,1152]{2,1,0:T(8,128)S(1)}, f32[8,8,1152]{2,1,0:T(8,128)S(1)}, u32[]{:S(2)}, u32[]{:S(2)}) collective-permute-start(f32[8,8,1152]{2,1,0:T(8,128)S(1)} %get-tuple-element.25), channel_id=1, source_target_pairs={{0,2},{1,3},{2,4},{3,5},{4,6},{5,7},{6,8},{7,9},{8,10},{9,11},{10,... | collective-permute-start | bytes 884744 | tf_op jit(solution)/shard_map/ppermute | solution.py:527
  36.4 0.0 collective-permute-start.6
  36.4 0.9 %add_bitcast_fusion.refs_2_ = f32[128,64]{1,0:T(8,128)S(1)} fusion(f32[2,2,64,128]{2,3,1,0:T(8,128)} %constant.17.clone, s32[]{:T(128)S(6)} %select_n.4, s32[]{:T(128)S(6)} %add.36), kind=kLoop, calls=%fused_computation.6 | loop fusion | flops 8192 | bytes 98312 | tf_op jit(solution)/shard_map/transpose | solution.py:618
  37.2 0.0 copy-done.1
  37.3 0.2 convolution_bitcast_fusion.refs_1_
  37.5 4.1 %gram.1.refs_0_ = f32[64,64]{1,0:T(8,128)S(1)} custom-call(f32[16,64,1024]{2,1,0:T(8,128)} %get-tuple-element.29.snap_ref.earlier.early_ref), custom_call_target="tpu_custom_call" | custom-call | flops 536870912 | bytes 4194304 | tf_op jit(solution)/shard_map/gram/pallas_call | solution.py:652
  41.7 0.0 collective-permute-done.5.left_halo
  41.7 0.0 collective-permute-done.6.right_halo
  41.7 0.0 copy-done
  41.7 13.3 %second.1 = (f32[16,64,1024]{2,1,0:T(8,128)}, f32[2,16,2048]{2,1,0:T(8,128)S(1)}, f32[1,2,16,2048]{3,2,1,0:T(8,128)S(1)}, f32[32,64]{1,0:T(8,128)S(1)}) custom-call(f32[8,8,1152]{2,1,0:T(8,128)S(1)} %collective-permute-done.5.left_halo, f32[16,8,1152]{2,1,0:T(8,128)S(1)} %get-tuple-element.26.own, f32[8,8,1152]{2,1,0:T(8,128)S(1)} %collective-permute-done.6.right_halo, ...), custom_call_target="tpu_custom_call" | custom-call | tf_op jit(solution)/shard_map/second/pallas_call | solution.py:663
  55.0 1.4 %collective-permute-start.7 = (f32[32,64]{1,0:T(8,128)S(1)}, f32[32,64]{1,0:T(8,128)S(1)}, u32[]{:S(2)}, u32[]{:S(2)}) collective-permute-start(f32[32,64]{1,0:T(8,128)S(1)} %get-tuple-element.30), channel_id=1, source_target_pairs={{0,1},{1,0},{2,3},{3,2},{4,5},{5,4},{6,7},{7,6},{8,9},{9,8},{10,11... | collective-permute-start | bytes 24584 | tf_op jit(solution)/shard_map/ppermute | solution.py:546
  56.4 2.4 %collective-permute-done.7 = f32[32,64]{1,0:T(8,128)S(1)} collective-permute-done((f32[32,64]{1,0:T(8,128)S(1)}, f32[32,64]{1,0:T(8,128)S(1)}, u32[]{:S(2)}, u32[]{:S(2)}) %collective-permute-start.7) | collective-permute-done | bytes 8224 | tf_op jit(solution)/shard_map/ppermute | solution.py:546
  58.8 0.8 collective-permute-start.8
  59.6 0.1 copy.11
  59.7 0.1 pad.3.clone
  59.8 0.7 collective-permute-done.8
  60.4 3.4 %collective-permute-start.9 = (f32[32,64]{1,0:T(8,128)S(1)}, f32[32,64]{1,0:T(8,128)S(1)}, u32[]{:S(2)}, u32[]{:S(2)}) collective-permute-start(f32[32,64]{1,0:T(8,128)S(1)} %add.31), channel_id=1, source_target_pairs={{0,4},{1,5},{2,6},{3,7},{4,0},{5,1},{6,2},{7,3},{8,12},{9,13},{10,... | collective-permute-start | bytes 24584 | tf_op jit(solution)/shard_map/ppermute | solution.py:546
  63.9 0.1 maximum_maximum_fusion.spread_ref
  64.0 0.6 collective-permute-start.12
  64.5 1.1 %collective-permute-done.9 = f32[32,64]{1,0:T(8,128)S(1)} collective-permute-done((f32[32,64]{1,0:T(8,128)S(1)}, f32[32,64]{1,0:T(8,128)S(1)}, u32[]{:S(2)}, u32[]{:S(2)}) %collective-permute-start.9) | collective-permute-done | bytes 8224 | tf_op jit(solution)/shard_map/ppermute | solution.py:546
  65.6 1.6 %collective-permute-start.10 = (f32[32,64]{1,0:T(8,128)S(1)}, f32[32,64]{1,0:T(8,128)S(1)}, u32[]{:S(2)}, u32[]{:S(2)}) collective-permute-start(f32[32,64]{1,0:T(8,128)S(1)} %add.32), channel_id=1, source_target_pairs={{0,8},{1,9},{2,10},{3,11},{4,12},{5,13},{6,14},{7,15},{8,0},{9,1},... | collective-permute-start | bytes 24584 | tf_op jit(solution)/shard_map/ppermute | solution.py:546
  67.2 2.2 %collective-permute-done.10 = f32[32,64]{1,0:T(8,128)S(1)} collective-permute-done((f32[32,64]{1,0:T(8,128)S(1)}, f32[32,64]{1,0:T(8,128)S(1)}, u32[]{:S(2)}, u32[]{:S(2)}) %collective-permute-start.10) | collective-permute-done | bytes 8224 | tf_op jit(solution)/shard_map/ppermute | solution.py:546
  69.3 2.6 %collective-permute-start.11 = (f32[32,64]{1,0:T(8,128)S(1)}, f32[32,64]{1,0:T(8,128)S(1)}, u32[]{:S(2)}, u32[]{:S(2)}) collective-permute-start(f32[32,64]{1,0:T(8,128)S(1)} %add.33.left_ref), channel_id=1, source_target_pairs={{0,16},{1,17},{2,18},{3,19},{4,20},{5,21},{6,22},{7,23},{8,24},{9,... | collective-permute-start | bytes 24584 | tf_op jit(solution)/shard_map/ppermute | solution.py:546
  71.9 0.1 fusion.4.unit_ref
  72.0 2.0 %collective-permute-done.11.other_ref = f32[32,64]{1,0:T(8,128)S(1)} collective-permute-done((f32[32,64]{1,0:T(8,128)S(1)}, f32[32,64]{1,0:T(8,128)S(1)}, u32[]{:S(2)}, u32[]{:S(2)}) %collective-permute-start.11) | collective-permute-done | bytes 8224 | tf_op jit(solution)/shard_map/ppermute | solution.py:546
  74.0 0.0 collective-permute-done.12.came_ref
  74.0 7.6 %merge.1 = (f32[32,16,2048]{2,1,0:T(8,128)}, f32[2,16,4096]{2,1,0:T(8,128)}) custom-call(f32[32,64]{1,0:T(8,128)S(1)} %add.33.left_ref, f32[32,64]{1,0:T(8,128)S(1)} %collective-permute-done.11.other_ref, f32[64,128]{1,0:T(8,128)S(1)} %maximum_maximum_fusion.spread_ref, f32[32,128]{1,0:T(8,128)S(1)} %fusion.4.unit_ref, ...), custom_call_target="tpu_custom_call" | custom-call | tf_op jit(solution)/shard_map/merge/pallas_call | solution.py:678
  (8 shorter events, 0.0 us)
Async XLA Ops:
  0.6 36.6 %copy-start.1 = (f32[64,32]{0,1:T(8,128)S(1)}, f32[64,32]{0,1:T(8,128)}, u32[]{:S(2)}) copy-start(f32[64,32]{0,1:T(8,128)} %param.16) | copy-start | bytes 24580
  3.6 15.9 %collective-permute-start = (f32[7,8,2176]{2,1,0:T(8,128)S(1)}, f32[7,8,2176]{2,1,0:T(8,128)S(1)}, u32[]{:S(2)}, u32[]{:S(2)}) collective-permute-start(f32[7,8,2176]{2,1,0:T(8,128)S(1)} %get-tuple-element.19), channel_id=1, source_target_pairs={{0,2},{1,3},{2,4},{3,5},{4,6},{5,7},{6,8},{7,9},{8,10},{9,11},{10,... | collective-permute-start | bytes 1462280 | tf_op jit(solution)/shard_map/ppermute | solution.py:527
  4.1 15.4 %collective-permute-start.1 = (f32[7,8,2176]{2,1,0:T(8,128)S(1)}, f32[7,8,2176]{2,1,0:T(8,128)S(1)}, u32[]{:S(2)}, u32[]{:S(2)}) collective-permute-start(f32[7,8,2176]{2,1,0:T(8,128)S(1)} %get-tuple-element.21), channel_id=1, source_target_pairs={{0,30},{1,31},{2,0},{3,1},{4,2},{5,3},{6,4},{7,5},{8,6},{9,7},{10,... | collective-permute-start | bytes 1462280 | tf_op jit(solution)/shard_map/ppermute | solution.py:527
  9.2 10.4 %collective-permute-start.3 = (f32[2,16,2176]{2,1,0:T(8,128)}, f32[2,16,2176]{2,1,0:T(8,128)S(1)}, u32[]{:S(2)}, u32[]{:S(2)}) collective-permute-start(f32[2,16,2176]{2,1,0:T(8,128)} %get-tuple-element.23), channel_id=1, source_target_pairs={{0,1},{1,0},{2,3},{3,2},{4,5},{5,4},{6,7},{7,6},{8,9},{9,8},{10,11... | collective-permute-start | bytes 835592 | tf_op jit(solution)/shard_map/ppermute | solution.py:527
  11.1 8.4 %collective-permute-start.2 = (f32[2,8,2176]{2,1,0:T(8,128)}, f32[2,8,2176]{2,1,0:T(8,128)S(1)}, u32[]{:S(2)}, u32[]{:S(2)}) collective-permute-start(f32[2,8,2176]{2,1,0:T(8,128)} %get-tuple-element.22), channel_id=1, source_target_pairs={{0,3},{1,2},{2,5},{3,4},{4,7},{5,6},{6,9},{7,8},{8,11},{9,10},{10,... | collective-permute-start | bytes 417800 | tf_op jit(solution)/shard_map/ppermute | solution.py:527
  11.1 8.4 %collective-permute-start.4 = (f32[2,8,2176]{2,1,0:T(8,128)}, f32[2,8,2176]{2,1,0:T(8,128)S(1)}, u32[]{:S(2)}, u32[]{:S(2)}) collective-permute-start(f32[2,8,2176]{2,1,0:T(8,128)} %get-tuple-element.24), channel_id=1, source_target_pairs={{0,31},{1,30},{2,1},{3,0},{4,3},{5,2},{6,5},{7,4},{8,7},{9,6},{10,... | collective-permute-start | bytes 417800 | tf_op jit(solution)/shard_map/ppermute | solution.py:527
  31.7 9.9 %copy-start = (f32[16,64,1024]{2,1,0:T(8,128)S(1)}, f32[16,64,1024]{2,1,0:T(8,128)}, u32[]{:S(2)}) copy-start(f32[16,64,1024]{2,1,0:T(8,128)} %get-tuple-element.29.snap_ref.earlier.early_ref) | copy-start | bytes 12582916
  31.8 9.9 %collective-permute-start.5 = (f32[8,8,1152]{2,1,0:T(8,128)S(1)}, f32[8,8,1152]{2,1,0:T(8,128)S(1)}, u32[]{:S(2)}, u32[]{:S(2)}) collective-permute-start(f32[8,8,1152]{2,1,0:T(8,128)S(1)} %get-tuple-element.25), channel_id=1, source_target_pairs={{0,2},{1,3},{2,4},{3,5},{4,6},{5,7},{6,8},{7,9},{8,10},{9,11},{10,... | collective-permute-start | bytes 884744 | tf_op jit(solution)/shard_map/ppermute | solution.py:527
  36.4 5.3 %collective-permute-start.6 = (f32[8,8,1152]{2,1,0:T(8,128)S(1)}, f32[8,8,1152]{2,1,0:T(8,128)S(1)}, u32[]{:S(2)}, u32[]{:S(2)}) collective-permute-start(f32[8,8,1152]{2,1,0:T(8,128)S(1)} %get-tuple-element.27), channel_id=1, source_target_pairs={{0,30},{1,31},{2,0},{3,1},{4,2},{5,3},{6,4},{7,5},{8,6},{9,7},{10,... | collective-permute-start | bytes 884744 | tf_op jit(solution)/shard_map/ppermute | solution.py:527
  55.0 3.8 %collective-permute-start.7 = (f32[32,64]{1,0:T(8,128)S(1)}, f32[32,64]{1,0:T(8,128)S(1)}, u32[]{:S(2)}, u32[]{:S(2)}) collective-permute-start(f32[32,64]{1,0:T(8,128)S(1)} %get-tuple-element.30), channel_id=1, source_target_pairs={{0,1},{1,0},{2,3},{3,2},{4,5},{5,4},{6,7},{7,6},{8,9},{9,8},{10,11... | collective-permute-start | bytes 24584 | tf_op jit(solution)/shard_map/ppermute | solution.py:546
  58.8 1.6 %collective-permute-start.8 = (f32[32,64]{1,0:T(8,128)S(1)}, f32[32,64]{1,0:T(8,128)S(1)}, u32[]{:S(2)}, u32[]{:S(2)}) collective-permute-start(f32[32,64]{1,0:T(8,128)S(1)} %add.30), channel_id=1, source_target_pairs={{0,2},{1,3},{2,0},{3,1},{4,6},{5,7},{6,4},{7,5},{8,10},{9,11},{10,... | collective-permute-start | bytes 24584 | tf_op jit(solution)/shard_map/ppermute | solution.py:546
  60.4 5.2 %collective-permute-start.9 = (f32[32,64]{1,0:T(8,128)S(1)}, f32[32,64]{1,0:T(8,128)S(1)}, u32[]{:S(2)}, u32[]{:S(2)}) collective-permute-start(f32[32,64]{1,0:T(8,128)S(1)} %add.31), channel_id=1, source_target_pairs={{0,4},{1,5},{2,6},{3,7},{4,0},{5,1},{6,2},{7,3},{8,12},{9,13},{10,... | collective-permute-start | bytes 24584 | tf_op jit(solution)/shard_map/ppermute | solution.py:546
  64.0 10.0 %collective-permute-start.12 = (f32[2,16,2048]{2,1,0:T(8,128)S(1)}, f32[2,16,2048]{2,1,0:T(8,128)S(1)}, u32[]{:S(2)}, u32[]{:S(2)}) collective-permute-start(f32[2,16,2048]{2,1,0:T(8,128)S(1)} %bitcast.15), channel_id=1, source_target_pairs={{0,1},{1,0},{2,3},{3,2},{4,5},{5,4},{6,7},{7,6},{8,9},{9,8},{10,11... | collective-permute-start | bytes 786440 | tf_op jit(solution)/shard_map/ppermute | solution.py:527
  65.6 3.7 %collective-permute-start.10 = (f32[32,64]{1,0:T(8,128)S(1)}, f32[32,64]{1,0:T(8,128)S(1)}, u32[]{:S(2)}, u32[]{:S(2)}) collective-permute-start(f32[32,64]{1,0:T(8,128)S(1)} %add.32), channel_id=1, source_target_pairs={{0,8},{1,9},{2,10},{3,11},{4,12},{5,13},{6,14},{7,15},{8,0},{9,1},... | collective-permute-start | bytes 24584 | tf_op jit(solution)/shard_map/ppermute | solution.py:546
  69.3 4.6 %collective-permute-start.11 = (f32[32,64]{1,0:T(8,128)S(1)}, f32[32,64]{1,0:T(8,128)S(1)}, u32[]{:S(2)}, u32[]{:S(2)}) collective-permute-start(f32[32,64]{1,0:T(8,128)S(1)} %add.33.left_ref), channel_id=1, source_target_pairs={{0,16},{1,17},{2,18},{3,19},{4,20},{5,21},{6,22},{7,23},{8,24},{9,... | collective-permute-start | bytes 24584 | tf_op jit(solution)/shard_map/ppermute | solution.py:546

commit v6 on v5

--- a/solution.py
+++ b/solution.py
@@ -298,7 +298,7 @@
                 prepare(place, base, tile, False)
                 return inner
 
-            lax.fori_loop(0, tiles - 1, by_tiles, 0)
+            lax.fori_loop(0, tiles - 1, by_tiles, 0, unroll=4)
             prepare(place, base, tiles - 1, True)
             return carry
 
@@ -383,7 +383,9 @@
             every = jnp.concatenate([now, split_rows(earlier[x])], axis=0)
             return total + outer_of(now, every)
 
-        both = lax.fori_loop(0, rows, add, jnp.zeros((2 * width, 4 * width), jnp.float32))
+        both = jnp.zeros((2 * width, 4 * width), jnp.float32)
+        for x in range(rows):
+            both = add(x, both)
         late_late, late_early = joined(both[:, : 2 * width]), joined(both[:, 2 * width :])
         lane = lanes_of((1, width))
         result = jnp.zeros(left_ref.shape, jnp.float32)

time: 81.9 us -> 79.7 us (0.973)
  Pallas kernels: 39.6 us -> 37.2 us
    pallas_call x1, Pallas kernels: 13.3 us -> 11.8 us  [body(): pl.pallas_call(functools.partial(second_kernel, groups, halves, fast), ou...]
    pallas_call x1, Pallas kernels: 12.2 us -> 11.3 us  [body(): pl.pallas_call(functools.partial(first_kernel, groups, halves), out_shape...]
where the time goes in v6:
time: 79.7 us; the launch traced here: 79.4 us
  Pallas kernels  37.2 us (47%)
  starting transfers between devices  27.9 us (35%)
  waiting for transfers between devices  10.3 us (13%)
  between operations  1.58 us (2%)
  local copies, waits for them, and re-layouts  1.06 us (1%)
  other arithmetic  1.06 us (1%)
    ppermute x8, starting transfers between devices, shifted(): return lax.ppermute(value, AXES, moves)  18 us
    pallas_call x1, Pallas kernels, body(): pl.pallas_call(functools.partial(second_kernel, groups, halves, fast), ou...  11.8 us
    pallas_call x1, Pallas kernels, body(): pl.pallas_call(functools.partial(first_kernel, groups, halves), out_shape...  11.3 us
    ppermute x5, starting transfers between devices, total_of(): other = lax.ppermute(value, AXES, [(i, i ^ bit) for i in range(size)])  9.97 us
    ppermute x5, waiting for transfers between devices, total_of(): other = lax.ppermute(value, AXES, [(i, i ^ bit) for i in range(size)])  8.09 us
    pallas_call x1, Pallas kernels, body(): pl.pallas_call(functools.partial(merge_kernel, halves), out_shape=[jax.Sh...  7.63 us
    pallas_call x1, Pallas kernels, body(): pl.pallas_call(gram_kernel, out_shape=jax.ShapeDtypeStruct((width // 2, w...  4.15 us
    pallas_call x1, Pallas kernels, body(): pl.pallas_call(functools.partial(pack_kernel, groups, block), out_shape=s...  2.32 us
  transfers between devices with their start and end apart: 13, of which 6 were waited for; matrix products, arithmetic and copies ran while one was open for 3% of the time, Pallas kernels for 5%

profile of v6, /device:TPU:0, one launch (start us, length us, event | category | flops | bytes accessed | tf_op | source)
XLA Modules:
  0.0 79.4 jit_solution(8218397191292136811)
XLA Ops:
  0.6 0.0 copy-start.1
  1.3 2.3 %pack.1 = (f32[7,8,2176]{2,1,0:T(8,128)S(1)}, f32[7,16,2176]{2,1,0:T(8,128)S(1)}, f32[7,8,2176]{2,1,0:T(8,128)S(1)}, f32[2,8,2176]{2,1,0:T(8,128)}, f32[2,16,2176]{2,1,0:T(8,128)}, /*index=5*/f32[2,8,2176]{2,1,0:T(8,128)}) custom-call(s32[1]{0:T(128)S(6)} %copy.12.step_ref, f32[1,2,16,4096]{3,2,1,0:T(8,128)} %refs_0_.1, f32[16,4096]{1,0:T(8,128)} %refs_1_.1, ...), custom_call_target="tpu_custom_call" | custom-call | tf_op jit(solution)/shard_map/pack/pallas_call | solution.py:592
  3.6 0.5 collective-permute-start
  4.1 5.0 %collective-permute-start.1 = (f32[7,8,2176]{2,1,0:T(8,128)S(1)}, f32[7,8,2176]{2,1,0:T(8,128)S(1)}, u32[]{:S(2)}, u32[]{:S(2)}) collective-permute-start(f32[7,8,2176]{2,1,0:T(8,128)S(1)} %get-tuple-element.21), channel_id=1, source_target_pairs={{0,30},{1,31},{2,0},{3,1},{4,2},{5,3},{6,4},{7,5},{8,6},{9,7},{10,... | collective-permute-start | bytes 1462280 | tf_op jit(solution)/shard_map/ppermute | solution.py:529
  9.2 1.9 %collective-permute-start.3 = (f32[2,16,2176]{2,1,0:T(8,128)}, f32[2,16,2176]{2,1,0:T(8,128)S(1)}, u32[]{:S(2)}, u32[]{:S(2)}) collective-permute-start(f32[2,16,2176]{2,1,0:T(8,128)} %get-tuple-element.23), channel_id=1, source_target_pairs={{0,1},{1,0},{2,3},{3,2},{4,5},{5,4},{6,7},{7,6},{8,9},{9,8},{10,11... | collective-permute-start | bytes 835592 | tf_op jit(solution)/shard_map/ppermute | solution.py:529
  11.1 0.0 collective-permute-start.2
  11.1 5.3 %collective-permute-start.4 = (f32[2,8,2176]{2,1,0:T(8,128)}, f32[2,8,2176]{2,1,0:T(8,128)S(1)}, u32[]{:S(2)}, u32[]{:S(2)}) collective-permute-start(f32[2,8,2176]{2,1,0:T(8,128)} %get-tuple-element.24), channel_id=1, source_target_pairs={{0,31},{1,30},{2,1},{3,0},{4,3},{5,2},{6,5},{7,4},{8,7},{9,6},{10,... | collective-permute-start | bytes 417800 | tf_op jit(solution)/shard_map/ppermute | solution.py:529
  16.4 0.9 %dynamic-slice_bitcast_fusion.1 = (f32[64,128]{0,1:T(8,128)S(1)}, f32[64,128]{0,1:T(8,128)S(1)}) fusion(f32[2,2,64,128]{2,3,1,0:T(8,128)} %constant.17.clone, s32[]{:T(128)S(6)} %select_n.4, s32[]{:T(128)S(6)} %add.36), kind=kLoop, calls=%fused_computation.5 | loop fusion | bytes 131080 | tf_op jit(solution)/shard_map/squeeze | solution.py:618
  17.3 2.2 %collective-permute-done.2.refs_3_ = f32[2,8,2176]{2,1,0:T(8,128)S(1)} collective-permute-done((f32[2,8,2176]{2,1,0:T(8,128)}, f32[2,8,2176]{2,1,0:T(8,128)S(1)}, u32[]{:S(2)}, u32[]{:S(2)}) %collective-permute-start.2) | collective-permute-done | bytes 139296 | tf_op jit(solution)/shard_map/ppermute | solution.py:529
  19.5 0.0 collective-permute-done.4.refs_5_
  19.5 0.0 collective-permute-done.3.refs_4_
  19.5 0.0 collective-permute-done.refs_0_
  19.6 0.0 collective-permute-done.1.refs_2_
  19.6 11.3 %first.1 = (f32[16,64,1024]{2,1,0:T(8,128)}, f32[8,32,8,1152]{3,2,1,0:T(8,128)S(1)}, f32[8,8,1152]{2,1,0:T(8,128)S(1)}, f32[16,8,1152]{2,1,0:T(8,128)S(1)}, f32[8,8,1152]{2,1,0:T(8,128)S(1)}) custom-call(f32[7,8,2176]{2,1,0:T(8,128)S(1)} %collective-permute-done.refs_0_, f32[7,16,2176]{2,1,0:T(8,128)S(1)} %get-tuple-element.20.refs_1_, ...), custom_call_target="tpu_custom_call" | custom-call | tf_op jit(solution)/shard_map/first/pallas_call | solution.py:631
  30.9 0.0 copy-start
  30.9 4.6 %collective-permute-start.5 = (f32[8,8,1152]{2,1,0:T(8,128)S(1)}, f32[8,8,1152]{2,1,0:T(8,128)S(1)}, u32[]{:S(2)}, u32[]{:S(2)}) collective-permute-start(f32[8,8,1152]{2,1,0:T(8,128)S(1)} %get-tuple-element.25), channel_id=1, source_target_pairs={{0,2},{1,3},{2,4},{3,5},{4,6},{5,7},{6,8},{7,9},{8,10},{9,11},{10,... | collective-permute-start | bytes 884744 | tf_op jit(solution)/shard_map/ppermute | solution.py:529
  35.5 0.0 collective-permute-start.6
  35.5 0.9 %add_bitcast_fusion.refs_2_ = f32[128,64]{1,0:T(8,128)S(1)} fusion(f32[2,2,64,128]{2,3,1,0:T(8,128)} %constant.17.clone, s32[]{:T(128)S(6)} %select_n.4, s32[]{:T(128)S(6)} %add.36), kind=kLoop, calls=%fused_computation.6 | loop fusion | flops 8192 | bytes 98312 | tf_op jit(solution)/shard_map/transpose | solution.py:620
  36.4 0.0 copy-done.1
  36.4 0.2 convolution_bitcast_fusion.refs_1_
  36.7 4.2 %gram.1.refs_0_ = f32[64,64]{1,0:T(8,128)S(1)} custom-call(f32[16,64,1024]{2,1,0:T(8,128)} %get-tuple-element.29.snap_ref.earlier.early_ref), custom_call_target="tpu_custom_call" | custom-call | flops 536870912 | bytes 4194304 | tf_op jit(solution)/shard_map/gram/pallas_call | solution.py:654
  40.8 0.0 collective-permute-done.5.left_halo
  40.9 0.0 collective-permute-done.6.right_halo
  40.9 0.0 copy-done
  40.9 11.8 %second.1 = (f32[16,64,1024]{2,1,0:T(8,128)}, f32[2,16,2048]{2,1,0:T(8,128)S(1)}, f32[1,2,16,2048]{3,2,1,0:T(8,128)S(1)}, f32[32,64]{1,0:T(8,128)S(1)}) custom-call(f32[8,8,1152]{2,1,0:T(8,128)S(1)} %collective-permute-done.5.left_halo, f32[16,8,1152]{2,1,0:T(8,128)S(1)} %get-tuple-element.26.own, f32[8,8,1152]{2,1,0:T(8,128)S(1)} %collective-permute-done.6.right_halo, ...), custom_call_target="tpu_custom_call" | custom-call | tf_op jit(solution)/shard_map/second/pallas_call | solution.py:665
  52.7 1.6 %collective-permute-start.7 = (f32[32,64]{1,0:T(8,128)S(1)}, f32[32,64]{1,0:T(8,128)S(1)}, u32[]{:S(2)}, u32[]{:S(2)}) collective-permute-start(f32[32,64]{1,0:T(8,128)S(1)} %get-tuple-element.30), channel_id=1, source_target_pairs={{0,1},{1,0},{2,3},{3,2},{4,5},{5,4},{6,7},{7,6},{8,9},{9,8},{10,11... | collective-permute-start | bytes 24584 | tf_op jit(solution)/shard_map/ppermute | solution.py:548
  54.2 2.2 %collective-permute-done.7 = f32[32,64]{1,0:T(8,128)S(1)} collective-permute-done((f32[32,64]{1,0:T(8,128)S(1)}, f32[32,64]{1,0:T(8,128)S(1)}, u32[]{:S(2)}, u32[]{:S(2)}) %collective-permute-start.7) | collective-permute-done | bytes 8224 | tf_op jit(solution)/shard_map/ppermute | solution.py:548
  56.5 0.8 collective-permute-start.8
  57.2 0.1 copy.11
  57.3 0.1 pad.3.clone
  57.4 0.7 collective-permute-done.8
  58.1 3.4 %collective-permute-start.9 = (f32[32,64]{1,0:T(8,128)S(1)}, f32[32,64]{1,0:T(8,128)S(1)}, u32[]{:S(2)}, u32[]{:S(2)}) collective-permute-start(f32[32,64]{1,0:T(8,128)S(1)} %add.31), channel_id=1, source_target_pairs={{0,4},{1,5},{2,6},{3,7},{4,0},{5,1},{6,2},{7,3},{8,12},{9,13},{10,... | collective-permute-start | bytes 24584 | tf_op jit(solution)/shard_map/ppermute | solution.py:548
  61.5 0.1 maximum_maximum_fusion.spread_ref
  61.6 0.6 collective-permute-start.12
  62.2 1.1 %collective-permute-done.9 = f32[32,64]{1,0:T(8,128)S(1)} collective-permute-done((f32[32,64]{1,0:T(8,128)S(1)}, f32[32,64]{1,0:T(8,128)S(1)}, u32[]{:S(2)}, u32[]{:S(2)}) %collective-permute-start.9) | collective-permute-done | bytes 8224 | tf_op jit(solution)/shard_map/ppermute | solution.py:548
  63.2 1.6 %collective-permute-start.10 = (f32[32,64]{1,0:T(8,128)S(1)}, f32[32,64]{1,0:T(8,128)S(1)}, u32[]{:S(2)}, u32[]{:S(2)}) collective-permute-start(f32[32,64]{1,0:T(8,128)S(1)} %add.32), channel_id=1, source_target_pairs={{0,8},{1,9},{2,10},{3,11},{4,12},{5,13},{6,14},{7,15},{8,0},{9,1},... | collective-permute-start | bytes 24584 | tf_op jit(solution)/shard_map/ppermute | solution.py:548
  64.8 2.2 %collective-permute-done.10 = f32[32,64]{1,0:T(8,128)S(1)} collective-permute-done((f32[32,64]{1,0:T(8,128)S(1)}, f32[32,64]{1,0:T(8,128)S(1)}, u32[]{:S(2)}, u32[]{:S(2)}) %collective-permute-start.10) | collective-permute-done | bytes 8224 | tf_op jit(solution)/shard_map/ppermute | solution.py:548
  67.0 2.6 %collective-permute-start.11 = (f32[32,64]{1,0:T(8,128)S(1)}, f32[32,64]{1,0:T(8,128)S(1)}, u32[]{:S(2)}, u32[]{:S(2)}) collective-permute-start(f32[32,64]{1,0:T(8,128)S(1)} %add.33.left_ref), channel_id=1, source_target_pairs={{0,16},{1,17},{2,18},{3,19},{4,20},{5,21},{6,22},{7,23},{8,24},{9,... | collective-permute-start | bytes 24584 | tf_op jit(solution)/shard_map/ppermute | solution.py:548
  69.6 0.1 fusion.4.unit_ref
  69.7 2.0 %collective-permute-done.11.other_ref = f32[32,64]{1,0:T(8,128)S(1)} collective-permute-done((f32[32,64]{1,0:T(8,128)S(1)}, f32[32,64]{1,0:T(8,128)S(1)}, u32[]{:S(2)}, u32[]{:S(2)}) %collective-permute-start.11) | collective-permute-done | bytes 8224 | tf_op jit(solution)/shard_map/ppermute | solution.py:548
  71.6 0.0 collective-permute-done.12.came_ref
  71.6 7.6 %merge.1 = (f32[32,16,2048]{2,1,0:T(8,128)}, f32[2,16,4096]{2,1,0:T(8,128)}) custom-call(f32[32,64]{1,0:T(8,128)S(1)} %add.33.left_ref, f32[32,64]{1,0:T(8,128)S(1)} %collective-permute-done.11.other_ref, f32[64,128]{1,0:T(8,128)S(1)} %maximum_maximum_fusion.spread_ref, f32[32,128]{1,0:T(8,128)S(1)} %fusion.4.unit_ref, ...), custom_call_target="tpu_custom_call" | custom-call | tf_op jit(solution)/shard_map/merge/pallas_call | solution.py:680
  (8 shorter events, 0.0 us)
Async XLA Ops:
  0.6 35.8 %copy-start.1 = (f32[64,32]{0,1:T(8,128)S(1)}, f32[64,32]{0,1:T(8,128)}, u32[]{:S(2)}) copy-start(f32[64,32]{0,1:T(8,128)} %param.16) | copy-start | bytes 24580
  3.6 15.9 %collective-permute-start = (f32[7,8,2176]{2,1,0:T(8,128)S(1)}, f32[7,8,2176]{2,1,0:T(8,128)S(1)}, u32[]{:S(2)}, u32[]{:S(2)}) collective-permute-start(f32[7,8,2176]{2,1,0:T(8,128)S(1)} %get-tuple-element.19), channel_id=1, source_target_pairs={{0,2},{1,3},{2,4},{3,5},{4,6},{5,7},{6,8},{7,9},{8,10},{9,11},{10,... | collective-permute-start | bytes 1462280 | tf_op jit(solution)/shard_map/ppermute | solution.py:529
  4.1 15.4 %collective-permute-start.1 = (f32[7,8,2176]{2,1,0:T(8,128)S(1)}, f32[7,8,2176]{2,1,0:T(8,128)S(1)}, u32[]{:S(2)}, u32[]{:S(2)}) collective-permute-start(f32[7,8,2176]{2,1,0:T(8,128)S(1)} %get-tuple-element.21), channel_id=1, source_target_pairs={{0,30},{1,31},{2,0},{3,1},{4,2},{5,3},{6,4},{7,5},{8,6},{9,7},{10,... | collective-permute-start | bytes 1462280 | tf_op jit(solution)/shard_map/ppermute | solution.py:529
  9.2 10.4 %collective-permute-start.3 = (f32[2,16,2176]{2,1,0:T(8,128)}, f32[2,16,2176]{2,1,0:T(8,128)S(1)}, u32[]{:S(2)}, u32[]{:S(2)}) collective-permute-start(f32[2,16,2176]{2,1,0:T(8,128)} %get-tuple-element.23), channel_id=1, source_target_pairs={{0,1},{1,0},{2,3},{3,2},{4,5},{5,4},{6,7},{7,6},{8,9},{9,8},{10,11... | collective-permute-start | bytes 835592 | tf_op jit(solution)/shard_map/ppermute | solution.py:529
  11.1 8.4 %collective-permute-start.2 = (f32[2,8,2176]{2,1,0:T(8,128)}, f32[2,8,2176]{2,1,0:T(8,128)S(1)}, u32[]{:S(2)}, u32[]{:S(2)}) collective-permute-start(f32[2,8,2176]{2,1,0:T(8,128)} %get-tuple-element.22), channel_id=1, source_target_pairs={{0,3},{1,2},{2,5},{3,4},{4,7},{5,6},{6,9},{7,8},{8,11},{9,10},{10,... | collective-permute-start | bytes 417800 | tf_op jit(solution)/shard_map/ppermute | solution.py:529
  11.1 8.4 %collective-permute-start.4 = (f32[2,8,2176]{2,1,0:T(8,128)}, f32[2,8,2176]{2,1,0:T(8,128)S(1)}, u32[]{:S(2)}, u32[]{:S(2)}) collective-permute-start(f32[2,8,2176]{2,1,0:T(8,128)} %get-tuple-element.24), channel_id=1, source_target_pairs={{0,31},{1,30},{2,1},{3,0},{4,3},{5,2},{6,5},{7,4},{8,7},{9,6},{10,... | collective-permute-start | bytes 417800 | tf_op jit(solution)/shard_map/ppermute | solution.py:529
  30.9 9.9 %copy-start = (f32[16,64,1024]{2,1,0:T(8,128)S(1)}, f32[16,64,1024]{2,1,0:T(8,128)}, u32[]{:S(2)}) copy-start(f32[16,64,1024]{2,1,0:T(8,128)} %get-tuple-element.29.snap_ref.earlier.early_ref) | copy-start | bytes 12582916
  30.9 9.9 %collective-permute-start.5 = (f32[8,8,1152]{2,1,0:T(8,128)S(1)}, f32[8,8,1152]{2,1,0:T(8,128)S(1)}, u32[]{:S(2)}, u32[]{:S(2)}) collective-permute-start(f32[8,8,1152]{2,1,0:T(8,128)S(1)} %get-tuple-element.25), channel_id=1, source_target_pairs={{0,2},{1,3},{2,4},{3,5},{4,6},{5,7},{6,8},{7,9},{8,10},{9,11},{10,... | collective-permute-start | bytes 884744 | tf_op jit(solution)/shard_map/ppermute | solution.py:529
  35.5 5.3 %collective-permute-start.6 = (f32[8,8,1152]{2,1,0:T(8,128)S(1)}, f32[8,8,1152]{2,1,0:T(8,128)S(1)}, u32[]{:S(2)}, u32[]{:S(2)}) collective-permute-start(f32[8,8,1152]{2,1,0:T(8,128)S(1)} %get-tuple-element.27), channel_id=1, source_target_pairs={{0,30},{1,31},{2,0},{3,1},{4,2},{5,3},{6,4},{7,5},{8,6},{9,7},{10,... | collective-permute-start | bytes 884744 | tf_op jit(solution)/shard_map/ppermute | solution.py:529
  52.7 3.8 %collective-permute-start.7 = (f32[32,64]{1,0:T(8,128)S(1)}, f32[32,64]{1,0:T(8,128)S(1)}, u32[]{:S(2)}, u32[]{:S(2)}) collective-permute-start(f32[32,64]{1,0:T(8,128)S(1)} %get-tuple-element.30), channel_id=1, source_target_pairs={{0,1},{1,0},{2,3},{3,2},{4,5},{5,4},{6,7},{7,6},{8,9},{9,8},{10,11... | collective-permute-start | bytes 24584 | tf_op jit(solution)/shard_map/ppermute | solution.py:548
  56.5 1.6 %collective-permute-start.8 = (f32[32,64]{1,0:T(8,128)S(1)}, f32[32,64]{1,0:T(8,128)S(1)}, u32[]{:S(2)}, u32[]{:S(2)}) collective-permute-start(f32[32,64]{1,0:T(8,128)S(1)} %add.30), channel_id=1, source_target_pairs={{0,2},{1,3},{2,0},{3,1},{4,6},{5,7},{6,4},{7,5},{8,10},{9,11},{10,... | collective-permute-start | bytes 24584 | tf_op jit(solution)/shard_map/ppermute | solution.py:548
  58.1 5.2 %collective-permute-start.9 = (f32[32,64]{1,0:T(8,128)S(1)}, f32[32,64]{1,0:T(8,128)S(1)}, u32[]{:S(2)}, u32[]{:S(2)}) collective-permute-start(f32[32,64]{1,0:T(8,128)S(1)} %add.31), channel_id=1, source_target_pairs={{0,4},{1,5},{2,6},{3,7},{4,0},{5,1},{6,2},{7,3},{8,12},{9,13},{10,... | collective-permute-start | bytes 24584 | tf_op jit(solution)/shard_map/ppermute | solution.py:548
  61.6 10.0 %collective-permute-start.12 = (f32[2,16,2048]{2,1,0:T(8,128)S(1)}, f32[2,16,2048]{2,1,0:T(8,128)S(1)}, u32[]{:S(2)}, u32[]{:S(2)}) collective-permute-start(f32[2,16,2048]{2,1,0:T(8,128)S(1)} %bitcast.15), channel_id=1, source_target_pairs={{0,1},{1,0},{2,3},{3,2},{4,5},{5,4},{6,7},{7,6},{8,9},{9,8},{10,11... | collective-permute-start | bytes 786440 | tf_op jit(solution)/shard_map/ppermute | solution.py:529
  63.2 3.7 %collective-permute-start.10 = (f32[32,64]{1,0:T(8,128)S(1)}, f32[32,64]{1,0:T(8,128)S(1)}, u32[]{:S(2)}, u32[]{:S(2)}) collective-permute-start(f32[32,64]{1,0:T(8,128)S(1)} %add.32), channel_id=1, source_target_pairs={{0,8},{1,9},{2,10},{3,11},{4,12},{5,13},{6,14},{7,15},{8,0},{9,1},... | collective-permute-start | bytes 24584 | tf_op jit(solution)/shard_map/ppermute | solution.py:548
  67.0 4.6 %collective-permute-start.11 = (f32[32,64]{1,0:T(8,128)S(1)}, f32[32,64]{1,0:T(8,128)S(1)}, u32[]{:S(2)}, u32[]{:S(2)}) collective-permute-start(f32[32,64]{1,0:T(8,128)S(1)} %add.33.left_ref), channel_id=1, source_target_pairs={{0,16},{1,17},{2,18},{3,19},{4,20},{5,21},{6,22},{7,23},{8,24},{9,... | collective-permute-start | bytes 24584 | tf_op jit(solution)/shard_map/ppermute | solution.py:548

commit v7 on v6

--- a/solution.py
+++ b/solution.py
@@ -325,7 +325,7 @@
     return (g[:m, :n] + g[m:, n:]) + (g[:m, n:] + g[m:, :n])
 
 
-def gram_kernel(snap_ref, gram_ref, snap, sems):
+def gram_kernel(snap_ref, gram_ref, split_ref, snap, sems):
     rows, width, _ = snap.shape
     parts = sems.shape[0]
     depth = rows // parts
@@ -341,6 +341,7 @@
         fetch(i).wait()
         for x in range(i * depth, (i + 1) * depth):
             both = split_rows(snap[x])
+            split_ref[x] = both
             total = total + outer_of(both, both)
     gram_ref[...] = joined(total)
 
@@ -380,7 +381,7 @@
     if with_left:
         def add(x, total):
             now = split_rows(snap[x])
-            every = jnp.concatenate([now, split_rows(earlier[x])], axis=0)
+            every = jnp.concatenate([now, earlier[x]], axis=0)
             return total + outer_of(now, every)
 
         both = jnp.zeros((2 * width, 4 * width), jnp.float32)
@@ -651,17 +652,22 @@
     ]
     if fast:
         outs.append(jax.ShapeDtypeStruct((sketch.shape[1], sketch.shape[0]), f32))
-        gram = pl.pallas_call(
+        gram, split = pl.pallas_call(
             gram_kernel,
-            out_shape=jax.ShapeDtypeStruct((width // 2, width // 2), f32),
+            out_shape=[
+                jax.ShapeDtypeStruct((width // 2, width // 2), f32),
+                jax.ShapeDtypeStruct((rows, width, length), jnp.bfloat16),
+            ],
             in_specs=[HBM],
-            out_specs=VMEM,
+            out_specs=[VMEM] * 2,
             scratch_shapes=[pltpu.VMEM(half_snap, f32), pltpu.SemaphoreType.DMA((4,))],
             cost_estimate=pl.CostEstimate(flops=2 * rows * width * width * length, bytes_accessed=2 * rows * width * length, transcendentals=0),
-            compiler_params=pltpu.CompilerParams(vmem_limit_bytes=12 * 2**20),
+            compiler_params=pltpu.CompilerParams(vmem_limit_bytes=16 * 2**20),
             name="gram",
         )(in_hbm(early))
         extra = [gram] + extra
+    else:
+        split = early
     made = pl.pallas_call(
         functools.partial(second_kernel, groups, halves, fast),
         out_shape=outs,
@@ -670,7 +676,7 @@
         scratch_shapes=grid[:4] + [pltpu.VMEM(half_snap, f32), pltpu.SemaphoreType.DMA((REACH,))],
         compiler_params=pltpu.CompilerParams(vmem_limit_bytes=32 * 2**20),
         name="second",
-    )(*beside, carry, early, *extra)
+    )(*beside, carry, split, *extra)
 
     ends = [made[1]]
     for shift in range(1, groups):

time: 79.7 us -> 79.7 us (level)
  no operation moved by 1% of the time
where the time goes in v7:
time: 79.7 us; the launch traced here: 79.4 us
  Pallas kernels  37.2 us (47%)
  starting transfers between devices  27.9 us (35%)
  waiting for transfers between devices  10.3 us (13%)
  between operations  1.56 us (2%)
  other arithmetic  1.06 us (1%)
  local copies, waits for them, and re-layouts  1.05 us (1%)
    ppermute x8, starting transfers between devices, shifted(): return lax.ppermute(value, AXES, moves)  18 us
    pallas_call x1, Pallas kernels, body(): pl.pallas_call(functools.partial(second_kernel, groups, halves, fast), ou...  11.8 us
    pallas_call x1, Pallas kernels, body(): pl.pallas_call(functools.partial(first_kernel, groups, halves), out_shape...  11.3 us
    ppermute x5, starting transfers between devices, total_of(): other = lax.ppermute(value, AXES, [(i, i ^ bit) for i in range(size)])  9.96 us
    ppermute x5, waiting for transfers between devices, total_of(): other = lax.ppermute(value, AXES, [(i, i ^ bit) for i in range(size)])  8.09 us
    pallas_call x1, Pallas kernels, body(): pl.pallas_call(functools.partial(merge_kernel, halves), out_shape=[jax.Sh...  7.64 us
    pallas_call x1, Pallas kernels, body(): pl.pallas_call(gram_kernel, out_shape=[jax.ShapeDtypeStruct((width // 2,...  4.16 us
    pallas_call x1, Pallas kernels, body(): pl.pallas_call(functools.partial(pack_kernel, groups, block), out_shape=s...  2.32 us
  transfers between devices with their start and end apart: 13, of which 6 were waited for; matrix products, arithmetic and copies ran while one was open for 3% of the time, Pallas kernels for 5%

profile of v7, /device:TPU:0, one launch (start us, length us, event | category | flops | bytes accessed | tf_op | source)
XLA Modules:
  0.0 79.4 jit_solution(18112157009389831831)
XLA Ops:
  0.6 0.0 copy-start
  1.3 2.3 %pack.1 = (f32[7,8,2176]{2,1,0:T(8,128)S(1)}, f32[7,16,2176]{2,1,0:T(8,128)S(1)}, f32[7,8,2176]{2,1,0:T(8,128)S(1)}, f32[2,8,2176]{2,1,0:T(8,128)}, f32[2,16,2176]{2,1,0:T(8,128)}, /*index=5*/f32[2,8,2176]{2,1,0:T(8,128)}) custom-call(s32[1]{0:T(128)S(6)} %copy.12.step_ref, f32[1,2,16,4096]{3,2,1,0:T(8,128)} %refs_0_.1, f32[16,4096]{1,0:T(8,128)} %refs_1_.1, ...), custom_call_target="tpu_custom_call" | custom-call | tf_op jit(solution)/shard_map/pack/pallas_call | solution.py:593
  3.6 0.5 collective-permute-start
  4.1 5.0 %collective-permute-start.1 = (f32[7,8,2176]{2,1,0:T(8,128)S(1)}, f32[7,8,2176]{2,1,0:T(8,128)S(1)}, u32[]{:S(2)}, u32[]{:S(2)}) collective-permute-start(f32[7,8,2176]{2,1,0:T(8,128)S(1)} %get-tuple-element.23), channel_id=1, source_target_pairs={{0,30},{1,31},{2,0},{3,1},{4,2},{5,3},{6,4},{7,5},{8,6},{9,7},{10,... | collective-permute-start | bytes 1462280 | tf_op jit(solution)/shard_map/ppermute | solution.py:530
  9.2 1.9 %collective-permute-start.3 = (f32[2,16,2176]{2,1,0:T(8,128)}, f32[2,16,2176]{2,1,0:T(8,128)S(1)}, u32[]{:S(2)}, u32[]{:S(2)}) collective-permute-start(f32[2,16,2176]{2,1,0:T(8,128)} %get-tuple-element.25), channel_id=1, source_target_pairs={{0,1},{1,0},{2,3},{3,2},{4,5},{5,4},{6,7},{7,6},{8,9},{9,8},{10,11... | collective-permute-start | bytes 835592 | tf_op jit(solution)/shard_map/ppermute | solution.py:530
  11.1 0.0 collective-permute-start.2
  11.1 5.3 %collective-permute-start.4 = (f32[2,8,2176]{2,1,0:T(8,128)}, f32[2,8,2176]{2,1,0:T(8,128)S(1)}, u32[]{:S(2)}, u32[]{:S(2)}) collective-permute-start(f32[2,8,2176]{2,1,0:T(8,128)} %get-tuple-element.26), channel_id=1, source_target_pairs={{0,31},{1,30},{2,1},{3,0},{4,3},{5,2},{6,5},{7,4},{8,7},{9,6},{10,... | collective-permute-start | bytes 417800 | tf_op jit(solution)/shard_map/ppermute | solution.py:530
  16.4 0.9 %dynamic-slice_bitcast_fusion.1 = (f32[64,128]{0,1:T(8,128)S(1)}, f32[64,128]{0,1:T(8,128)S(1)}) fusion(f32[2,2,64,128]{2,3,1,0:T(8,128)} %constant.17.clone, s32[]{:T(128)S(6)} %select_n.4, s32[]{:T(128)S(6)} %add.36), kind=kLoop, calls=%fused_computation.5 | loop fusion | bytes 131080 | tf_op jit(solution)/shard_map/squeeze | solution.py:619
  17.3 2.2 %collective-permute-done.2.refs_3_ = f32[2,8,2176]{2,1,0:T(8,128)S(1)} collective-permute-done((f32[2,8,2176]{2,1,0:T(8,128)}, f32[2,8,2176]{2,1,0:T(8,128)S(1)}, u32[]{:S(2)}, u32[]{:S(2)}) %collective-permute-start.2) | collective-permute-done | bytes 139296 | tf_op jit(solution)/shard_map/ppermute | solution.py:530
  19.5 0.0 collective-permute-done.4.refs_5_
  19.5 0.0 collective-permute-done.3.refs_4_
  19.5 0.0 collective-permute-done.refs_0_
  19.6 0.0 collective-permute-done.1.refs_2_
  19.6 11.3 %first.1 = (f32[16,64,1024]{2,1,0:T(8,128)}, f32[8,32,8,1152]{3,2,1,0:T(8,128)S(1)}, f32[8,8,1152]{2,1,0:T(8,128)S(1)}, f32[16,8,1152]{2,1,0:T(8,128)S(1)}, f32[8,8,1152]{2,1,0:T(8,128)S(1)}) custom-call(f32[7,8,2176]{2,1,0:T(8,128)S(1)} %collective-permute-done.refs_0_, f32[7,16,2176]{2,1,0:T(8,128)S(1)} %get-tuple-element.22.refs_1_, ...), custom_call_target="tpu_custom_call" | custom-call | tf_op jit(solution)/shard_map/first/pallas_call | solution.py:632
  30.9 4.6 %collective-permute-start.5 = (f32[8,8,1152]{2,1,0:T(8,128)S(1)}, f32[8,8,1152]{2,1,0:T(8,128)S(1)}, u32[]{:S(2)}, u32[]{:S(2)}) collective-permute-start(f32[8,8,1152]{2,1,0:T(8,128)S(1)} %get-tuple-element.27), channel_id=1, source_target_pairs={{0,2},{1,3},{2,4},{3,5},{4,6},{5,7},{6,8},{7,9},{8,10},{9,11},{10,... | collective-permute-start | bytes 884744 | tf_op jit(solution)/shard_map/ppermute | solution.py:530
  35.5 0.0 collective-permute-start.6
  35.5 0.9 %add_bitcast_fusion.refs_2_ = f32[128,64]{1,0:T(8,128)S(1)} fusion(f32[2,2,64,128]{2,3,1,0:T(8,128)} %constant.17.clone, s32[]{:T(128)S(6)} %select_n.4, s32[]{:T(128)S(6)} %add.36), kind=kLoop, calls=%fused_computation.6 | loop fusion | flops 8192 | bytes 98312 | tf_op jit(solution)/shard_map/transpose | solution.py:621
  36.4 0.0 copy-done
  36.4 0.2 convolution_bitcast_fusion.refs_1_
  36.7 4.2 %gram.1 = (f32[64,64]{1,0:T(8,128)S(1)}, bf16[16,128,1024]{2,1,0:T(8,128)(2,1)S(1)}) custom-call(f32[16,64,1024]{2,1,0:T(8,128)} %get-tuple-element.31.snap_ref.early_ref), custom_call_target="tpu_custom_call" | custom-call | flops 536870912 | bytes 4194304 | tf_op jit(solution)/shard_map/gram/pallas_call | solution.py:655
  40.8 0.0 collective-permute-done.5.left_halo
  40.9 0.0 collective-permute-done.6.right_halo
  40.9 11.8 %second.1 = (f32[16,64,1024]{2,1,0:T(8,128)}, f32[2,16,2048]{2,1,0:T(8,128)S(1)}, f32[1,2,16,2048]{3,2,1,0:T(8,128)S(1)}, f32[32,64]{1,0:T(8,128)S(1)}) custom-call(f32[8,8,1152]{2,1,0:T(8,128)S(1)} %collective-permute-done.5.left_halo, f32[16,8,1152]{2,1,0:T(8,128)S(1)} %get-tuple-element.28.own, f32[8,8,1152]{2,1,0:T(8,128)S(1)} %collective-permute-done.6.right_halo, ...), custom_call_target="tpu_custom_call" | custom-call | tf_op jit(solution)/shard_map/second/pallas_call | solution.py:671
  52.6 1.6 %collective-permute-start.7 = (f32[32,64]{1,0:T(8,128)S(1)}, f32[32,64]{1,0:T(8,128)S(1)}, u32[]{:S(2)}, u32[]{:S(2)}) collective-permute-start(f32[32,64]{1,0:T(8,128)S(1)} %get-tuple-element.34), channel_id=1, source_target_pairs={{0,1},{1,0},{2,3},{3,2},{4,5},{5,4},{6,7},{7,6},{8,9},{9,8},{10,11... | collective-permute-start | bytes 24584 | tf_op jit(solution)/shard_map/ppermute | solution.py:549
  54.2 2.2 %collective-permute-done.7 = f32[32,64]{1,0:T(8,128)S(1)} collective-permute-done((f32[32,64]{1,0:T(8,128)S(1)}, f32[32,64]{1,0:T(8,128)S(1)}, u32[]{:S(2)}, u32[]{:S(2)}) %collective-permute-start.7) | collective-permute-done | bytes 8224 | tf_op jit(solution)/shard_map/ppermute | solution.py:549
  56.4 0.8 collective-permute-start.8
  57.2 0.1 copy.11
  57.3 0.1 pad.3.clone
  57.4 0.7 collective-permute-done.8
  58.1 3.4 %collective-permute-start.9 = (f32[32,64]{1,0:T(8,128)S(1)}, f32[32,64]{1,0:T(8,128)S(1)}, u32[]{:S(2)}, u32[]{:S(2)}) collective-permute-start(f32[32,64]{1,0:T(8,128)S(1)} %add.31), channel_id=1, source_target_pairs={{0,4},{1,5},{2,6},{3,7},{4,0},{5,1},{6,2},{7,3},{8,12},{9,13},{10,... | collective-permute-start | bytes 24584 | tf_op jit(solution)/shard_map/ppermute | solution.py:549
  61.5 0.1 maximum_maximum_fusion.spread_ref
  61.6 0.6 collective-permute-start.12
  62.1 1.1 %collective-permute-done.9 = f32[32,64]{1,0:T(8,128)S(1)} collective-permute-done((f32[32,64]{1,0:T(8,128)S(1)}, f32[32,64]{1,0:T(8,128)S(1)}, u32[]{:S(2)}, u32[]{:S(2)}) %collective-permute-start.9) | collective-permute-done | bytes 8224 | tf_op jit(solution)/shard_map/ppermute | solution.py:549
  63.2 1.6 %collective-permute-start.10 = (f32[32,64]{1,0:T(8,128)S(1)}, f32[32,64]{1,0:T(8,128)S(1)}, u32[]{:S(2)}, u32[]{:S(2)}) collective-permute-start(f32[32,64]{1,0:T(8,128)S(1)} %add.32), channel_id=1, source_target_pairs={{0,8},{1,9},{2,10},{3,11},{4,12},{5,13},{6,14},{7,15},{8,0},{9,1},... | collective-permute-start | bytes 24584 | tf_op jit(solution)/shard_map/ppermute | solution.py:549
  64.8 2.2 %collective-permute-done.10 = f32[32,64]{1,0:T(8,128)S(1)} collective-permute-done((f32[32,64]{1,0:T(8,128)S(1)}, f32[32,64]{1,0:T(8,128)S(1)}, u32[]{:S(2)}, u32[]{:S(2)}) %collective-permute-start.10) | collective-permute-done | bytes 8224 | tf_op jit(solution)/shard_map/ppermute | solution.py:549
  67.0 2.6 %collective-permute-start.11 = (f32[32,64]{1,0:T(8,128)S(1)}, f32[32,64]{1,0:T(8,128)S(1)}, u32[]{:S(2)}, u32[]{:S(2)}) collective-permute-start(f32[32,64]{1,0:T(8,128)S(1)} %add.33.left_ref), channel_id=1, source_target_pairs={{0,16},{1,17},{2,18},{3,19},{4,20},{5,21},{6,22},{7,23},{8,24},{9,... | collective-permute-start | bytes 24584 | tf_op jit(solution)/shard_map/ppermute | solution.py:549
  69.6 0.1 fusion.4.unit_ref
  69.6 2.0 %collective-permute-done.11.other_ref = f32[32,64]{1,0:T(8,128)S(1)} collective-permute-done((f32[32,64]{1,0:T(8,128)S(1)}, f32[32,64]{1,0:T(8,128)S(1)}, u32[]{:S(2)}, u32[]{:S(2)}) %collective-permute-start.11) | collective-permute-done | bytes 8224 | tf_op jit(solution)/shard_map/ppermute | solution.py:549
  71.6 0.0 collective-permute-done.12.came_ref
  71.6 7.6 %merge.1 = (f32[32,16,2048]{2,1,0:T(8,128)}, f32[2,16,4096]{2,1,0:T(8,128)}) custom-call(f32[32,64]{1,0:T(8,128)S(1)} %add.33.left_ref, f32[32,64]{1,0:T(8,128)S(1)} %collective-permute-done.11.other_ref, f32[64,128]{1,0:T(8,128)S(1)} %maximum_maximum_fusion.spread_ref, f32[32,128]{1,0:T(8,128)S(1)} %fusion.4.unit_ref, ...), custom_call_target="tpu_custom_call" | custom-call | tf_op jit(solution)/shard_map/merge/pallas_call | solution.py:686
  (8 shorter events, 0.0 us)
Async XLA Ops:
  0.6 35.8 %copy-start = (f32[64,32]{0,1:T(8,128)S(1)}, f32[64,32]{0,1:T(8,128)}, u32[]{:S(2)}) copy-start(f32[64,32]{0,1:T(8,128)} %param.16) | copy-start | bytes 24580
  3.6 15.9 %collective-permute-start = (f32[7,8,2176]{2,1,0:T(8,128)S(1)}, f32[7,8,2176]{2,1,0:T(8,128)S(1)}, u32[]{:S(2)}, u32[]{:S(2)}) collective-permute-start(f32[7,8,2176]{2,1,0:T(8,128)S(1)} %get-tuple-element.21), channel_id=1, source_target_pairs={{0,2},{1,3},{2,4},{3,5},{4,6},{5,7},{6,8},{7,9},{8,10},{9,11},{10,... | collective-permute-start | bytes 1462280 | tf_op jit(solution)/shard_map/ppermute | solution.py:530
  4.1 15.4 %collective-permute-start.1 = (f32[7,8,2176]{2,1,0:T(8,128)S(1)}, f32[7,8,2176]{2,1,0:T(8,128)S(1)}, u32[]{:S(2)}, u32[]{:S(2)}) collective-permute-start(f32[7,8,2176]{2,1,0:T(8,128)S(1)} %get-tuple-element.23), channel_id=1, source_target_pairs={{0,30},{1,31},{2,0},{3,1},{4,2},{5,3},{6,4},{7,5},{8,6},{9,7},{10,... | collective-permute-start | bytes 1462280 | tf_op jit(solution)/shard_map/ppermute | solution.py:530
  9.2 10.4 %collective-permute-start.3 = (f32[2,16,2176]{2,1,0:T(8,128)}, f32[2,16,2176]{2,1,0:T(8,128)S(1)}, u32[]{:S(2)}, u32[]{:S(2)}) collective-permute-start(f32[2,16,2176]{2,1,0:T(8,128)} %get-tuple-element.25), channel_id=1, source_target_pairs={{0,1},{1,0},{2,3},{3,2},{4,5},{5,4},{6,7},{7,6},{8,9},{9,8},{10,11... | collective-permute-start | bytes 835592 | tf_op jit(solution)/shard_map/ppermute | solution.py:530
  11.1 8.4 %collective-permute-start.2 = (f32[2,8,2176]{2,1,0:T(8,128)}, f32[2,8,2176]{2,1,0:T(8,128)S(1)}, u32[]{:S(2)}, u32[]{:S(2)}) collective-permute-start(f32[2,8,2176]{2,1,0:T(8,128)} %get-tuple-element.24), channel_id=1, source_target_pairs={{0,3},{1,2},{2,5},{3,4},{4,7},{5,6},{6,9},{7,8},{8,11},{9,10},{10,... | collective-permute-start | bytes 417800 | tf_op jit(solution)/shard_map/ppermute | solution.py:530
  11.1 8.4 %collective-permute-start.4 = (f32[2,8,2176]{2,1,0:T(8,128)}, f32[2,8,2176]{2,1,0:T(8,128)S(1)}, u32[]{:S(2)}, u32[]{:S(2)}) collective-permute-start(f32[2,8,2176]{2,1,0:T(8,128)} %get-tuple-element.26), channel_id=1, source_target_pairs={{0,31},{1,30},{2,1},{3,0},{4,3},{5,2},{6,5},{7,4},{8,7},{9,6},{10,... | collective-permute-start | bytes 417800 | tf_op jit(solution)/shard_map/ppermute | solution.py:530
  30.9 9.9 %collective-permute-start.5 = (f32[8,8,1152]{2,1,0:T(8,128)S(1)}, f32[8,8,1152]{2,1,0:T(8,128)S(1)}, u32[]{:S(2)}, u32[]{:S(2)}) collective-permute-start(f32[8,8,1152]{2,1,0:T(8,128)S(1)} %get-tuple-element.27), channel_id=1, source_target_pairs={{0,2},{1,3},{2,4},{3,5},{4,6},{5,7},{6,8},{7,9},{8,10},{9,11},{10,... | collective-permute-start | bytes 884744 | tf_op jit(solution)/shard_map/ppermute | solution.py:530
  35.5 5.3 %collective-permute-start.6 = (f32[8,8,1152]{2,1,0:T(8,128)S(1)}, f32[8,8,1152]{2,1,0:T(8,128)S(1)}, u32[]{:S(2)}, u32[]{:S(2)}) collective-permute-start(f32[8,8,1152]{2,1,0:T(8,128)S(1)} %get-tuple-element.29), channel_id=1, source_target_pairs={{0,30},{1,31},{2,0},{3,1},{4,2},{5,3},{6,4},{7,5},{8,6},{9,7},{10,... | collective-permute-start | bytes 884744 | tf_op jit(solution)/shard_map/ppermute | solution.py:530
  52.6 3.8 %collective-permute-start.7 = (f32[32,64]{1,0:T(8,128)S(1)}, f32[32,64]{1,0:T(8,128)S(1)}, u32[]{:S(2)}, u32[]{:S(2)}) collective-permute-start(f32[32,64]{1,0:T(8,128)S(1)} %get-tuple-element.34), channel_id=1, source_target_pairs={{0,1},{1,0},{2,3},{3,2},{4,5},{5,4},{6,7},{7,6},{8,9},{9,8},{10,11... | collective-permute-start | bytes 24584 | tf_op jit(solution)/shard_map/ppermute | solution.py:549
  56.4 1.6 %collective-permute-start.8 = (f32[32,64]{1,0:T(8,128)S(1)}, f32[32,64]{1,0:T(8,128)S(1)}, u32[]{:S(2)}, u32[]{:S(2)}) collective-permute-start(f32[32,64]{1,0:T(8,128)S(1)} %add.30), channel_id=1, source_target_pairs={{0,2},{1,3},{2,0},{3,1},{4,6},{5,7},{6,4},{7,5},{8,10},{9,11},{10,... | collective-permute-start | bytes 24584 | tf_op jit(solution)/shard_map/ppermute | solution.py:549
  58.1 5.2 %collective-permute-start.9 = (f32[32,64]{1,0:T(8,128)S(1)}, f32[32,64]{1,0:T(8,128)S(1)}, u32[]{:S(2)}, u32[]{:S(2)}) collective-permute-start(f32[32,64]{1,0:T(8,128)S(1)} %add.31), channel_id=1, source_target_pairs={{0,4},{1,5},{2,6},{3,7},{4,0},{5,1},{6,2},{7,3},{8,12},{9,13},{10,... | collective-permute-start | bytes 24584 | tf_op jit(solution)/shard_map/ppermute | solution.py:549
  61.6 10.0 %collective-permute-start.12 = (f32[2,16,2048]{2,1,0:T(8,128)S(1)}, f32[2,16,2048]{2,1,0:T(8,128)S(1)}, u32[]{:S(2)}, u32[]{:S(2)}) collective-permute-start(f32[2,16,2048]{2,1,0:T(8,128)S(1)} %bitcast.15), channel_id=1, source_target_pairs={{0,1},{1,0},{2,3},{3,2},{4,5},{5,4},{6,7},{7,6},{8,9},{9,8},{10,11... | collective-permute-start | bytes 786440 | tf_op jit(solution)/shard_map/ppermute | solution.py:530
  63.2 3.7 %collective-permute-start.10 = (f32[32,64]{1,0:T(8,128)S(1)}, f32[32,64]{1,0:T(8,128)S(1)}, u32[]{:S(2)}, u32[]{:S(2)}) collective-permute-start(f32[32,64]{1,0:T(8,128)S(1)} %add.32), channel_id=1, source_target_pairs={{0,8},{1,9},{2,10},{3,11},{4,12},{5,13},{6,14},{7,15},{8,0},{9,1},... | collective-permute-start | bytes 24584 | tf_op jit(solution)/shard_map/ppermute | solution.py:549
  67.0 4.6 %collective-permute-start.11 = (f32[32,64]{1,0:T(8,128)S(1)}, f32[32,64]{1,0:T(8,128)S(1)}, u32[]{:S(2)}, u32[]{:S(2)}) collective-permute-start(f32[32,64]{1,0:T(8,128)S(1)} %add.33.left_ref), channel_id=1, source_target_pairs={{0,16},{1,17},{2,18},{3,19},{4,20},{5,21},{6,22},{7,23},{8,24},{9,... | collective-permute-start | bytes 24584 | tf_op jit(solution)/shard_map/ppermute | solution.py:549
